TPU v7x, 32 devices: a whole 2x2x4 slice. The times are simulated.
32 devices in a mesh: dp: 8 (over z, y), tensor: 4 (over x, core).
Axes of the slice: x: 2, y: 2, z: 4, core: 2. Of those that a mesh axis runs over, the one named last changes fastest.
Arguments:
- frames: bfloat16 [4, 8, 512, 1024], P(None, 'dp', 'tensor'), may hold values from -6 to 6
- skip_frames: bfloat16 [4, 8, 512, 1024], P(None, 'dp', 'tensor'), may hold values from -6 to 6
- time_embed: bfloat16 [4, 8, 1024], P(None, 'dp'), may hold values from -6 to 6
- lengths: int32 [4, 8], P(None, 'dp'), may hold values from 128 to 512, as said below
- out_grad: bfloat16 [4, 8, 512, 1024], P(None, 'dp', 'tensor'), may hold values from -6 to 6
- skip_weight: float32 [2048, 1024], P(('dp', 'tensor')), may hold values from -0.125 to 0.125
- adapt_weight: float32 [1024, 4096], P(None, ('dp', 'tensor')), may hold values from -0.1875 to 0.1875
- input_weight: float32 [1024, 3, 1024], P('dp', None, 'tensor'), may hold values from -0.1875 to 0.1875
- output_weight: float32 [1024, 1024], P('tensor', 'dp'), may hold values from -2 to 2
- up_weight: float32 [1024, 4096], P('dp', 'tensor'), may hold values from -0.1875 to 0.1875
- down_weight: float32 [4096, 1024], P('tensor', 'dp'), may hold values from -0.09375 to 0.09375
- skip_first: float32 [2048, 1024], P(('dp', 'tensor')), may hold values from -80 to 80
- adapt_first: float32 [1024, 4096], P(None, ('dp', 'tensor')), may hold values from -40 to 40
- input_first: float32 [1024, 3, 1024], P('dp', None, 'tensor'), may hold values from -80 to 80
- output_first: float32 [1024, 1024], P('tensor', 'dp'), may hold values from -8 to 8
- up_first: float32 [1024, 4096], P('dp', 'tensor'), may hold values from -32 to 32
- down_first: float32 [4096, 1024], P('tensor', 'dp'), may hold values from -64 to 64
- skip_second: float32 [2048, 1024], P(('dp', 'tensor')), may hold values from 16.384 to 65.536
- adapt_second: float32 [1024, 4096], P(None, ('dp', 'tensor')), may hold values from 4.096 to 16.384
- input_second: float32 [1024, 3, 1024], P('dp', None, 'tensor'), may hold values from 16.384 to 65.536
- output_second: float32 [1024, 1024], P('tensor', 'dp'), may hold values from 0.128 to 0.512
- up_second: float32 [1024, 4096], P('dp', 'tensor'), may hold values from 2.62144 to 10.48576
- down_second: float32 [4096, 1024], P('tensor', 'dp'), may hold values from 8.192 to 32.768
Outputs:
- block_out: bfloat16 [4, 8, 512, 1024], P(None, 'dp', 'tensor')
- frames_grad: float32 [4, 8, 512, 1024], P(None, 'dp', 'tensor')
- skips_grad: float32 [4, 8, 512, 1024], P(None, 'dp', 'tensor')
- time_grad: float32 [4, 8, 1024], P(None, 'dp')
- skip_mean: float32 [2048, 1024], P(('dp', 'tensor'))
- skip_square: float32 [2048, 1024], P(('dp', 'tensor'))
- skip_master: float32 [2048, 1024], P(('dp', 'tensor'))
- skip_copy: bfloat16 [2048, 1024], P(('dp', 'tensor'))
- adapt_mean: float32 [1024, 4096], P(None, ('dp', 'tensor'))
- adapt_square: float32 [1024, 4096], P(None, ('dp', 'tensor'))
- adapt_master: float32 [1024, 4096], P(None, ('dp', 'tensor'))
- adapt_copy: bfloat16 [1024, 4096], P(None, ('dp', 'tensor'))
- input_mean: float32 [1024, 3, 1024], P('dp', None, 'tensor')
- input_square: float32 [1024, 3, 1024], P('dp', None, 'tensor')
- input_master: float32 [1024, 3, 1024], P('dp', None, 'tensor')
- input_copy: bfloat16 [1024, 3, 1024], P('dp', None, 'tensor')
- output_mean: float32 [1024, 1024], P('tensor', 'dp')
- output_square: float32 [1024, 1024], P('tensor', 'dp')
- output_master: float32 [1024, 1024], P('tensor', 'dp')
- output_copy: bfloat16 [1024, 1024], P('tensor', 'dp')
- up_mean: float32 [1024, 4096], P('dp', 'tensor')
- up_square: float32 [1024, 4096], P('dp', 'tensor')
- up_master: float32 [1024, 4096], P('dp', 'tensor')
- up_copy: bfloat16 [1024, 4096], P('dp', 'tensor')
- down_mean: float32 [4096, 1024], P('tensor', 'dp')
- down_square: float32 [4096, 1024], P('tensor', 'dp')
- down_master: float32 [4096, 1024], P('tensor', 'dp')
- down_copy: bfloat16 [4096, 1024], P('tensor', 'dp')
Inputs may be any that keep to these rules, and one draw needn't show every extreme that they name: `lengths`: in every column some micro-batch's utterance has exactly 512 frames; frames at positions from an utterance's length on are padding.
All inputs are finite; a program needn't handle non-finite values.
Results may differ from a plain program's by a relative error of at most 0.02.
The roundings to bfloat16 on the way count: a program that leaves them out, or rounds other values in their place, can miss the bound.
Values may be sent and summed in bfloat16 or wider, within the bound.
No kernel may reach another device: no remote copies, remote signals or barrier semaphores. Data moves between devices by JAX's collectives and lax.ppermute only.
A program may use at most 192 MiB of HBM per device.

v0:
```python
from functools import partial

import jax
import jax.numpy as jnp
from jax import lax
from jax.sharding import PartitionSpec as P

HEAD_DIM = 64
STEP = 10


norm_eps = 1e-06
neg_large = -1e30
rates = (0.04, 0.06, 0.06, 0.6, 0.06, 0.03)
beta_first = 0.9
beta_second = 0.999
decay_rate = 0.01
adam_eps = 1e-08


def layer_norm(values):
    center = values - jnp.mean(values, axis=-1, keepdims=True)
    spread = jnp.mean(center * center, axis=-1, keepdims=True)
    return center * lax.rsqrt(spread + norm_eps)


def modulate(values, shift, scale):
    return layer_norm(values) * (1.0 + scale) + shift


def rotate(values, positions):
    half = values.shape[-1] // 2
    frequency = 10000.0 ** (-jnp.arange(half).astype(jnp.float32) / half)
    angles = positions[:, None] * frequency[None, :]
    cosine = jnp.cos(angles)[:, None, :]
    sine = jnp.sin(angles)[:, None, :]
    first = values[..., :half]
    second = values[..., half:]
    return jnp.concatenate(
        [first * cosine - second * sine, second * cosine + first * sine], axis=-1
    )


def activate(values):
    return jax.nn.gelu(values, approximate=True)


def contract_last(left, right):
    return lax.dot_general(
        left, right, (((1,), (1,)), ((), ())), preferred_element_type=jnp.float32
    )


def gather_rows(values):
    return lax.all_gather(values, "tensor", axis=0, tiled=True)


def gather_grads(values):
    return lax.all_gather(values, "tensor", axis=0, tiled=True)


def scatter_rows(values, weight, count):

    def term(start, size):
        return jnp.dot(values, weight, preferred_element_type=jnp.float32)

    return lax.psum_scatter(
        term(jnp.int32(0), count * lax.axis_size("tensor")).astype(jnp.bfloat16),
        "tensor",
        scatter_dimension=0,
        tiled=True,
    ).astype(jnp.float32)


def scatter_grads(values, weight, count):

    def term(start, size):
        return contract_last(values, weight)

    return lax.psum_scatter(
        term(jnp.int32(0), count * lax.axis_size("tensor")).astype(jnp.bfloat16),
        "tensor",
        scatter_dimension=0,
        tiled=True,
    ).astype(jnp.float32)


def attend_block(queries, keys, values, key_ok, scale):
    scores = jnp.einsum("qhd,khd->hqk", queries, keys, preferred_element_type=jnp.float32) * scale
    scores = jnp.where(key_ok[None, None, :], scores, neg_large)
    top = jnp.max(scores, axis=-1, keepdims=True)
    weights = jnp.exp(scores - top)
    total = jnp.sum(weights, axis=-1, keepdims=True)
    shares = (weights / total).astype(jnp.bfloat16)
    mixed = jnp.einsum("hqk,khd->qhd", shares, values, preferred_element_type=jnp.float32)
    return (mixed.astype(jnp.bfloat16), (top + jnp.log(total))[:, :, 0])


def attend_back(carry, item, keys, values, key_ok, scale):
    key_grad, value_grad = carry
    queries, mixed_grad, logsum = item
    scores = jnp.einsum("qhd,khd->hqk", queries, keys, preferred_element_type=jnp.float32) * scale
    scores = jnp.where(key_ok[None, None, :], scores, neg_large)
    shares = jnp.exp(scores - logsum[:, :, None])
    share_grad = jnp.einsum("qhd,khd->hqk", mixed_grad, values, preferred_element_type=jnp.float32)
    inner = jnp.sum(share_grad * shares, axis=-1, keepdims=True)
    score_grad = (shares * (share_grad - inner)).astype(jnp.bfloat16)
    query_grad = (
        jnp.einsum("hqk,khd->qhd", score_grad, keys, preferred_element_type=jnp.float32) * scale
    )
    key_grad = (
        key_grad
        + jnp.einsum("hqk,qhd->khd", score_grad, queries, preferred_element_type=jnp.float32)
        * scale
    )
    value_grad = value_grad + jnp.einsum(
        "hqk,qhd->khd", shares.astype(jnp.bfloat16), mixed_grad, preferred_element_type=jnp.float32
    )
    return ((key_grad, value_grad), query_grad)


def adam_update(master, first, second, grad, rate):
    first_new = beta_first * first + (1.0 - beta_first) * grad
    second_new = beta_second * second + (1.0 - beta_second) * grad * grad
    first_hat = first_new / (1.0 - beta_first**STEP)
    second_hat = second_new / (1.0 - beta_second**STEP)
    master_new = master - rate * (
        first_hat / (jnp.sqrt(second_hat) + adam_eps) + decay_rate * master
    )
    return (first_new, second_new, master_new, master_new.astype(jnp.bfloat16))


def body(
    frames,
    skip_frames,
    time_embed,
    lengths,
    out_grad,
    skip_weight,
    adapt_weight,
    input_weight,
    output_weight,
    up_weight,
    down_weight,
    skip_first,
    adapt_first,
    input_first,
    output_first,
    up_first,
    down_first,
    skip_second,
    adapt_second,
    input_second,
    output_second,
    up_second,
    down_second,
):
    micro = frames.shape[0]
    rows = frames.shape[2]
    width = frames.shape[3]
    parts = lax.axis_size("tensor")
    full_length = rows * parts
    highest = lax.Precision.HIGHEST
    skip_low = skip_weight.astype(jnp.bfloat16)
    adapt_low = adapt_weight.astype(jnp.bfloat16)
    time_values = time_embed[:, 0, :].astype(jnp.float32)
    time_active, time_back = jax.vjp(jax.nn.silu, time_values)
    time_low = time_active.astype(jnp.bfloat16)
    shared_skip, shared_adapt = (
        lax.all_gather(skip_low, ("dp", "tensor"), axis=0, tiled=True),
        lax.all_gather(adapt_low, ("dp", "tensor"), axis=1, tiled=True),
    )
    adapt_all = jnp.dot(time_low, shared_adapt, preferred_element_type=jnp.float32)
    input_part, output_part, up_part, down_part = (
        lax.all_gather(input_weight.astype(jnp.bfloat16), "dp", axis=0, tiled=True),
        lax.all_gather(output_weight.astype(jnp.bfloat16), "dp", axis=1, tiled=True),
        lax.all_gather(up_weight.astype(jnp.bfloat16), "dp", axis=0, tiled=True),
        lax.all_gather(down_weight.astype(jnp.bfloat16), "dp", axis=1, tiled=True),
    )
    heads = input_part.shape[2] // HEAD_DIM
    inner = heads * HEAD_DIM
    scale = HEAD_DIM ** (-0.5)
    block = min(full_length, 512)
    blocks = full_length // block
    tensor_index = lax.axis_index("tensor")
    row_index = tensor_index * rows + jnp.arange(rows, dtype=jnp.int32)
    key_index = jnp.arange(full_length, dtype=jnp.int32)
    positions = key_index.astype(jnp.float32)
    turn = partial(rotate, positions=positions)
    skip_total = jnp.zeros(shared_skip.shape, jnp.float32)
    input_total = jnp.zeros(input_part.shape, jnp.float32)
    output_total = jnp.zeros(output_part.shape, jnp.float32)
    up_total = jnp.zeros(up_part.shape, jnp.float32)
    down_total = jnp.zeros(down_part.shape, jnp.float32)
    results, frame_grads, skip_grads, adapt_grads = ([], [], [], [])
    for step in range(micro):
        length = lengths[step, 0]
        row_keep = (row_index < length).astype(jnp.float32)[:, None]
        key_ok = key_index < length
        joined = jnp.concatenate([frames[step, 0], skip_frames[step, 0]], axis=1)
        hidden = jnp.dot(joined, shared_skip, preferred_element_type=jnp.float32)
        shift_one, scale_one, shift_two, scale_two = jnp.split(adapt_all[step], 4)
        normed_one, norm_one_back = jax.vjp(modulate, hidden, shift_one, scale_one)
        gathered_one = gather_rows(normed_one.astype(jnp.bfloat16))
        project = jnp.einsum(
            "nd,dce->nce", gathered_one, input_part, preferred_element_type=jnp.float32
        )
        query_turned, query_back = jax.vjp(
            turn, project[:, 0].reshape(full_length, heads, HEAD_DIM)
        )
        key_turned, key_back = jax.vjp(turn, project[:, 1].reshape(full_length, heads, HEAD_DIM))
        queries = query_turned.astype(jnp.bfloat16)
        keys = key_turned.astype(jnp.bfloat16)
        values = project[:, 2].reshape(full_length, heads, HEAD_DIM).astype(jnp.bfloat16)
        query_blocks = queries.reshape(blocks, block, heads, HEAD_DIM)
        mixed, logsum = lax.map(
            lambda piece: attend_block(piece, keys, values, key_ok, scale), query_blocks
        )
        mixed_flat = mixed.reshape(full_length, inner)
        attended = scatter_rows(mixed_flat, output_part, rows)
        middle = hidden + attended
        normed_two, norm_two_back = jax.vjp(modulate, middle, shift_two, scale_two)
        gathered_two = gather_rows(normed_two.astype(jnp.bfloat16))
        lifted = jnp.dot(gathered_two, up_part, preferred_element_type=jnp.float32)
        gated, gate_back = jax.vjp(activate, lifted)
        gated_low = gated.astype(jnp.bfloat16)
        fed = scatter_rows(gated_low, down_part, rows)
        results.append((row_keep * (middle + fed)).astype(jnp.bfloat16))
        outer_grad = row_keep * out_grad[step, 0].astype(jnp.float32)
        outer_full = gather_grads(outer_grad.astype(jnp.bfloat16))
        down_total = down_total + jnp.einsum(
            "nf,nd->fd", gated_low, outer_full, preferred_element_type=jnp.float32
        )
        gated_grad = contract_last(outer_full, down_part)
        lifted_grad = gate_back(gated_grad)[0].astype(jnp.bfloat16)
        up_total = up_total + jnp.einsum(
            "nd,nf->df", gathered_two, lifted_grad, preferred_element_type=jnp.float32
        )
        normed_two_grad = scatter_grads(lifted_grad, up_part, rows)
        middle_part, shift_two_grad, scale_two_grad = norm_two_back(normed_two_grad)
        middle_grad = outer_grad + middle_part
        middle_full = gather_grads(middle_grad.astype(jnp.bfloat16))
        output_total = output_total + jnp.einsum(
            "ne,nd->ed", mixed_flat, middle_full, preferred_element_type=jnp.float32
        )
        mixed_grad = contract_last(middle_full, output_part).astype(jnp.bfloat16)
        grad_blocks = mixed_grad.reshape(blocks, block, heads, HEAD_DIM)
        empty = jnp.zeros((full_length, heads, HEAD_DIM), jnp.float32)
        (key_grad, value_grad), query_grad = lax.scan(
            lambda carry, item: attend_back(carry, item, keys, values, key_ok, scale),
            (empty, empty),
            (query_blocks, grad_blocks, logsum),
        )
        query_pre = query_back(query_grad.reshape(full_length, heads, HEAD_DIM))[0]
        key_pre = key_back(key_grad)[0]
        project_grad = jnp.stack(
            [
                query_pre.reshape(full_length, inner),
                key_pre.reshape(full_length, inner),
                value_grad.reshape(full_length, inner),
            ],
            axis=1,
        ).astype(jnp.bfloat16)
        input_total = input_total + jnp.einsum(
            "nd,nce->dce", gathered_one, project_grad, preferred_element_type=jnp.float32
        )
        normed_one_grad = scatter_grads(
            project_grad.reshape(full_length, 3 * inner), input_part.reshape(width, 3 * inner), rows
        )
        hidden_part, shift_one_grad, scale_one_grad = norm_one_back(normed_one_grad)
        hidden_low = (middle_grad + hidden_part).astype(jnp.bfloat16)
        skip_total = skip_total + jnp.einsum(
            "nj,nd->jd", joined, hidden_low, preferred_element_type=jnp.float32
        )
        joined_grad = contract_last(hidden_low, shared_skip)
        frame_grads.append(joined_grad[:, :width])
        skip_grads.append(joined_grad[:, width:])
        adapt_grads.append(
            jnp.concatenate([shift_one_grad, scale_one_grad, shift_two_grad, scale_two_grad])
        )
    adapt_grad_all = jnp.stack(adapt_grads)
    time_float = time_low.astype(jnp.float32)
    time_part = lax.dot_general(
        adapt_grad_all,
        shared_adapt.astype(jnp.float32),
        (((1,), (1,)), ((), ())),
        precision=highest,
    )
    adapt_total = jnp.einsum("md,me->de", time_float, adapt_grad_all, precision=highest)
    skip_sum, adapt_sum = (
        lax.psum_scatter(skip_total, ("dp", "tensor"), scatter_dimension=0, tiled=True),
        lax.psum_scatter(adapt_total, ("dp", "tensor"), scatter_dimension=1, tiled=True),
    )
    time_grad = lax.psum(time_back(time_part)[0], "tensor")
    input_sum, output_sum, up_sum, down_sum = (
        lax.psum_scatter(input_total, "dp", scatter_dimension=0, tiled=True),
        lax.psum_scatter(output_total, "dp", scatter_dimension=1, tiled=True),
        lax.psum_scatter(up_total, "dp", scatter_dimension=0, tiled=True),
        lax.psum_scatter(down_total, "dp", scatter_dimension=1, tiled=True),
    )
    skip_new = adam_update(skip_weight, skip_first, skip_second, skip_sum, rates[0])
    adapt_new = adam_update(adapt_weight, adapt_first, adapt_second, adapt_sum, rates[1])
    input_new = adam_update(input_weight, input_first, input_second, input_sum, rates[2])
    output_new = adam_update(output_weight, output_first, output_second, output_sum, rates[3])
    up_new = adam_update(up_weight, up_first, up_second, up_sum, rates[4])
    down_new = adam_update(down_weight, down_first, down_second, down_sum, rates[5])
    return (
        jnp.stack(results)[:, None],
        jnp.stack(frame_grads)[:, None],
        jnp.stack(skip_grads)[:, None],
        time_grad[:, None, :],
        skip_new[0],
        skip_new[1],
        skip_new[2],
        skip_new[3],
        adapt_new[0],
        adapt_new[1],
        adapt_new[2],
        adapt_new[3],
        input_new[0],
        input_new[1],
        input_new[2],
        input_new[3],
        output_new[0],
        output_new[1],
        output_new[2],
        output_new[3],
        up_new[0],
        up_new[1],
        up_new[2],
        up_new[3],
        down_new[0],
        down_new[1],
        down_new[2],
        down_new[3],
    )


def solution(mesh):
    return jax.shard_map(
        body,
        mesh=mesh,
        in_specs=(
            P(None, "dp", "tensor", None),
            P(None, "dp", "tensor", None),
            P(None, "dp", None),
            P(None, "dp"),
            P(None, "dp", "tensor", None),
            P(("dp", "tensor"), None),
            P(None, ("dp", "tensor")),
            P("dp", None, "tensor"),
            P("tensor", "dp"),
            P("dp", "tensor"),
            P("tensor", "dp"),
            P(("dp", "tensor"), None),
            P(None, ("dp", "tensor")),
            P("dp", None, "tensor"),
            P("tensor", "dp"),
            P("dp", "tensor"),
            P("tensor", "dp"),
            P(("dp", "tensor"), None),
            P(None, ("dp", "tensor")),
            P("dp", None, "tensor"),
            P("tensor", "dp"),
            P("dp", "tensor"),
            P("tensor", "dp"),
        ),
        out_specs=(
            P(None, "dp", "tensor", None),
            P(None, "dp", "tensor", None),
            P(None, "dp", "tensor", None),
            P(None, "dp", None),
            P(("dp", "tensor"), None),
            P(("dp", "tensor"), None),
            P(("dp", "tensor"), None),
            P(("dp", "tensor"), None),
            P(None, ("dp", "tensor")),
            P(None, ("dp", "tensor")),
            P(None, ("dp", "tensor")),
            P(None, ("dp", "tensor")),
            P("dp", None, "tensor"),
            P("dp", None, "tensor"),
            P("dp", None, "tensor"),
            P("dp", None, "tensor"),
            P("tensor", "dp"),
            P("tensor", "dp"),
            P("tensor", "dp"),
            P("tensor", "dp"),
            P("dp", "tensor"),
            P("dp", "tensor"),
            P("dp", "tensor"),
            P("dp", "tensor"),
            P("tensor", "dp"),
            P("tensor", "dp"),
            P("tensor", "dp"),
            P("tensor", "dp"),
        ),
        check_vma=False,
    )
```

profile of v0, /device:TPU:0, one launch (start us, length us, event | category | flops | bytes accessed | tf_op | source)
XLA Modules:
  0.0 1793.4 jit_solution(4404244207036680246)
XLA Ops:
  14.7 61.6 %all-gather.22.cloned.1.call-done = bf16[2048,1024]{1,0:T(8,128)(2,1)} async-done(((bf16[64,1024]{1,0:T(8,128)(2,1)}), bf16[2048,1024]{1,0:T(8,128)(2,1)}) %all-gather.22.cloned.1.call-update) | async-done | bytes 4194320 | tf_op jit(solution)/shard_map/all_gather | solution.py:170
  80.1 90.5 %all-gather.24.cloned.1.call-done = bf16[1024,4096]{1,0:T(8,128)(2,1)} async-done(((bf16[1024,128]{1,0:T(8,128)(2,1)}), bf16[1024,4096]{1,0:T(8,128)(2,1)}) %all-gather.24.cloned.1.call-update) | async-done | bytes 8388624 | tf_op jit(solution)/shard_map/all_gather | solution.py:171
  178.4 29.4 %all_gather.70 = bf16[256,1024]{1,0:T(8,128)(2,1)S(1)} all-gather(bf16[256,128]{1,0:T(8,128)(2,1)S(1)} %convert_element_type.694), channel_id=1, replica_groups=mesh['dp'=8,'tensor'=4] {'dp'}, dimensions={1}, use_global_device_ids=true | all-gather | bytes 589824 | tf_op jit(solution)/shard_map/all_gather | solution.py:176
  220.4 17.2 all-gather.44.cloned.1.call-done
  250.2 20.8 %reduce-scatter.35.cloned.1.call-done = bf16[128,1024]{1,0:T(8,128)(2,1)} async-done(((bf16[512,1024]{1,0:T(8,128)(2,1)}), bf16[128,1024]{1,0:T(8,128)(2,1)}) %reduce-scatter.35.cloned.1.call-update) | async-done | bytes 262160 | tf_op jit(solution)/shard_map/reduce_scatter | solution.py:67
  273.5 16.4 all-gather.60.cloned.1.call-done
  289.9 53.9 %all-gather.34.cloned.1.call-done = bf16[1024,1024]{1,0:T(8,128)(2,1)} async-done(((bf16[1024,128]{1,0:T(8,128)(2,1)}), bf16[1024,1024]{1,0:T(8,128)(2,1)}) %all-gather.34.cloned.1.call-update) | async-done | bytes 2097168 | tf_op jit(solution)/shard_map/all_gather | solution.py:178
  348.3 45.9 %all-gather.32.cloned.1.call-done = bf16[1024,1024]{1,0:T(8,128)(2,1)} async-done(((bf16[128,1024]{1,0:T(8,128)(2,1)}), bf16[1024,1024]{1,0:T(8,128)(2,1)}) %all-gather.32.cloned.1.call-update) | async-done | bytes 2097168 | tf_op jit(solution)/shard_map/all_gather | solution.py:177
  394.2 17.5 all-gather.46.cloned.1.call-done
  448.2 26.2 %reduce-scatter.37.cloned.1.call-done = bf16[128,1024]{1,0:T(8,128)(2,1)} async-done(((bf16[512,1024]{1,0:T(8,128)(2,1)}), bf16[128,1024]{1,0:T(8,128)(2,1)}) %reduce-scatter.37.cloned.1.call-update) | async-done | bytes 262160 | tf_op jit(solution)/shard_map/reduce_scatter | solution.py:67
  527.7 24.4 %reduce-scatter.23.cloned.1.call-done = bf16[128,1024]{1,0:T(8,128)(2,1)} async-done(((bf16[512,1024]{1,0:T(8,128)(2,1)}), bf16[128,1024]{1,0:T(8,128)(2,1)}) %reduce-scatter.23.cloned.1.call-update) | async-done | bytes 262160 | tf_op jit(solution)/shard_map/reduce_scatter | solution.py:67
  622.3 22.7 %reduce-scatter.39.cloned.1.call-done = bf16[128,1024]{1,0:T(8,128)(2,1)} async-done(((bf16[512,1024]{1,0:T(8,128)(2,1)}), bf16[128,1024]{1,0:T(8,128)(2,1)}) %reduce-scatter.39.cloned.1.call-update) | async-done | bytes 262160 | tf_op jit(solution)/shard_map/reduce_scatter | solution.py:80
  648.0 24.4 %reduce-scatter.25.cloned.1.call-done = bf16[128,1024]{1,0:T(8,128)(2,1)} async-done(((bf16[512,1024]{1,0:T(8,128)(2,1)}), bf16[128,1024]{1,0:T(8,128)(2,1)}) %reduce-scatter.25.cloned.1.call-update) | async-done | bytes 262160 | tf_op jit(solution)/shard_map/reduce_scatter | solution.py:67
  773.4 24.3 %reduce-scatter.41.cloned.1.call-done = bf16[128,1024]{1,0:T(8,128)(2,1)} async-done(((bf16[512,1024]{1,0:T(8,128)(2,1)}), bf16[128,1024]{1,0:T(8,128)(2,1)}) %reduce-scatter.41.cloned.1.call-update) | async-done | bytes 262160 | tf_op jit(solution)/shard_map/reduce_scatter | solution.py:80
  799.4 25.8 %reduce-scatter.27.cloned.1.call-done = bf16[128,1024]{1,0:T(8,128)(2,1)} async-done(((bf16[512,1024]{1,0:T(8,128)(2,1)}), bf16[128,1024]{1,0:T(8,128)(2,1)}) %reduce-scatter.27.cloned.1.call-update) | async-done | bytes 262160 | tf_op jit(solution)/shard_map/reduce_scatter | solution.py:67
  930.3 25.8 %reduce-scatter.43.cloned.1.call-done = bf16[128,1024]{1,0:T(8,128)(2,1)} async-done(((bf16[512,1024]{1,0:T(8,128)(2,1)}), bf16[128,1024]{1,0:T(8,128)(2,1)}) %reduce-scatter.43.cloned.1.call-update) | async-done | bytes 262160 | tf_op jit(solution)/shard_map/reduce_scatter | solution.py:80
  959.1 24.5 %reduce-scatter.29.cloned.1.call-done = bf16[128,1024]{1,0:T(8,128)(2,1)} async-done(((bf16[512,1024]{1,0:T(8,128)(2,1)}), bf16[128,1024]{1,0:T(8,128)(2,1)}) %reduce-scatter.29.cloned.1.call-update) | async-done | bytes 262160 | tf_op jit(solution)/shard_map/reduce_scatter | solution.py:67
  987.4 23.6 %reduce-scatter.33.cloned.1.call-done = bf16[128,1024]{1,0:T(8,128)(2,1)} async-done(((bf16[512,1024]{1,0:T(8,128)(2,1)}), bf16[128,1024]{1,0:T(8,128)(2,1)}) %reduce-scatter.33.cloned.1.call-update) | async-done | bytes 262160 | tf_op jit(solution)/shard_map/reduce_scatter | solution.py:67
  1016.7 15.9 all-gather.54.cloned.1.call-done
  1195.9 85.8 %reduce-scatter.63.cloned.1.call-done = f32[128,1024]{1,0:T(8,128)} async-done(((f32[1024,1024]{1,0:T(8,128)}), f32[128,1024]{1,0:T(8,128)}) %reduce-scatter.63.cloned.1.call-update) | async-done | bytes 524304 | tf_op jit(solution)/shard_map/reduce_scatter | solution.py:298
  1284.2 89.3 %reduce-scatter.65.cloned.1.call-done = f32[1024,128]{1,0:T(8,128)} async-done(((f32[1024,1024]{1,0:T(8,128)}), f32[1024,128]{1,0:T(8,128)}) %reduce-scatter.65.cloned.1.call-update) | async-done | bytes 524304 | tf_op jit(solution)/shard_map/reduce_scatter | solution.py:299
  1376.1 76.0 %reduce-scatter.59.cloned.1.call-done = f32[128,3,256]{2,0,1:T(8,128)} async-done(((f32[1024,3,256]{2,0,1:T(8,128)}), f32[128,3,256]{2,0,1:T(8,128)}) %reduce-scatter.59.cloned.1.call-update) | async-done | bytes 393232 | tf_op jit(solution)/shard_map/reduce_scatter | solution.py:296
  1454.5 148.4 %reduce-scatter.55.cloned.1.call-done = f32[64,1024]{1,0:T(8,128)} async-done(((f32[2048,1024]{1,0:T(8,128)}), f32[64,1024]{1,0:T(8,128)}) %reduce-scatter.55.cloned.1.call-update) | async-done | bytes 262160 | tf_op jit(solution)/shard_map/reduce_scatter | solution.py:291
  1604.8 178.9 %reduce-scatter.57.cloned.1.call-done = f32[1024,128]{1,0:T(8,128)} async-done(((f32[1024,4096]{1,0:T(8,128)}), f32[1024,128]{1,0:T(8,128)}) %reduce-scatter.57.cloned.1.call-update) | async-done | bytes 524304 | tf_op jit(solution)/shard_map/reduce_scatter | solution.py:292
  (914 shorter events, 606.1 us)
Async XLA Ops:
  9.0 161.6 %all-gather.24.cloned.1.call-start = ((), (), s32[]{:S(2)}) async-start(), calls=%async_computation.23 | async-start | bytes 8650752 | tf_op jit(solution)/shard_map/all_gather | solution.py:171
  10.9 209.5 %all-gather.28.cloned.1.call-start = ((), (), s32[]{:S(2)}) async-start(), calls=%async_computation.25 | async-start | bytes 1769472 | tf_op jit(solution)/shard_map/all_gather | solution.py:175
  12.8 224.8 %all-gather.44.cloned.1.call-start = ((), (), s32[]{:S(2)}) async-start(), calls=%async_computation.39 | async-start | bytes 1310720 | tf_op jit(solution)/shard_map/all_gather | solution.py:55
  176.7 94.4 %reduce-scatter.35.cloned.1.call-start = ((), (), s32[]{:S(2)}) async-start(), calls=%async_computation.40 | async-start | bytes 1310720 | tf_op jit(solution)/shard_map/reduce_scatter | solution.py:67
  248.5 95.3 %all-gather.34.cloned.1.call-start = ((), (), s32[]{:S(2)}) async-start(), calls=%async_computation.29 | async-start | bytes 2359296 | tf_op jit(solution)/shard_map/all_gather | solution.py:178
  249.3 144.9 %all-gather.32.cloned.1.call-start = ((), (), s32[]{:S(2)}) async-start(), calls=%async_computation.28 | async-start | bytes 2359296 | tf_op jit(solution)/shard_map/all_gather | solution.py:177
  250.2 161.5 %all-gather.46.cloned.1.call-start = ((), (), s32[]{:S(2)}) async-start(), calls=%async_computation.41 | async-start | bytes 1310720 | tf_op jit(solution)/shard_map/all_gather | solution.py:55
  273.3 173.1 %reduce-scatter.51.cloned.1.call-start = ((), (), s32[]{:S(2)}) async-start(), calls=%async_computation.56 | async-start | bytes 1310720 | tf_op jit(solution)/shard_map/reduce_scatter | solution.py:80
  608.4 101.8 %all-gather.36.cloned.1.call-start = ((), (), s32[]{:S(2)}) async-start(), calls=%async_computation.31 | async-start | bytes 1310720 | tf_op jit(solution)/shard_map/all_gather | solution.py:55
  615.2 114.0 %all-gather.50.cloned.1.call-start = ((), (), s32[]{:S(2)}) async-start(), calls=%async_computation.45 | async-start | bytes 1310720 | tf_op jit(solution)/shard_map/all_gather | solution.py:59
  676.9 93.5 %reduce-scatter.31.cloned.1.call-start = ((), (), s32[]{:S(2)}) async-start(), calls=%async_computation.36 | async-start | bytes 1310720 | tf_op jit(solution)/shard_map/reduce_scatter | solution.py:67
  763.2 99.6 %all-gather.42.cloned.1.call-start = ((), (), s32[]{:S(2)}) async-start(), calls=%async_computation.37 | async-start | bytes 1310720 | tf_op jit(solution)/shard_map/all_gather | solution.py:55
  772.6 109.1 %all-gather.52.cloned.1.call-start = ((), (), s32[]{:S(2)}) async-start(), calls=%async_computation.47 | async-start | bytes 1310720 | tf_op jit(solution)/shard_map/all_gather | solution.py:59
  773.3 127.2 %all-gather.38.cloned.1.call-start = ((), (), s32[]{:S(2)}) async-start(), calls=%async_computation.33 | async-start | bytes 1310720 | tf_op jit(solution)/shard_map/all_gather | solution.py:55
  828.4 100.0 %reduce-scatter.47.cloned.1.call-start = ((), (), s32[]{:S(2)}) async-start(), calls=%async_computation.52 | async-start | bytes 1310720 | tf_op jit(solution)/shard_map/reduce_scatter | solution.py:80
  915.0 95.9 %reduce-scatter.33.cloned.1.call-start = ((), (), s32[]{:S(2)}) async-start(), calls=%async_computation.38 | async-start | bytes 1310720 | tf_op jit(solution)/shard_map/reduce_scatter | solution.py:67
  919.7 112.9 %all-gather.54.cloned.1.call-start = ((), (), s32[]{:S(2)}) async-start(), calls=%async_computation.49 | async-start | bytes 1310720 | tf_op jit(solution)/shard_map/all_gather | solution.py:59
  1016.5 104.8 %reduce-scatter.49.cloned.1.call-start = ((), (), s32[]{:S(2)}) async-start(), calls=%async_computation.54 | async-start | bytes 1310720 | tf_op jit(solution)/shard_map/reduce_scatter | solution.py:80
  1079.1 115.0 %reduce-scatter.61.cloned.1.call-start = ((), (), s32[]{:S(2)}) async-start(), calls=%async_computation.62 | async-start | bytes 1179648 | tf_op jit(solution)/shard_map/reduce_scatter | solution.py:297
  1084.4 197.2 %reduce-scatter.63.cloned.1.call-start = ((), (), s32[]{:S(2)}) async-start(), calls=%async_computation.63 | async-start | bytes 4718592 | tf_op jit(solution)/shard_map/reduce_scatter | solution.py:298
  1094.1 279.4 %reduce-scatter.65.cloned.1.call-start = ((), (), s32[]{:S(2)}) async-start(), calls=%async_computation.64 | async-start | bytes 4718592 | tf_op jit(solution)/shard_map/reduce_scatter | solution.py:299
  1106.3 345.8 %reduce-scatter.59.cloned.1.call-start = ((), (), s32[]{:S(2)}) async-start(), calls=%async_computation.61 | async-start | bytes 3538944 | tf_op jit(solution)/shard_map/reduce_scatter | solution.py:296
  1115.6 487.3 %reduce-scatter.55.cloned.1.call-start = ((), (), s32[]{:S(2)}) async-start(), calls=%async_computation.59 | async-start | bytes 8650752 | tf_op jit(solution)/shard_map/reduce_scatter | solution.py:291
  1142.8 641.0 %reduce-scatter.57.cloned.1.call-start = ((), (), s32[]{:S(2)}) async-start(), calls=%async_computation.60 | async-start | bytes 17301504 | tf_op jit(solution)/shard_map/reduce_scatter | solution.py:292
  (301 other events, 8751.6 us)
Sparse Core Ops, SparseCore 0:
  11.5 64.7 all-gather.21
  79.7 90.8 all-gather.23
  173.2 47.1 all-gather.27
  246.1 24.8 reduce-scatter.34
  292.7 51.0 all-gather.33
  346.7 47.4 all-gather.31
  421.5 24.8 reduce-scatter.50
  592.0 24.8 reduce-scatter.52
  620.0 24.8 reduce-scatter.38
  647.5 24.8 reduce-scatter.24
  745.4 24.8 reduce-scatter.30
  800.3 24.8 reduce-scatter.26
  903.5 24.8 reduce-scatter.46
  931.1 24.8 reduce-scatter.42
  958.6 24.8 reduce-scatter.28
  986.0 24.8 reduce-scatter.32
  1071.1 24.8 reduce-scatter.48
  1098.6 24.8 reduce-scatter.44
  1126.9 63.8 reduce-scatter.60
  1194.7 86.9 reduce-scatter.62
  1285.3 88.1 reduce-scatter.64
  1377.6 74.4 reduce-scatter.58
  1454.5 148.3 reduce-scatter.54
  1605.1 178.6 reduce-scatter.56
  (19 shorter events, 338.1 us)
where the time goes:
time: 1800 us; the launch traced here: 1790 us
  waiting for transfers between devices  1340 us (74%)
  matrix products  242 us (13%)
  other arithmetic  103 us (6%)
  local copies, waits for them, and re-layouts  43 us (2%)
  blocking collectives  39.9 us (2%)
  between operations  18.2 us (1%)
    reduce_scatter x1, waiting for transfers between devices, body(): lax.psum_scatter(adapt_total, ('dp', 'tensor'), scatter_dimension=1, tile...  179 us
    reduce_scatter x8, waiting for transfers between devices, scatter_rows(): lax.psum_scatter(term(jnp.int32(0), count * lax.axis_size('tensor')).asty...  177 us
    reduce_scatter x1, waiting for transfers between devices, body(): lax.psum_scatter(skip_total, ('dp', 'tensor'), scatter_dimension=0, tiled...  148 us
    all_gather x8, waiting for transfers between devices, gather_rows(): return lax.all_gather(values, 'tensor', axis=0, tiled=True)  118 us
    all_gather x8, waiting for transfers between devices, gather_grads(): return lax.all_gather(values, 'tensor', axis=0, tiled=True)  103 us
    reduce_scatter x8, waiting for transfers between devices, scatter_grads(): lax.psum_scatter(term(jnp.int32(0), count * lax.axis_size('tensor')).asty...  98.8 us
    all_gather x1, waiting for transfers between devices, body(): lax.all_gather(adapt_low, ('dp', 'tensor'), axis=1, tiled=True)  90.5 us
    reduce_scatter x1, waiting for transfers between devices, body(): lax.psum_scatter(down_total, 'dp', scatter_dimension=1, tiled=True)  89.3 us
  transfers between devices with their start and end apart: 43, of which 41 were waited for; matrix products, arithmetic and copies ran while one was open for 16% of the time, Pallas kernels for 0%

commit v1 on v0

v1 whole, which is shorter than its diff:
```python
import math

import jax
import jax.numpy as jnp
from jax import lax
from jax.sharding import PartitionSpec as P

HEAD_DIM = 64
STEP = 10

norm_eps = 1e-06
neg_large = -1e30
rates = (0.04, 0.06, 0.06, 0.6, 0.06, 0.03)
beta_first = 0.9
beta_second = 0.999
decay_rate = 0.01
adam_eps = 1e-08
low = jnp.bfloat16
f32 = jnp.float32


def bits_of(axis):
    count = lax.axis_size(axis).bit_length() - 1
    return [1 << place for place in reversed(range(count))]


def my_bit(axis, mask):
    return (lax.axis_index(axis) // mask) % 2


def swap(values, axis, mask):
    count = lax.axis_size(axis)
    return lax.ppermute(values, axis, [(i, i ^ mask) for i in range(count)])


def pick(values, index, dim):
    return lax.dynamic_index_in_dim(values, index, dim, keepdims=False)


def joined_pair(mine, other, bit, dim):
    first = jnp.where(bit == 1, other, mine)
    second = jnp.where(bit == 1, mine, other)
    return jnp.concatenate([first, second], axis=dim)


def gather_rows(shard, order):
    dp_bits, tensor_bits = bits_of("dp"), bits_of("tensor")
    pieces = {0: shard.reshape((1,) * len(dp_bits) + shard.shape)}
    for axis, mask in order:
        arrived = {key: swap(piece, axis, mask) for key, piece in pieces.items()}
        if axis == "tensor":
            pieces.update({key | mask: piece for key, piece in arrived.items()})
        else:
            bit = my_bit(axis, mask)
            pieces = {
                key: joined_pair(piece, arrived[key], bit, dp_bits.index(mask))
                for key, piece in pieces.items()
            }
    return [
        pieces[key].reshape(-1, shard.shape[1]) for key in range(1 << len(tensor_bits))
    ]


def gather_all(shard, order):
    dp_bits, tensor_bits = bits_of("dp"), bits_of("tensor")
    dims = [("dp", mask) for mask in dp_bits] + [("tensor", mask) for mask in tensor_bits]
    piece = shard.reshape((1,) * len(dims) + shard.shape)
    for axis, mask in order:
        arrived = swap(piece, axis, mask)
        piece = joined_pair(piece, arrived, my_bit(axis, mask), dims.index((axis, mask)))
    return piece.reshape(-1, shard.shape[1])


def scatter_rows(pieces, order):
    dp_bits = bits_of("dp")
    columns = pieces[0].shape[1]
    pieces = {
        key: piece.reshape((2,) * len(dp_bits) + (-1, columns)) for key, piece in enumerate(pieces)
    }
    for axis, mask in order:
        if axis == "tensor":
            arrived = {
                key ^ mask: swap(piece, axis, mask) for key, piece in pieces.items() if key & mask
            }
            kept = {key: piece for key, piece in pieces.items() if not key & mask}
        else:
            bit, dim = my_bit(axis, mask), dp_bits.index(mask)
            arrived = {
                key: swap(
                    lax.dynamic_slice_in_dim(piece, 1 - bit, 1, dim), axis, mask
                )
                for key, piece in pieces.items()
            }
            kept = {
                key: lax.dynamic_slice_in_dim(piece, bit, 1, dim) for key, piece in pieces.items()
            }
        pieces = {
            key: (piece.astype(f32) + arrived[key].astype(f32)).astype(piece.dtype)
            for key, piece in kept.items()
        }
    return pieces[0].reshape(-1, columns)


def scatter_all(total, order):
    dims = [("dp", mask) for mask in bits_of("dp")]
    dims += [("tensor", mask) for mask in bits_of("tensor")]
    columns = total.shape[1]
    piece = total.reshape((2,) * len(dims) + (-1, columns))
    for axis, mask in order:
        bit, dim = my_bit(axis, mask), dims.index((axis, mask))
        arrived = swap(lax.dynamic_slice_in_dim(piece, 1 - bit, 1, dim), axis, mask)
        kept = lax.dynamic_slice_in_dim(piece, bit, 1, dim)
        piece = (kept.astype(f32) + arrived.astype(f32)).astype(piece.dtype)
    return piece.reshape(-1, columns)


def to_owner(take):
    me = lax.axis_index("tensor")
    count = lax.axis_size("tensor")
    return [
        take(me) if step == 0 else swap(take(me ^ step), "tensor", step) for step in range(count)
    ]


def from_owner(blocks):
    me = lax.axis_index("tensor")
    arrived = [
        block if step == 0 else swap(block, "tensor", step) for step, block in enumerate(blocks)
    ]
    return unflip(jnp.stack(arrived), 0, "tensor")


def unflip(values, dim, axis):
    masks = bits_of(axis)
    shape = values.shape
    values = values.reshape(shape[:dim] + (2,) * len(masks) + shape[dim + 1 :])
    for place, mask in enumerate(masks):
        values = jnp.where(
            my_bit(axis, mask) == 1, jnp.flip(values, dim + place), values
        )
    return values.reshape(shape)


def exchange_all(values):
    shape = values.shape
    dims = [("dp", mask) for mask in bits_of("dp")]
    dims += [("tensor", mask) for mask in bits_of("tensor")]
    values = values.reshape((2,) * len(dims) + shape[2:])
    for dim, (axis, mask) in enumerate(dims):
        kept = lax.slice_in_dim(values, 0, 1, axis=dim)
        arrived = swap(lax.slice_in_dim(values, 1, 2, axis=dim), axis, mask)
        values = jnp.concatenate([kept, arrived], axis=dim)
    return values.reshape(shape)


def mean_last(values):
    return jnp.mean(values, axis=-1, keepdims=True)


def normalise(values):
    center = values - mean_last(values)
    inverse = lax.rsqrt(mean_last(center * center) + norm_eps)
    return center * inverse, inverse


def norm_back(normal, inverse, grad, scale):
    scaled = grad * (1.0 + scale)
    return inverse * (scaled - mean_last(scaled) - normal * mean_last(scaled * normal))


def turn(values, cosine, sine):
    half = HEAD_DIM // 2
    first, second = values[..., :half], values[..., half:]
    return jnp.concatenate([first * cosine - second * sine, second * cosine + first * sine], axis=-1)


def contract_last(left, right):
    return lax.dot_general(
        left, right, (((1,), (1,)), ((), ())), preferred_element_type=f32
    )


def contract_first(left, right):
    return lax.dot_general(
        left, right, (((0,), (0,)), ((), ())), preferred_element_type=f32
    )


def dot(left, right):
    return jnp.dot(left, right, preferred_element_type=f32)


def rounded_sum(terms):
    total = None
    for term in terms:
        term = term.astype(low).astype(f32)
        total = term if total is None else total + term
    return total


def scores_of(queries, keys, key_ok):
    scores = jnp.einsum("qhd,khd->hqk", queries, keys, preferred_element_type=f32)
    return jnp.where(key_ok[None, None, :], scores * HEAD_DIM**-0.5, neg_large)


def attend(queries, keys, values, key_ok):
    scores = scores_of(queries, keys, key_ok)
    top = jnp.max(scores, axis=-1, keepdims=True)
    weights = jnp.exp(scores - top)
    total = jnp.sum(weights, axis=-1, keepdims=True)
    shares = (weights / total).astype(low)
    mixed = jnp.einsum("hqk,khd->qhd", shares, values, preferred_element_type=f32)
    return mixed.astype(low), top + jnp.log(total)


def attend_back(queries, keys, values, key_ok, logsum, mixed_grad):
    scale = HEAD_DIM**-0.5
    shares = jnp.exp(scores_of(queries, keys, key_ok) - logsum)
    share_grad = jnp.einsum("qhd,khd->hqk", mixed_grad, values, preferred_element_type=f32)
    inner = jnp.sum(share_grad * shares, axis=-1, keepdims=True)
    score_grad = (shares * (share_grad - inner)).astype(low)
    query_grad = jnp.einsum("hqk,khd->qhd", score_grad, keys, preferred_element_type=f32)
    key_grad = jnp.einsum("hqk,qhd->khd", score_grad, queries, preferred_element_type=f32)
    value_grad = jnp.einsum(
        "hqk,qhd->khd", shares.astype(low), mixed_grad, preferred_element_type=f32
    )
    return query_grad * scale, key_grad * scale, value_grad


def gelu_pair(values):
    root = math.sqrt(2.0 / math.pi)
    cube = 0.044715 * values * values
    slope = jnp.tanh(root * values * (1.0 + cube))
    gate = 0.5 * (1.0 + slope)
    back = gate + 0.5 * values * (1.0 - slope * slope) * root * (1.0 + 3.0 * cube)
    return values * gate, back


def adam_update(master, first, second, grad, rate):
    first_new = beta_first * first + (1.0 - beta_first) * grad
    second_new = beta_second * second + (1.0 - beta_second) * grad * grad
    first_hat = first_new / (1.0 - beta_first**STEP)
    second_hat = second_new / (1.0 - beta_second**STEP)
    master_new = master - rate * (
        first_hat / (jnp.sqrt(second_hat) + adam_eps) + decay_rate * master
    )
    return (first_new, second_new, master_new, master_new.astype(low))


def orders():
    dp_bits, tensor_bits = bits_of("dp"), bits_of("tensor")
    far = [("dp", mask) for mask in dp_bits[:-2]]
    near = [("dp", mask) for mask in dp_bits[-2:]]
    across, core = ("tensor", tensor_bits[0]), ("tensor", tensor_bits[1])
    return (
        far + [across, near[0], near[1], core],
        far + [near[1], near[0], across, core],
    )


def body(
    frames,
    skip_frames,
    time_embed,
    lengths,
    out_grad,
    skip_weight,
    adapt_weight,
    input_weight,
    output_weight,
    up_weight,
    down_weight,
    skip_first,
    adapt_first,
    input_first,
    output_first,
    up_first,
    down_first,
    skip_second,
    adapt_second,
    input_second,
    output_second,
    up_second,
    down_second,
):
    micro, _, rows, width = frames.shape
    parts = lax.axis_size("tensor")
    groups = lax.axis_size("dp")
    length_all = rows * parts
    me = lax.axis_index("tensor")
    inner = input_weight.shape[2]
    heads = inner // HEAD_DIM
    highest = lax.Precision.HIGHEST
    order_p, order_q = orders()

    frame_blocks = to_owner(lambda index: pick(frames, index, 0)[0])
    skip_blocks = to_owner(lambda index: pick(skip_frames, index, 0)[0])
    joined = jnp.concatenate(
        [jnp.concatenate(frame_blocks, axis=0), jnp.concatenate(skip_blocks, axis=0)], axis=1
    )
    skip_all = gather_all(skip_weight.astype(low), order_p)

    adapt_low = adapt_weight.astype(low)
    time_values = time_embed[:, 0, :].astype(f32)
    time_low = jax.nn.silu(time_values).astype(low)
    time_all = unflip(time_low, 0, "tensor")[None]
    for mask in reversed(bits_of("dp")):
        time_all = jnp.concatenate([time_all, swap(time_all, "dp", mask)], axis=0)
    time_rows = time_all.reshape(groups * micro, width)
    adapt_mine = dot(time_rows, adapt_low).reshape(groups, micro, -1)
    adapt_vector = unflip(unflip(exchange_all(adapt_mine), 0, "dp"), 1, "tensor").reshape(-1)
    shift_one, scale_one, shift_two, scale_two = jnp.split(adapt_vector, 4)

    attention_shard = jnp.concatenate(
        [input_weight.reshape(-1, 3 * inner), output_weight.T], axis=1
    ).astype(low)
    attention_all = gather_rows(attention_shard, order_p)
    up_all = gather_rows(up_weight.astype(low), order_q)
    down_all = gather_rows(down_weight.T.astype(low), order_q)
    outer_blocks = to_owner(lambda index: pick(out_grad, index, 0)[0])

    row_index = jnp.concatenate(
        [(me ^ step) * rows + jnp.arange(rows, dtype=jnp.int32) for step in range(parts)]
    )
    length = pick(lengths, me, 0)[0]
    key_ok = row_index < length
    keep = key_ok.astype(f32)[:, None]
    half = HEAD_DIM // 2
    frequency = 10000.0 ** (-jnp.arange(half).astype(f32) / half)
    angles = row_index.astype(f32)[:, None] * frequency[None, :]
    cosine, sine = jnp.cos(angles)[:, None, :], jnp.sin(angles)[:, None, :]

    hidden = dot(joined, skip_all)
    normal_one, inverse_one = normalise(hidden)
    normed_one = (normal_one * (1.0 + scale_one) + shift_one).astype(low)
    shaped = (length_all, heads, HEAD_DIM)
    parted = []
    for weight in attention_all:
        project = dot(normed_one, weight[:, : 3 * inner])
        queries = turn(project[:, :inner].reshape(shaped), cosine, sine).astype(low)
        keys = turn(project[:, inner : 2 * inner].reshape(shaped), cosine, sine).astype(low)
        values = project[:, 2 * inner :].reshape(shaped).astype(low)
        mixed, logsum = attend(queries, keys, values, key_ok)
        parted.append((queries, keys, values, mixed.reshape(length_all, inner), logsum))
    attended = rounded_sum(
        contract_last(part[3], weight[:, 3 * inner :])
        for part, weight in zip(parted, attention_all)
    )
    middle = hidden + attended
    normal_two, inverse_two = normalise(middle)
    normed_two = (normal_two * (1.0 + scale_two) + shift_two).astype(low)
    outer_grad = keep * jnp.concatenate(outer_blocks, axis=0).astype(f32)
    outer_low = outer_grad.astype(low)
    gated, lifted_grad, up_grad, down_grad = [], [], [], []
    for up_part, down_part in zip(up_all, down_all):
        value, slope = gelu_pair(dot(normed_two, up_part))
        gated.append(value.astype(low))
        down_grad.append(contract_first(outer_low, gated[-1]).astype(low))
        lifted_grad.append((dot(outer_low, down_part) * slope).astype(low))
    down_sum = scatter_rows(down_grad, order_p[::-1]).T.astype(f32)
    for back in lifted_grad:
        up_grad.append(contract_first(normed_two, back).astype(low))
    up_sum = scatter_rows(up_grad, order_q[::-1]).astype(f32)
    normed_two_grad = rounded_sum(
        contract_last(back, up_part) for back, up_part in zip(lifted_grad, up_all)
    )
    fed = rounded_sum(contract_last(value, part) for value, part in zip(gated, down_all))
    result = (keep * (middle + fed)).astype(low)
    results = from_owner([result[step * rows : (step + 1) * rows] for step in range(parts)])

    middle_grad = outer_grad + norm_back(normal_two, inverse_two, normed_two_grad, scale_two)
    middle_low = middle_grad.astype(low)
    attention_grad, normed_one_terms = [], []
    for (queries, keys, values, mixed, logsum), weight in zip(parted, attention_all):
        mixed_grad = dot(middle_low, weight[:, 3 * inner :]).astype(low).reshape(shaped)
        query_grad, key_grad, value_grad = attend_back(
            queries, keys, values, key_ok, logsum, mixed_grad
        )
        project_grad = jnp.concatenate(
            [
                turn(query_grad, cosine, -sine).reshape(length_all, inner),
                turn(key_grad, cosine, -sine).reshape(length_all, inner),
                value_grad.reshape(length_all, inner),
            ],
            axis=1,
        ).astype(low)
        attention_grad.append(
            jnp.concatenate(
                [contract_first(normed_one, project_grad), contract_first(middle_low, mixed)],
                axis=1,
            ).astype(low)
        )
        normed_one_terms.append(contract_last(project_grad, weight[:, : 3 * inner]))
    attention_sum = scatter_rows(attention_grad, order_p[::-1]).astype(f32)
    input_sum = attention_sum[:, : 3 * inner].reshape(input_weight.shape)
    output_sum = attention_sum[:, 3 * inner :].T
    normed_one_grad = rounded_sum(normed_one_terms)
    hidden_grad = middle_grad + norm_back(normal_one, inverse_one, normed_one_grad, scale_one)
    hidden_low = hidden_grad.astype(low)
    skip_sum = scatter_all(contract_first(joined, hidden_low).astype(low), order_q[::-1]).astype(f32)
    hidden_back = from_owner([hidden_low[step * rows : (step + 1) * rows] for step in range(parts)])
    joined_grad = contract_last(hidden_back.reshape(micro * rows, width), skip_all)
    frame_grads = joined_grad[:, :width].reshape(frames.shape)
    skip_grads = joined_grad[:, width:].reshape(frames.shape)

    adapt_back = jnp.concatenate(
        [
            jnp.sum(normed_one_grad, axis=0),
            jnp.sum(normed_one_grad * normal_one, axis=0),
            jnp.sum(normed_two_grad, axis=0),
            jnp.sum(normed_two_grad * normal_two, axis=0),
        ]
    ).reshape(groups, parts, -1)
    adapt_rows = exchange_all(unflip(unflip(adapt_back, 0, "dp"), 1, "tensor"))
    adapt_rows = adapt_rows.reshape(groups * micro, -1)
    adapt_sum = lax.dot_general(
        time_rows.astype(f32), adapt_rows, (((0,), (0,)), ((), ())), precision=highest
    )
    time_part = lax.dot_general(
        adapt_rows, adapt_low.astype(f32), (((1,), (1,)), ((), ())), precision=highest
    ).reshape(groups, micro, width)
    for mask in bits_of("dp"):
        time_part = time_part[:mask] + swap(time_part[mask:], "dp", mask)
    time_part = unflip(time_part[0], 0, "tensor")
    for mask in bits_of("tensor"):
        time_part = time_part + swap(time_part, "tensor", mask)
    sigmoid = jax.nn.sigmoid(time_values)
    time_grad = time_part * (sigmoid * (1.0 + time_values * (1.0 - sigmoid)))

    skip_new = adam_update(skip_weight, skip_first, skip_second, skip_sum, rates[0])
    adapt_new = adam_update(adapt_weight, adapt_first, adapt_second, adapt_sum, rates[1])
    input_new = adam_update(input_weight, input_first, input_second, input_sum, rates[2])
    output_new = adam_update(output_weight, output_first, output_second, output_sum, rates[3])
    up_new = adam_update(up_weight, up_first, up_second, up_sum, rates[4])
    down_new = adam_update(down_weight, down_first, down_second, down_sum, rates[5])
    return (
        results[:, None],
        frame_grads,
        skip_grads,
        time_grad[:, None, :],
        *skip_new,
        *adapt_new,
        *input_new,
        *output_new,
        *up_new,
        *down_new,
    )


def solution(mesh):
    return jax.shard_map(
        body,
        mesh=mesh,
        in_specs=(
            P(None, "dp", "tensor", None),
            P(None, "dp", "tensor", None),
            P(None, "dp", None),
            P(None, "dp"),
            P(None, "dp", "tensor", None),
            P(("dp", "tensor"), None),
            P(None, ("dp", "tensor")),
            P("dp", None, "tensor"),
            P("tensor", "dp"),
            P("dp", "tensor"),
            P("tensor", "dp"),
            P(("dp", "tensor"), None),
            P(None, ("dp", "tensor")),
            P("dp", None, "tensor"),
            P("tensor", "dp"),
            P("dp", "tensor"),
            P("tensor", "dp"),
            P(("dp", "tensor"), None),
            P(None, ("dp", "tensor")),
            P("dp", None, "tensor"),
            P("tensor", "dp"),
            P("dp", "tensor"),
            P("tensor", "dp"),
        ),
        out_specs=(
            P(None, "dp", "tensor", None),
            P(None, "dp", "tensor", None),
            P(None, "dp", "tensor", None),
            P(None, "dp", None),
            P(("dp", "tensor"), None),
            P(("dp", "tensor"), None),
            P(("dp", "tensor"), None),
            P(("dp", "tensor"), None),
            P(None, ("dp", "tensor")),
            P(None, ("dp", "tensor")),
            P(None, ("dp", "tensor")),
            P(None, ("dp", "tensor")),
            P("dp", None, "tensor"),
            P("dp", None, "tensor"),
            P("dp", None, "tensor"),
            P("dp", None, "tensor"),
            P("tensor", "dp"),
            P("tensor", "dp"),
            P("tensor", "dp"),
            P("tensor", "dp"),
            P("dp", "tensor"),
            P("dp", "tensor"),
            P("dp", "tensor"),
            P("dp", "tensor"),
            P("tensor", "dp"),
            P("tensor", "dp"),
            P("tensor", "dp"),
            P("tensor", "dp"),
        ),
        check_vma=False,
    )
```

time: 1800 us -> 833 us (0.46)
  waiting for transfers between devices: 1340 us -> 374 us
  local copies, waits for them, and re-layouts: 43 us -> 145 us
  matrix products: 242 us -> 149 us
  starting transfers between devices: 4.46 us -> 73.2 us
  blocking collectives: 39.9 us -> 0 us
  other arithmetic: 103 us -> 78.4 us
    reduce_scatter x22 -> x0, waiting for transfers between devices: 854 us -> none  [the longest x1 179 us: body(): lax.psum_scatter(adapt_total, ('dp', 'tensor'), scatter_dimension=1, tile...]
    all_gather x21 -> x0, waiting for transfers between devices: 486 us -> none  [the longest x8 118 us: gather_rows(): return lax.all_gather(values, 'tensor', axis=0, tiled=True)]
    ppermute x0 -> x85, waiting for transfers between devices: none -> 374 us  [swap(): return lax.ppermute(values, axis, [(i, i ^ mask) for i in range(count)])]
    ppermute x0 -> x85, starting transfers between devices: none -> 73.2 us  [swap(): return lax.ppermute(values, axis, [(i, i ^ mask) for i in range(count)])]
    dot_general x67 -> x61, matrix products: 183 us -> 115 us  [the longest x17 46 us: contract_first(): lax.dot_general(left, right, (((0,), (0,)), ((), ())), preferred_element_...]
    reduce_sum x31 -> x6, other arithmetic: 35.4 us -> 3.07 us  [the longest x4 2.38 us: attend(): total = jnp.sum(weights, axis=-1, keepdims=True)]
    ppermute x0 -> x8, local copies, waits for them, and re-layouts: none -> 32.1 us  [swap(): return lax.ppermute(values, axis, [(i, i ^ mask) for i in range(count)])]
    all_gather x1 -> x0, blocking collectives: 29.4 us -> none  [body(): lax.all_gather(output_weight.astype(jnp.bfloat16), 'dp', axis=1, tiled=True)]
  transfers between devices with their start and end apart: 43 -> 85, of which waited for: 41 -> 35; matrix products, arithmetic and copies ran while one was open for 16% -> 35% of each run, Pallas kernels for 0% -> 0%
where the time goes in v1:
time: 833 us; the launch traced here: 824 us
  waiting for transfers between devices  374 us (45%)
  matrix products  149 us (18%)
  local copies, waits for them, and re-layouts  145 us (17%)
  other arithmetic  78.4 us (9%)
  starting transfers between devices  73.2 us (9%)
    ppermute x85, waiting for transfers between devices, swap(): return lax.ppermute(values, axis, [(i, i ^ mask) for i in range(count)])  374 us
    ppermute x85, starting transfers between devices, swap(): return lax.ppermute(values, axis, [(i, i ^ mask) for i in range(count)])  73.2 us
    dot_general x17, matrix products, contract_first(): lax.dot_general(left, right, (((0,), (0,)), ((), ())), preferred_element_...  46 us
    dot_general x18, matrix products, dot(): return jnp.dot(left, right, preferred_element_type=f32)  46 us
    dot_general x17, matrix products, contract_last(): lax.dot_general(left, right, (((1,), (1,)), ((), ())), preferred_element_...  33.9 us
    ppermute x8, local copies, waits for them, and re-layouts, swap(): return lax.ppermute(values, axis, [(i, i ^ mask) for i in range(count)])  32.1 us
    unnamed x362, local copies, waits for them, and re-layouts  23.7 us
    convert_element_type x16, other arithmetic, scatter_rows(): (piece.astype(f32) + arrived[key].astype(f32)).astype(piece.dtype)  19.4 us
  transfers between devices with their start and end apart: 85, of which 35 were waited for; matrix products, arithmetic and copies ran while one was open for 35% of the time, Pallas kernels for 0%

profile of v1, /device:TPU:0, one launch (start us, length us, event | category | flops | bytes accessed | tf_op | source)
XLA Modules:
  0.0 823.5 jit_solution(8005232133202758077)
XLA Ops:
  29.3 9.2 %collective-permute-done.13 = bf16[4,4,1024]{2,1,0:T(4,128)(2,1)S(1)} collective-permute-done((bf16[4,4,1024]{2,1,0:T(4,128)(2,1)S(1)}, bf16[4,4,1024]{2,1,0:T(4,128)(2,1)S(1)}, u32[]{:S(2)}, u32[]{:S(2)}) %collective-permute-start.13) | collective-permute-done | bytes 32800 | tf_op jit(solution)/shard_map/ppermute | solution.py:33
  53.5 6.8 collective-permute-done.28
  65.5 10.4 %collective-permute-done.8 = bf16[2,1,1,2,1,64,1024]{6,5,4,3,2,1,0:T(8,128)(2,1)S(1)} collective-permute-done((bf16[2,1,1,2,1,64,1024]{6,5,4,3,2,1,0:T(8,128)(2,1)S(1)}, bf16[2,1,1,2,1,64,1024]{6,5,4,3,2,1,0:T(8,128)(2,1)S(1)}, u32[]{:S(2)}, u32[]{:S(2)}) %collective-permute-start.8) | collective-permute-done | bytes 524320 | tf_op jit(solution)/shard_map/ppermute | solution.py:33
  77.6 20.7 %collective-permute-done.29 = bf16[2,1,2,128,1024]{3,4,2,1,0:T(8,128)(2,1)S(1)} collective-permute-done((bf16[2,1,2,128,1024]{3,4,2,1,0:T(8,128)(2,1)S(1)}, bf16[2,1,2,128,1024]{3,4,2,1,0:T(8,128)(2,1)S(1)}, u32[]{:S(2)}, u32[]{:S(2)}) %collective-permute-start.29) | collective-permute-done | bytes 1048608 | tf_op jit(solution)/shard_map/ppermute | solution.py:33
  122.4 14.0 %collective-permute-done.25 = bf16[2,2,1,128,1024]{3,4,2,1,0:T(8,128)(2,1)} collective-permute-done((bf16[2,2,1,128,1024]{3,4,2,1,0:T(8,128)(2,1)}, bf16[2,2,1,128,1024]{3,4,2,1,0:T(8,128)(2,1)}, u32[]{:S(2)}, u32[]{:S(2)}) %collective-permute-start.25) | collective-permute-done | bytes 1048608 | tf_op jit(solution)/shard_map/ppermute | solution.py:33
  167.2 5.8 collective-permute-done.4
  302.1 20.8 %collective-permute-done.81 = bf16[2,2,1,128,1024]{3,4,2,1,0:T(8,128)(2,1)} collective-permute-done((bf16[2,2,1,128,1024]{3,4,2,1,0:T(8,128)(2,1)}, bf16[2,2,1,128,1024]{3,4,2,1,0:T(8,128)(2,1)}, u32[]{:S(2)}, u32[]{:S(2)}) %collective-permute-start.81) | collective-permute-done | bytes 1048608 | tf_op jit(solution)/shard_map/ppermute | solution.py:33
  328.2 16.7 %collective-permute-done.78 = bf16[2,2,1,128,1024]{3,4,2,1,0:T(8,128)(2,1)} collective-permute-done((bf16[2,2,1,128,1024]{3,4,2,1,0:T(8,128)(2,1)S(1)}, bf16[2,2,1,128,1024]{3,4,2,1,0:T(8,128)(2,1)}, u32[]{:S(2)}, u32[]{:S(2)}) %collective-permute-start.78) | collective-permute-done | bytes 1048608 | tf_op jit(solution)/shard_map/ppermute | solution.py:33
  351.8 9.6 %collective-permute-done.79 = bf16[2,1,1,128,1024]{3,4,2,1,0:T(8,128)(2,1)} collective-permute-done((bf16[2,1,1,128,1024]{3,4,2,1,0:T(8,128)(2,1)}, bf16[2,1,1,128,1024]{3,4,2,1,0:T(8,128)(2,1)}, u32[]{:S(2)}, u32[]{:S(2)}) %collective-permute-start.79) | collective-permute-done | bytes 524320 | tf_op jit(solution)/shard_map/ppermute | solution.py:33
  369.0 11.0 %collective-permute-done.84 = bf16[1,1,1,128,1024]{3,4,2,1,0:T(8,128)(2,1)S(1)} collective-permute-done((bf16[1,1,1,128,1024]{3,4,2,1,0:T(8,128)(2,1)S(1)}, bf16[1,1,1,128,1024]{3,4,2,1,0:T(8,128)(2,1)S(1)}, u32[]{:S(2)}, u32[]{:S(2)}) %collective-permute-start.84) | collective-permute-done | bytes 262176 | tf_op jit(solution)/shard_map/ppermute | solution.py:33
  383.2 13.4 %collective-permute-done.30 = bf16[1,1,1,128,1024]{3,4,2,1,0:T(8,128)(2,1)S(1)} collective-permute-done((bf16[1,1,1,128,1024]{3,4,2,1,0:T(8,128)(2,1)S(1)}, bf16[1,1,1,128,1024]{3,4,2,1,0:T(8,128)(2,1)S(1)}, u32[]{:S(2)}, u32[]{:S(2)}) %collective-permute-start.30) | collective-permute-done | bytes 262176 | tf_op jit(solution)/shard_map/ppermute | solution.py:33
  397.2 13.3 %collective-permute-done.31 = bf16[2,1,1,128,1024]{3,4,2,1,0:T(8,128)(2,1)S(1)} collective-permute-done((bf16[2,1,1,128,1024]{3,4,2,1,0:T(8,128)(2,1)S(1)}, bf16[2,1,1,128,1024]{3,4,2,1,0:T(8,128)(2,1)S(1)}, u32[]{:S(2)}, u32[]{:S(2)}) %collective-permute-start.31) | collective-permute-done | bytes 524320 | tf_op jit(solution)/shard_map/ppermute | solution.py:33
  411.8 24.5 %collective-permute-done.32 = bf16[2,1,2,128,1024]{3,4,2,1,0:T(8,128)(2,1)} collective-permute-done((bf16[2,1,2,128,1024]{3,4,2,1,0:T(8,128)(2,1)}, bf16[2,1,2,128,1024]{3,4,2,1,0:T(8,128)(2,1)}, u32[]{:S(2)}, u32[]{:S(2)}) %collective-permute-start.32) | collective-permute-done | bytes 1048608 | tf_op jit(solution)/shard_map/ppermute | solution.py:33
  456.3 29.1 %collective-permute-done.36 = bf16[2,2,2,128,1024]{3,4,2,1,0:T(8,128)(2,1)} collective-permute-done((bf16[2,2,2,128,1024]{3,4,2,1,0:T(8,128)(2,1)}, bf16[2,2,2,128,1024]{3,4,2,1,0:T(8,128)(2,1)}, u32[]{:S(2)}, u32[]{:S(2)}) %collective-permute-start.36) | collective-permute-done | bytes 2097184 | tf_op jit(solution)/shard_map/ppermute | solution.py:33
  489.4 5.6 multiply_convert_fusion.5
  585.1 5.7 convolution_convert_fusion
  645.4 5.4 collective-permute-done.46
  668.7 62.8 %collective-permute-done.59 = bf16[2,2,2,1,1,64,1024]{6,5,4,3,2,1,0:T(8,128)(2,1)S(1)} collective-permute-done((bf16[2,2,2,1,1,64,1024]{6,5,4,3,2,1,0:T(8,128)(2,1)S(1)}, bf16[2,2,2,1,1,64,1024]{6,5,4,3,2,1,0:T(8,128)(2,1)S(1)}, u32[]{:S(2)}, u32[]{:S(2)}) %collective-permute-start.59) | collective-permute-done | bytes 1048608 | tf_op jit(solution)/shard_map/ppermute | solution.py:33
  736.9 10.0 %collective-permute-done.60 = bf16[2,1,2,1,1,64,1024]{6,5,4,3,2,1,0:T(8,128)(2,1)S(1)} collective-permute-done((bf16[2,1,2,1,1,64,1024]{6,5,4,3,2,1,0:T(8,128)(2,1)S(1)}, bf16[2,1,2,1,1,64,1024]{6,5,4,3,2,1,0:T(8,128)(2,1)S(1)}, u32[]{:S(2)}, u32[]{:S(2)}) %collective-permute-start.60) | collective-permute-done | bytes 524320 | tf_op jit(solution)/shard_map/ppermute | solution.py:33
  751.5 17.9 %collective-permute-done.68 = bf16[2,1,1,128,1024]{3,4,2,1,0:T(8,128)(2,1)S(1)} collective-permute-done((bf16[2,1,1,128,1024]{3,4,2,1,0:T(8,128)(2,1)S(1)}, bf16[2,1,1,128,1024]{3,4,2,1,0:T(8,128)(2,1)S(1)}, u32[]{:S(2)}, u32[]{:S(2)}) %collective-permute-start.68) | collective-permute-done | bytes 524320 | tf_op jit(solution)/shard_map/ppermute | solution.py:33
  774.5 6.0 collective-permute-done.69
  780.7 12.4 %collective-permute-done.74 = bf16[2,1,2,128,1024]{4,3,2,1,0:T(8,128)(2,1)S(1)} collective-permute-done((bf16[2,1,2,128,1024]{4,3,2,1,0:T(8,128)(2,1)S(1)}, bf16[2,1,2,128,1024]{4,3,2,1,0:T(8,128)(2,1)S(1)}, u32[]{:S(2)}, u32[]{:S(2)}) %collective-permute-start.74) | collective-permute-done | bytes 1048608 | tf_op jit(solution)/shard_map/ppermute | solution.py:33
  796.3 10.8 %collective-permute-done.70 = bf16[1,1,1,128,1024]{3,4,2,1,0:T(8,128)(2,1)S(1)} collective-permute-done((bf16[1,1,1,128,1024]{3,4,2,1,0:T(8,128)(2,1)S(1)}, bf16[1,1,1,128,1024]{3,4,2,1,0:T(8,128)(2,1)S(1)}, u32[]{:S(2)}, u32[]{:S(2)}) %collective-permute-start.70) | collective-permute-done | bytes 262176 | tf_op jit(solution)/shard_map/ppermute | solution.py:33
  810.6 11.2 %collective-permute-done.76 = bf16[1,1,1,128,1024]{4,3,2,1,0:T(8,128)(2,1)S(1)} collective-permute-done((bf16[1,1,1,128,1024]{4,3,2,1,0:T(8,128)(2,1)S(1)}, bf16[1,1,1,128,1024]{4,3,2,1,0:T(8,128)(2,1)S(1)}, u32[]{:S(2)}, u32[]{:S(2)}) %collective-permute-start.76) | collective-permute-done | bytes 262176 | tf_op jit(solution)/shard_map/ppermute | solution.py:33
  (822 shorter events, 466.5 us)
Async XLA Ops:
  5.9 38.7 %collective-permute-start.6 = (bf16[1,1,1,1,1,64,1024]{6,5,4,3,2,1,0:T(8,128)(2,1)S(1)}, bf16[1,1,1,1,1,64,1024]{6,5,4,3,2,1,0:T(8,128)(2,1)}, u32[]{:S(2)}, u32[]{:S(2)}) collective-permute-start(bf16[1,1,1,1,1,64,1024]{6,5,4,3,2,1,0:T(8,128)(2,1)S(1)} %convert_bitcast_fusion.3), channel_id=1, source_target_pairs={{0,16},{4,20},{8,24},{12,28},{16,0},{20,4},{24,8},{28,12},{1,17},{... | collective-permute-start | bytes 393224 | tf_op jit(solution)/shard_map/ppermute | solution.py:33
  99.9 48.0 %collective-permute-start.35 = (bf16[2,2,2,128,1024]{3,4,2,1,0:T(8,128)(2,1)}, bf16[2,2,2,128,1024]{3,4,2,1,0:T(8,128)(2,1)}, u32[]{:S(2)}, u32[]{:S(2)}) collective-permute-start(bf16[2,2,2,128,1024]{3,4,2,1,0:T(8,128)(2,1)} %pad_maximum_fusion.4), channel_id=1, source_target_pairs={{0,2},{1,3},{2,0},{3,1},{4,6},{5,7},{6,4},{7,5},{8,10},{9,11},{10,... | collective-permute-start | bytes 6291464 | tf_op jit(solution)/shard_map/ppermute | solution.py:33
  100.5 53.0 %collective-permute-start.33 = (bf16[2,2,2,128,1024]{3,4,2,1,0:T(8,128)(2,1)}, bf16[2,2,2,128,1024]{3,4,2,1,0:T(8,128)(2,1)}, u32[]{:S(2)}, u32[]{:S(2)}) collective-permute-start(bf16[2,2,2,128,1024]{3,4,2,1,0:T(8,128)(2,1)} %pad_maximum_fusion.4), channel_id=1, source_target_pairs={{0,1},{1,0},{2,3},{3,2},{4,5},{5,4},{6,7},{7,6},{8,9},{9,8},{10,11... | collective-permute-start | bytes 6291464 | tf_op jit(solution)/shard_map/ppermute | solution.py:33
  102.1 41.2 %collective-permute-start.22 = (bf16[2,2,2,128,1024]{3,4,2,1,0:T(8,128)(2,1)}, bf16[2,2,2,128,1024]{3,4,2,1,0:T(8,128)(2,1)}, u32[]{:S(2)}, u32[]{:S(2)}) collective-permute-start(bf16[2,2,2,128,1024]{3,4,2,1,0:T(8,128)(2,1)} %pad_maximum_fusion.2), channel_id=1, source_target_pairs={{0,1},{1,0},{2,3},{3,2},{4,5},{5,4},{6,7},{7,6},{8,9},{9,8},{10,11... | collective-permute-start | bytes 6291464 | tf_op jit(solution)/shard_map/ppermute | solution.py:33
  109.3 49.5 %collective-permute-start.10 = (bf16[2,2,2,2,1,64,1024]{6,5,4,3,2,1,0:T(8,128)(2,1)}, bf16[2,2,2,2,1,64,1024]{6,5,4,3,2,1,0:T(8,128)(2,1)}, u32[]{:S(2)}, u32[]{:S(2)}) collective-permute-start(bf16[2,2,2,2,1,64,1024]{6,5,4,3,2,1,0:T(8,128)(2,1)} %pad_maximum_fusion.1), channel_id=1, source_target_pairs={{0,1},{1,0},{2,3},{3,2},{4,5},{5,4},{6,7},{7,6},{8,9},{9,8},{10,11... | collective-permute-start | bytes 6291464 | tf_op jit(solution)/shard_map/ppermute | solution.py:33
  162.9 88.0 %collective-permute-start.42 = (bf16[128,1024]{1,0:T(8,128)(2,1)}, bf16[128,1024]{1,0:T(8,128)(2,1)}, u32[]{:S(2)}, u32[]{:S(2)}) collective-permute-start(bf16[128,1024]{1,0:T(8,128)(2,1)} %get-tuple-element.175), channel_id=1, source_target_pairs={{0,1},{1,0},{2,3},{3,2},{4,5},{5,4},{6,7},{7,6},{8,9},{9,8},{10,11... | collective-permute-start | bytes 786440 | tf_op jit(solution)/shard_map/ppermute | solution.py:33
  163.0 88.0 %collective-permute-start.44 = (bf16[128,1024]{1,0:T(8,128)(2,1)}, bf16[128,1024]{1,0:T(8,128)(2,1)}, u32[]{:S(2)}, u32[]{:S(2)}) collective-permute-start(bf16[128,1024]{1,0:T(8,128)(2,1)} %get-tuple-element.176), channel_id=1, source_target_pairs={{0,3},{1,2},{2,1},{3,0},{4,7},{5,6},{6,5},{7,4},{8,11},{9,10},{10,... | collective-permute-start | bytes 786440 | tf_op jit(solution)/shard_map/ppermute | solution.py:33
  163.6 87.3 %collective-permute-start.43 = (bf16[128,1024]{1,0:T(8,128)(2,1)}, bf16[128,1024]{1,0:T(8,128)(2,1)}, u32[]{:S(2)}, u32[]{:S(2)}) collective-permute-start(bf16[128,1024]{1,0:T(8,128)(2,1)} %get-tuple-element.177), channel_id=1, source_target_pairs={{0,2},{1,3},{2,0},{3,1},{4,6},{5,7},{6,4},{7,5},{8,10},{9,11},{10,... | collective-permute-start | bytes 786440 | tf_op jit(solution)/shard_map/ppermute | solution.py:33
  166.2 38.3 %collective-permute-start.26 = (bf16[2,2,2,128,1024]{3,4,2,1,0:T(8,128)(2,1)S(1)}, bf16[2,2,2,128,1024]{3,4,2,1,0:T(8,128)(2,1)}, u32[]{:S(2)}, u32[]{:S(2)}) collective-permute-start(bf16[2,2,2,128,1024]{3,4,2,1,0:T(8,128)(2,1)S(1)} %copy-done.14), channel_id=1, source_target_pairs={{0,1},{1,0},{2,3},{3,2},{4,5},{5,4},{6,7},{7,6},{8,9},{9,8},{10,11... | collective-permute-start | bytes 6291464 | tf_op jit(solution)/shard_map/ppermute | solution.py:33
  173.0 71.0 %collective-permute-start.37 = (bf16[2,2,2,128,1024]{3,4,2,1,0:T(8,128)(2,1)}, bf16[2,2,2,128,1024]{3,4,2,1,0:T(8,128)(2,1)}, u32[]{:S(2)}, u32[]{:S(2)}) collective-permute-start(bf16[2,2,2,128,1024]{3,4,2,1,0:T(8,128)(2,1)} %collective-permute-done.35), channel_id=1, source_target_pairs={{0,1},{1,0},{2,3},{3,2},{4,5},{5,4},{6,7},{7,6},{8,9},{9,8},{10,11... | collective-permute-start | bytes 6291464 | tf_op jit(solution)/shard_map/ppermute | solution.py:33
  300.5 44.4 %collective-permute-start.78 = (bf16[2,2,1,128,1024]{3,4,2,1,0:T(8,128)(2,1)S(1)}, bf16[2,2,1,128,1024]{3,4,2,1,0:T(8,128)(2,1)}, u32[]{:S(2)}, u32[]{:S(2)}) collective-permute-start(bf16[2,2,1,128,1024]{3,4,2,1,0:T(8,128)(2,1)S(1)} %constant_dynamic-slice_fusion.4), channel_id=1, source_target_pairs={{0,4},{4,0},{8,12},{12,8},{16,20},{20,16},{24,28},{28,24},{1,5},{5... | collective-permute-start | bytes 3145736 | tf_op jit(solution)/shard_map/ppermute | solution.py:33
  439.3 46.1 %collective-permute-start.36 = (bf16[2,2,2,128,1024]{3,4,2,1,0:T(8,128)(2,1)}, bf16[2,2,2,128,1024]{3,4,2,1,0:T(8,128)(2,1)}, u32[]{:S(2)}, u32[]{:S(2)}) collective-permute-start(bf16[2,2,2,128,1024]{3,4,2,1,0:T(8,128)(2,1)} %pad_maximum_fusion.5), channel_id=1, source_target_pairs={{0,2},{1,3},{2,0},{3,1},{4,6},{5,7},{6,4},{7,5},{8,10},{9,11},{10,... | collective-permute-start | bytes 6291464 | tf_op jit(solution)/shard_map/ppermute | solution.py:33
  444.1 50.9 %collective-permute-start.34 = (bf16[2,2,2,128,1024]{3,4,2,1,0:T(8,128)(2,1)}, bf16[2,2,2,128,1024]{3,4,2,1,0:T(8,128)(2,1)}, u32[]{:S(2)}, u32[]{:S(2)}) collective-permute-start(bf16[2,2,2,128,1024]{3,4,2,1,0:T(8,128)(2,1)} %pad_maximum_fusion.5), channel_id=1, source_target_pairs={{0,1},{1,0},{2,3},{3,2},{4,5},{5,4},{6,7},{7,6},{8,9},{9,8},{10,11... | collective-permute-start | bytes 6291464 | tf_op jit(solution)/shard_map/ppermute | solution.py:33
  565.1 93.6 %collective-permute-start.72 = (bf16[2,2,2,128,1024]{4,3,2,1,0:T(8,128)(2,1)}, bf16[2,2,2,128,1024]{4,3,2,1,0:T(8,128)(2,1)}, u32[]{:S(2)}, u32[]{:S(2)}) collective-permute-start(bf16[2,2,2,128,1024]{4,3,2,1,0:T(8,128)(2,1)} %bitcast.135), channel_id=1, source_target_pairs={{0,1},{1,0},{2,3},{3,2},{4,5},{5,4},{6,7},{7,6},{8,9},{9,8},{10,11... | collective-permute-start | bytes 6291464 | tf_op jit(solution)/shard_map/ppermute | solution.py:33
  569.1 69.0 %collective-permute-start.41 = (bf16[128,1024]{1,0:T(8,128)(2,1)}, bf16[128,1024]{1,0:T(8,128)(2,1)}, u32[]{:S(2)}, u32[]{:S(2)}) collective-permute-start(bf16[128,1024]{1,0:T(8,128)(2,1)} %get-tuple-element.179), channel_id=1, source_target_pairs={{0,3},{1,2},{2,1},{3,0},{4,7},{5,6},{6,5},{7,4},{8,11},{9,10},{10,... | collective-permute-start | bytes 786440 | tf_op jit(solution)/shard_map/ppermute | solution.py:33
  569.7 68.8 %collective-permute-start.40 = (bf16[128,1024]{1,0:T(8,128)(2,1)}, bf16[128,1024]{1,0:T(8,128)(2,1)}, u32[]{:S(2)}, u32[]{:S(2)}) collective-permute-start(bf16[128,1024]{1,0:T(8,128)(2,1)} %get-tuple-element.180), channel_id=1, source_target_pairs={{0,2},{1,3},{2,0},{3,1},{4,6},{5,7},{6,4},{7,5},{8,10},{9,11},{10,... | collective-permute-start | bytes 786440 | tf_op jit(solution)/shard_map/ppermute | solution.py:33
  571.2 68.0 %collective-permute-start.39 = (bf16[128,1024]{1,0:T(8,128)(2,1)}, bf16[128,1024]{1,0:T(8,128)(2,1)}, u32[]{:S(2)}, u32[]{:S(2)}) collective-permute-start(bf16[128,1024]{1,0:T(8,128)(2,1)} %get-tuple-element.181), channel_id=1, source_target_pairs={{0,1},{1,0},{2,3},{3,2},{4,5},{5,4},{6,7},{7,6},{8,9},{9,8},{10,11... | collective-permute-start | bytes 786440 | tf_op jit(solution)/shard_map/ppermute | solution.py:33
  644.7 103.0 %collective-permute-start.71 = (bf16[2,2,2,128,1024]{4,3,2,1,0:T(8,128)(2,1)}, bf16[2,2,2,128,1024]{4,3,2,1,0:T(8,128)(2,1)S(1)}, u32[]{:S(2)}, u32[]{:S(2)}) collective-permute-start(bf16[2,2,2,128,1024]{4,3,2,1,0:T(8,128)(2,1)} %bitcast.477), channel_id=1, source_target_pairs={{0,1},{1,0},{2,3},{3,2},{4,5},{5,4},{6,7},{7,6},{8,9},{9,8},{10,11... | collective-permute-start | bytes 6291464 | tf_op jit(solution)/shard_map/ppermute | solution.py:33
  661.4 86.4 %collective-permute-start.73 = (bf16[2,2,2,128,1024]{4,3,2,1,0:T(8,128)(2,1)S(1)}, bf16[2,2,2,128,1024]{4,3,2,1,0:T(8,128)(2,1)S(1)}, u32[]{:S(2)}, u32[]{:S(2)}) collective-permute-start(bf16[2,2,2,128,1024]{4,3,2,1,0:T(8,128)(2,1)S(1)} %fusion), channel_id=1, source_target_pairs={{0,2},{1,3},{2,0},{3,1},{4,6},{5,7},{6,4},{7,5},{8,10},{9,11},{10,... | collective-permute-start | bytes 6291464 | tf_op jit(solution)/shard_map/ppermute | solution.py:33
  664.0 67.5 %collective-permute-start.59 = (bf16[2,2,2,1,1,64,1024]{6,5,4,3,2,1,0:T(8,128)(2,1)S(1)}, bf16[2,2,2,1,1,64,1024]{6,5,4,3,2,1,0:T(8,128)(2,1)S(1)}, u32[]{:S(2)}, u32[]{:S(2)}) collective-permute-start(bf16[2,2,2,1,1,64,1024]{6,5,4,3,2,1,0:T(8,128)(2,1)S(1)} %constant_dynamic-slice_fusion.16), channel_id=1, source_target_pairs={{0,2},{1,3},{2,0},{3,1},{4,6},{5,7},{6,4},{7,5},{8,10},{9,11},{10,... | collective-permute-start | bytes 3145736 | tf_op jit(solution)/shard_map/ppermute | solution.py:33
  665.6 68.4 %collective-permute-start.64 = (bf16[2,2,1,128,1024]{3,4,2,1,0:T(8,128)(2,1)S(1)}, bf16[2,2,1,128,1024]{3,4,2,1,0:T(8,128)(2,1)S(1)}, u32[]{:S(2)}, u32[]{:S(2)}) collective-permute-start(bf16[2,2,1,128,1024]{3,4,2,1,0:T(8,128)(2,1)S(1)} %constant_dynamic-slice_fusion.12), channel_id=1, source_target_pairs={{0,4},{4,0},{8,12},{12,8},{16,20},{20,16},{24,28},{28,24},{1,5},{5... | collective-permute-start | bytes 3145736 | tf_op jit(solution)/shard_map/ppermute | solution.py:33
  667.2 67.3 %collective-permute-start.67 = (bf16[2,2,1,128,1024]{3,4,2,1,0:T(8,128)(2,1)S(1)}, bf16[2,2,1,128,1024]{3,4,2,1,0:T(8,128)(2,1)S(1)}, u32[]{:S(2)}, u32[]{:S(2)}) collective-permute-start(bf16[2,2,1,128,1024]{3,4,2,1,0:T(8,128)(2,1)S(1)} %constant_dynamic-slice_fusion.10), channel_id=1, source_target_pairs={{0,4},{4,0},{8,12},{12,8},{16,20},{20,16},{24,28},{28,24},{1,5},{5... | collective-permute-start | bytes 3145736 | tf_op jit(solution)/shard_map/ppermute | solution.py:33
  734.4 40.1 %collective-permute-start.65 = (bf16[2,1,1,128,1024]{3,4,2,1,0:T(8,128)(2,1)S(1)}, bf16[2,1,1,128,1024]{3,4,2,1,0:T(8,128)(2,1)S(1)}, u32[]{:S(2)}, u32[]{:S(2)}) collective-permute-start(bf16[2,1,1,128,1024]{3,4,2,1,0:T(8,128)(2,1)S(1)} %constant_dynamic-slice_fusion.11), channel_id=1, source_target_pairs={{0,8},{4,12},{8,0},{12,4},{16,24},{20,28},{24,16},{28,20},{1,9},{5... | collective-permute-start | bytes 1572872 | tf_op jit(solution)/shard_map/ppermute | solution.py:33
  749.4 43.7 %collective-permute-start.74 = (bf16[2,1,2,128,1024]{4,3,2,1,0:T(8,128)(2,1)S(1)}, bf16[2,1,2,128,1024]{4,3,2,1,0:T(8,128)(2,1)S(1)}, u32[]{:S(2)}, u32[]{:S(2)}) collective-permute-start(bf16[2,1,2,128,1024]{4,3,2,1,0:T(8,128)(2,1)S(1)} %constant_dynamic-slice_fusion.7), channel_id=1, source_target_pairs={{0,8},{4,12},{8,0},{12,4},{16,24},{20,28},{24,16},{28,20},{1,9},{5... | collective-permute-start | bytes 3145736 | tf_op jit(solution)/shard_map/ppermute | solution.py:33
  (241 other events, 2165.6 us)

commit v2 on v1

v2 whole, which is shorter than its diff:
```python
import functools
import math

import jax
import jax.numpy as jnp
from jax import lax
from jax.experimental import pallas as pl
from jax.experimental.pallas import tpu as pltpu
from jax.sharding import PartitionSpec as P

HEAD_DIM = 64
STEP = 10
LIMIT = 56 * 1024 * 1024

norm_eps = 1e-06
neg_large = -1e30
rates = (0.04, 0.06, 0.06, 0.6, 0.06, 0.03)
beta_first = 0.9
beta_second = 0.999
decay_rate = 0.01
adam_eps = 1e-08
low = jnp.bfloat16
f32 = jnp.float32


def bits_of(axis):
    count = lax.axis_size(axis).bit_length() - 1
    return [1 << place for place in reversed(range(count))]


def my_bit(axis, mask):
    return (lax.axis_index(axis) // mask) % 2


def swap(values, axis, mask):
    count = lax.axis_size(axis)
    return lax.ppermute(values, axis, [(i, i ^ mask) for i in range(count)])


def pick(values, index, dim):
    return lax.dynamic_index_in_dim(values, index, dim, keepdims=False)


def struct(shape, dtype):
    return jax.ShapeDtypeStruct(shape, dtype)


def whole(array):
    shape = array.shape
    return pl.BlockSpec(shape, lambda *_: (0,) * len(shape))


def each(array):
    shape = array.shape[1:]
    return pl.BlockSpec((None,) + shape, lambda i, *_: (i,) + (0,) * len(shape))


class Line:
    def __init__(self):
        self.last = ()

    def run(self, kernel, outs, ins, *, grid=(1,), in_specs=None, out_specs=None, scratch=(), flops=0, prefetch=()):
        in_specs = [whole(value) for value in ins] if in_specs is None else in_specs
        out_specs = [whole(value) for value in outs] if out_specs is None else out_specs
        deps = self.last
        skip = len(prefetch) + len(ins)

        def inner(*refs):
            kernel(*refs[:skip], *refs[skip + len(deps) :])

        moved = sum(value.size * value.dtype.itemsize for value in (*ins, *outs))
        results = pl.pallas_call(
            inner,
            grid_spec=pltpu.PrefetchScalarGridSpec(
                num_scalar_prefetch=len(prefetch),
                grid=grid,
                in_specs=in_specs + [pl.BlockSpec(memory_space=pl.ANY)] * len(deps),
                out_specs=out_specs,
                scratch_shapes=list(scratch),
            ),
            out_shape=list(outs),
            cost_estimate=pl.CostEstimate(flops=flops, bytes_accessed=moved, transcendentals=0),
            compiler_params=pltpu.CompilerParams(vmem_limit_bytes=LIMIT),
        )(*prefetch, *ins, *deps)
        self.last = (results[-1],)
        return results

    def need(self, *values):
        self.last += values

    def tie(self, values):
        return lax.optimization_barrier((values, self.last))[0]


def merge(line, pairs, bits):
    count = len(pairs)

    def kernel(bits, *refs):
        for place in range(count):
            (mine, other), out = refs[2 * place : 2 * place + 2], refs[2 * count + place]
            out[:, pl.ds(bits[place], 1)] = mine[...][:, None]
            out[:, pl.ds(1 - bits[place], 1)] = other[...][:, None]

    outs = [struct((mine.shape[0], 2) + mine.shape[1:], low) for mine, _ in pairs]
    return line.run(kernel, outs, [value for pair in pairs for value in pair], prefetch=[bits])


def split(line, pairs, bits):
    count = len(pairs)

    def kernel(bits, *refs):
        for place in range(count):
            terms, outs = refs[2 * place : 2 * place + 2], refs[2 * (count + place) : 2 * (count + place) + 2]
            for index, out in zip((1 - bits[place], bits[place]), outs):
                total = sum(term[:, pl.ds(index, 1)].astype(f32) for term in terms)
                out[...] = total[:, 0].astype(low)

    outs = [struct(pair[0].shape[:1] + pair[0].shape[2:], low) for pair in pairs for _ in range(2)]
    results = line.run(kernel, outs, [value for pair in pairs for value in pair], prefetch=[bits])
    return list(zip(results[::2], results[1::2]))


def bit_array(axis, mask):
    return my_bit(axis, mask).astype(jnp.int32)[None]


def bit_of(step, relative):
    return jnp.zeros((1,), jnp.int32) if step in relative else bit_array(*step)


class Gather:
    def __init__(self, line, shard, order, dims, relative):
        self.line, self.order, self.dims, self.relative = line, list(order), dims, relative
        self.sizes = {dim: 1 for dim in dims}
        self.columns = shard.shape[1]
        self.mine = shard
        self.begin()

    def begin(self):
        self.step = self.order.pop(0)
        self.arrived = swap(self.mine, *self.step)

    def pair(self):
        place = self.dims.index(self.step)
        outer = math.prod(self.sizes[dim] for dim in self.dims[:place])
        shape = (outer, -1, self.columns)
        return self.mine.reshape(shape), self.arrived.reshape(shape)

    def end(self, piece):
        self.mine = piece.reshape(-1, self.columns)
        self.sizes[self.step] = 2
        self.begin()


class Scatter:
    def __init__(self, line, kept, sent, order, dims, relative):
        self.line, self.order, self.dims, self.relative = line, list(order), dims, relative
        self.sizes = {dim: 2 if dim in self.order else 1 for dim in dims}
        self.columns = kept.shape[-1]
        self.begin(kept, sent)

    def begin(self, kept, sent):
        self.step = self.order.pop(0)
        self.sizes[self.step] = 1
        flat = (-1, self.columns)
        self.terms = [kept.reshape(flat), swap(sent.reshape(flat), *self.step)]

    def pair(self):
        place = self.dims.index(self.order[0])
        outer = math.prod(self.sizes[dim] for dim in self.dims[:place])
        return [term.reshape(outer, 2, -1, self.columns) for term in self.terms]

    def end(self, halves):
        sent, kept = halves
        self.begin(kept, sent)


def go(line, *walks):
    gathers = isinstance(walks[0], Gather)
    steps = [walk.step if gathers else walk.order[0] for walk in walks]
    bits = jnp.concatenate([bit_of(step, walk.relative) for step, walk in zip(steps, walks)])
    results = (merge if gathers else split)(line, [walk.pair() for walk in walks], bits)
    for walk, result in zip(walks, results):
        walk.end(result)


class Weights:
    def __init__(self, pair, step, across):
        self.across = step == across
        self.mine, self.arrived = pair
        if not self.across:
            shape = (2, -1) + self.mine.shape[1:]
            self.mine, self.arrived = self.mine.reshape(shape), self.arrived.reshape(shape)

    def flip(self, core):
        other = object.__new__(Weights)
        other.across = self.across
        other.mine, other.arrived = swap(self.mine, *core), swap(self.arrived, *core)
        return other

    def ins(self):
        return [self.mine, self.arrived]

    def specs(self):
        return [whole(value) if self.across else each(value) for value in self.ins()]

    def scratch(self):
        shape = self.mine.shape[1:]
        return pltpu.VMEM((1,) + shape if self.across else (shape[0], 2) + shape[1:], low)

    def load(self, bit, refs, held):
        mine, arrived = refs
        if self.across:
            step = pl.program_id(0)

            @pl.when(step == 0)
            def _():
                held[...] = mine[...]

            @pl.when(step > 0)
            def _():
                held[...] = arrived[...]

        else:
            held[:, pl.ds(bit, 1)] = mine[...][:, None]
            held[:, pl.ds(1 - bit, 1)] = arrived[...][:, None]
        return held[...].reshape(-1, held.shape[-1])


class Halves:
    def __init__(self, weights, arrived=None):
        self.across, self.arrived = weights.across, arrived
        columns = weights.mine.shape[-1]
        width = weights.mine.shape[1] * (1 if self.across else 2 * weights.mine.shape[2])
        if arrived is None:
            self.outs = [struct((2, width, columns), low)]
        elif self.across:
            self.outs = [struct((width, columns), low)] * 2
        else:
            self.outs = [struct(weights.mine.shape, low)] * 2

    def ins(self):
        return [] if self.arrived is None else [self.arrived]

    def in_specs(self):
        return [each(value) for value in self.ins()]

    def specs(self):
        if self.arrived is not None and self.across:
            return [whole(value) for value in self.outs]
        return [each(value) for value in self.outs]

    def store(self, bit, ins, outs, total):
        if self.arrived is None:
            outs[0][...] = total.astype(low)
            return
        kept, sent = outs
        total = (total + ins[0][...].astype(f32)).astype(low)
        if self.across:
            step = pl.program_id(0)

            @pl.when(step == 0)
            def _():
                kept[...] = total

            @pl.when(step > 0)
            def _():
                sent[...] = total

        else:
            total = total.reshape(kept.shape[0], 2, *kept.shape[1:])
            kept[...] = jnp.where(bit == 1, total[:, 1], total[:, 0])
            sent[...] = jnp.where(bit == 1, total[:, 0], total[:, 1])


def to_owner(take):
    me = lax.axis_index("tensor")
    count = lax.axis_size("tensor")
    return [
        take(me) if step == 0 else swap(take(me ^ step), "tensor", step) for step in range(count)
    ]


def from_owner(blocks):
    return [block if step == 0 else swap(block, "tensor", step) for step, block in enumerate(blocks)]


def unflip(values, dim, axis):
    masks = bits_of(axis)
    shape = values.shape
    values = values.reshape(shape[:dim] + (2,) * len(masks) + shape[dim + 1 :])
    for place, mask in enumerate(masks):
        values = jnp.where(
            my_bit(axis, mask) == 1, jnp.flip(values, dim + place), values
        )
    return values.reshape(shape)


def exchange_all(values):
    shape = values.shape
    dims = [("dp", mask) for mask in bits_of("dp")]
    dims += [("tensor", mask) for mask in bits_of("tensor")]
    values = values.reshape((2,) * len(dims) + shape[2:])
    for dim, (axis, mask) in enumerate(dims):
        kept = lax.slice_in_dim(values, 0, 1, axis=dim)
        arrived = swap(lax.slice_in_dim(values, 1, 2, axis=dim), axis, mask)
        values = jnp.concatenate([kept, arrived], axis=dim)
    return values.reshape(shape)


def mean_last(values):
    return jnp.mean(values, axis=-1, keepdims=True)


def normalise(values):
    center = values - mean_last(values)
    inverse = lax.rsqrt(mean_last(center * center) + norm_eps)
    return center * inverse, inverse


def norm_back(normal, inverse, grad, scale):
    scaled = grad * (1.0 + scale)
    return inverse * (scaled - mean_last(scaled) - normal * mean_last(scaled * normal))


def dg(left, right, left_dim, right_dim):
    return lax.dot_general(
        left, right, (((left_dim,), (right_dim,)), ((), ())), preferred_element_type=f32
    )


def pack_attention_kernel(skip, inputs, output, *outs):
    *skip_outs, qk, vo = outs
    half = skip.shape[1] // 2
    inner = inputs.shape[2]
    for place, out in enumerate(skip_outs):
        out[...] = skip[:, place * half : (place + 1) * half].astype(low)
    qk[:, :inner] = inputs[0].astype(low)
    qk[:, inner:] = inputs[1].astype(low)
    vo[:, :inner] = inputs[2].astype(low)
    vo[:, inner:] = output[...].T.astype(low)


def pack_attention(line, skip, inputs, output):
    outs = [struct((skip.shape[0], skip.shape[1] // 2), low)] * 2
    outs += [struct((inputs.shape[1], 2 * inputs.shape[2]), low)] * 2
    return line.run(pack_attention_kernel, outs, [skip, inputs, output])


def pack_feed_kernel(up, down, *outs):
    half = up.shape[1] // 2
    for place, out in enumerate(outs):
        here = slice(place * half, (place + 1) * half)
        out[:, :half] = up[:, here].astype(low)
        out[:, half:] = down[here, :].T.astype(low)


def pack_feed(line, up, down):
    return line.run(pack_feed_kernel, [struct(up.shape, low)] * 2, [up, down])


def put_together(bit, pairs, held):
    for (mine, arrived), full in zip(pairs, held):
        full[:, pl.ds(bit, 1)] = mine[...][:, None]
        full[:, pl.ds(1 - bit, 1)] = arrived[...][:, None]
    return [full[...].reshape(-1, full.shape[-1]) for full in held]


def together(pairs):
    return [pltpu.VMEM((pair[0].shape[0], 2) + pair[0].shape[1:], low) for pair in pairs]


def enter(line, blocks, pairs, bit, keep):
    count = len(blocks)
    length, depth = sum(block.shape[0] for block in blocks), pairs[0][0].shape[0] * 2 * pairs[0][0].shape[1]
    half = pairs[0][0].shape[-1]

    def kernel(bit, *refs):
        blocks, skips, keep = refs[:count], refs[count : count + 4], refs[count + 4]
        hidden, outer, joined, *held = refs[count + 5 :]
        rows = blocks[0].shape[0]
        for place, block in enumerate(blocks):
            here = slice(place * rows, (place + 1) * rows)
            joined[here, :] = block[:, :depth]
            outer[here, :] = (keep[here, :] * block[:, depth:].astype(f32)).astype(low)
        first, second = put_together(bit[0], (skips[:2], skips[2:]), held)
        hidden[:, :half] = dg(joined[...], first, 1, 0)
        hidden[:, half:] = dg(joined[...], second, 1, 0)

    return line.run(
        kernel,
        [struct((length, 2 * half), f32), struct((length, 2 * half), low)],
        [*blocks, *pairs[0], *pairs[1], keep],
        prefetch=[bit],
        scratch=[pltpu.VMEM((length, depth), low), *together(pairs)],
        flops=4 * length * half * depth,
    )


def half_turn(values):
    lanes = lax.broadcasted_iota(jnp.int32, values.shape, 1) % HEAD_DIM
    width = values.shape[1]
    half = HEAD_DIM // 2
    return jnp.where(
        lanes < half, pltpu.roll(values, width - half, 1), pltpu.roll(values, half, 1)
    )


def shares_of(keys, queries, ok):
    scores = jnp.where(ok > 0, dg(keys, queries, 1, 1), neg_large)
    weights = jnp.exp(scores - jnp.max(scores, axis=0, keepdims=True))
    return weights * (1.0 / jnp.sum(weights, axis=0, keepdims=True))


def attend_piece(normed, qk, vo, cosine, sine, ok, held, mixed):
    inner = qk.shape[1] // 2
    rows = normed.shape[0]
    for part in range(3):
        weight = (qk[:, :inner], qk[:, inner:], vo[:, :inner])[part]
        project = dg(normed[...], weight, 1, 0)
        if part < 2:
            project = project * cosine[...] + half_turn(project) * sine[...]
        if part == 0:
            project = project * HEAD_DIM**-0.5
        held[:, part * inner : (part + 1) * inner] = project.astype(low)
    queries = held[:, :inner]
    keys = held[:, inner : 2 * inner]
    values = held[:, 2 * inner :]
    owner = lax.broadcasted_iota(jnp.int32, (rows, inner), 1) // HEAD_DIM
    zero = jnp.zeros((), low)
    total = None
    for head in range(inner // HEAD_DIM):
        mine = owner == head
        shares = shares_of(keys, jnp.where(mine, queries, zero), ok[...]).astype(low)
        term = dg(shares, jnp.where(mine, values, zero), 0, 0)
        total = term if total is None else total + term
    mixed[...] = total.astype(low)
    return dg(mixed[...], vo[:, inner:], 1, 1).astype(low).astype(f32)


def add_up(total, term, step):
    @pl.when(step == 0)
    def _():
        total[...] = term

    @pl.when(step > 0)
    def _():
        total[...] += term


def attend(line, qk, vo, bits, cosine, sine, ok, hidden, shift, scale, normed=None, before=None):
    rows, width = hidden.shape
    inner = qk.mine.shape[-1] // 2
    total = struct((rows, width), f32)
    outs = [struct((2, rows, 3 * inner), low), struct((2, rows, inner), low), total, struct((rows, width), low)]
    plain = [cosine, sine, ok, hidden, shift, scale]
    plain += [] if before is None else [normed, before]

    def kernel(bits, *refs):
        qk_refs, vo_refs, refs = refs[:2], refs[2:4], refs[4:]
        (cosine, sine, ok, hidden, shift, scale, *more), refs = refs[: len(plain)], refs[len(plain) :]
        held, mixed, out, after, qk_held, vo_held = refs
        step = pl.program_id(0)

        def modulate(values):
            normal, _ = normalise(values)
            after[...] = (normal * (1.0 + scale[...]) + shift[...]).astype(low)

        if not more:

            @pl.when(step == 0)
            def _():
                modulate(hidden[...])

        qk_now = qk.load(bits[0], qk_refs, qk_held)
        vo_now = vo.load(bits[1], vo_refs, vo_held)
        normed = more[0] if more else after
        add_up(out, attend_piece(normed, qk_now, vo_now, cosine, sine, ok, held, mixed), step)
        if more:

            @pl.when(step == pl.num_programs(0) - 1)
            def _():
                total = hidden[...] + (more[1][...] + out[...])
                out[...] = total
                modulate(total)

    return line.run(
        kernel,
        outs,
        [*qk.ins(), *vo.ins(), *plain],
        grid=(2,),
        in_specs=[*qk.specs(), *vo.specs(), *(whole(value) for value in plain)],
        out_specs=[each(outs[0]), each(outs[1]), whole(total), whole(total)],
        scratch=[qk.scratch(), vo.scratch()],
        prefetch=[bits],
        flops=2 * rows * (8 * width * inner + 16 * rows * inner),
    )


def gelu_pair(values):
    root = math.sqrt(2.0 / math.pi)
    cube = 0.044715 * values * values
    slope = jnp.tanh(root * values * (1.0 + cube))
    gate = 0.5 * (1.0 + slope)
    back = gate + 0.5 * values * (1.0 - slope * slope) * root * (1.0 + 3.0 * cube)
    return values * gate, back


def feed(line, normed, outer, weights, bits, place, halves):
    rows, width = normed.shape
    half = weights.mine.shape[-1] // 2
    end = struct((rows, width), low)
    extra = halves.ins()

    def kernel(bits, *refs):
        pair, (normed, outer), refs = refs[:2], refs[2:4], refs[4:]
        before, refs = refs[: len(extra)], refs[len(extra) :]
        outs, (fed, back, fed_total, back_total, held) = refs[: len(halves.outs)], refs[len(halves.outs) :]
        step = pl.program_id(0)
        now = weights.load(bits[place], pair, held)
        up, down = now[:, :half], now[:, half:]
        value, slope = gelu_pair(dg(normed[...], up, 1, 0))
        gated = value.astype(low)
        lifted = (dg(outer[...], down, 1, 0) * slope).astype(low)
        grad = jnp.concatenate([dg(normed[...], lifted, 0, 0), dg(outer[...], gated, 0, 0)], axis=1)
        halves.store(bits[place], before, outs, grad)
        add_up(fed_total, dg(gated, down, 1, 1), step)
        add_up(back_total, dg(lifted, up, 1, 1), step)

        @pl.when(step == pl.num_programs(0) - 1)
        def _():
            fed[...] = fed_total[...].astype(low)
            back[...] = back_total[...].astype(low)

    return line.run(
        kernel,
        [*halves.outs, end, end],
        [*weights.ins(), normed, outer, *extra],
        grid=(2,),
        in_specs=[*weights.specs(), whole(normed), whole(outer), *halves.in_specs()],
        out_specs=[*halves.specs(), whole(end), whole(end)],
        scratch=[pltpu.VMEM((rows, width), f32)] * 2 + [weights.scratch()],
        prefetch=[bits],
        flops=24 * rows * width * half,
    )


def bend_kernel(middle, outer, keep, scale, *refs):
    *parts, result, middle_grad, middle_low, sums = refs
    count = len(parts) // 2
    fed = sum(part[...].astype(f32) for part in parts[:count])
    grad = sum(part[...].astype(f32) for part in parts[count:])
    result[...] = (keep[...] * (middle[...] + fed)).astype(low)
    normal, inverse = normalise(middle[...])
    total = outer[...].astype(f32) + norm_back(normal, inverse, grad, scale[...])
    middle_grad[...] = total
    middle_low[...] = total.astype(low)
    sums[0:1, :] = jnp.sum(grad, axis=0, keepdims=True)
    sums[1:2, :] = jnp.sum(grad * normal, axis=0, keepdims=True)


def bend(line, middle, outer, keep, scale, fed, back):
    shape = middle.shape
    outs = [struct(shape, low), struct(shape, f32), struct((2, shape[1]), f32), struct(shape, low)]

    def kernel(*refs):
        *refs, sums, middle_low = refs
        bend_kernel(*refs, middle_low, sums)

    return line.run(kernel, outs, [middle, outer, keep, scale, *fed, *back])


def back_piece(normed, middle_low, qk, vo, held, mixed, cosine, sine, ok, project):
    inner = qk.shape[1] // 2
    rows = normed.shape[0]
    queries = held[:, :inner]
    keys = held[:, inner : 2 * inner]
    values = held[:, 2 * inner :]
    above = dg(middle_low[...], vo[:, inner:], 1, 0).astype(low)
    owner = lax.broadcasted_iota(jnp.int32, (rows, inner), 1) // HEAD_DIM
    zero = jnp.zeros((), low)
    query_grad = key_grad = value_grad = jnp.zeros((rows, inner), f32)
    for head in range(inner // HEAD_DIM):
        mine = owner == head
        queries_here = jnp.where(mine, queries, zero)
        above_here = jnp.where(mine, above, zero)
        shares = shares_of(keys, queries_here, ok[...])
        share_grad = dg(values, above_here, 1, 1)
        inside = jnp.sum(share_grad * shares, axis=0, keepdims=True)
        score_grad = (shares * (share_grad - inside)).astype(low)
        value_grad += dg(shares.astype(low), above_here, 1, 0)
        key_grad += dg(score_grad, queries_here, 1, 0)
        query_grad += dg(score_grad, jnp.where(mine, keys, zero), 0, 0)
    query_grad = query_grad * HEAD_DIM**-0.5
    for place, grad in enumerate((query_grad, key_grad)):
        turned = grad * cosine[...] - half_turn(grad) * sine[...]
        project[:, place * inner : (place + 1) * inner] = turned.astype(low)
    project[:, 2 * inner :] = value_grad.astype(low)
    qk_grad = dg(normed[...], project[:, : 2 * inner], 0, 0)
    vo_grad = jnp.concatenate(
        [dg(normed[...], project[:, 2 * inner :], 0, 0), dg(middle_low[...], mixed[...], 0, 0)], axis=1
    )
    term = dg(project[:, : 2 * inner], qk, 1, 1)
    term += dg(project[:, 2 * inner :], vo[:, :inner], 1, 1)
    return qk_grad, vo_grad, term.astype(low).astype(f32)


def attend_back(line, normed, middle_low, qk, vo, bits, held, mixed, cosine, sine, ok, qk_halves, vo_halves, last=()):
    rows, width = normed.shape
    inner = qk.mine.shape[-1] // 2
    plain = [normed, middle_low, held, mixed, cosine, sine, ok, *last]
    extra = [*qk_halves.ins(), *vo_halves.ins()]
    counts = len(qk_halves.outs), len(vo_halves.outs)
    scratch = [pltpu.VMEM((rows, 3 * inner), low), qk.scratch(), vo.scratch()]
    outs = [*qk_halves.outs, *vo_halves.outs]
    out_specs = [*qk_halves.specs(), *vo_halves.specs()]
    if last:
        ends = [struct((2, width), f32), struct((rows, width), low)]
        scratch = [pltpu.VMEM((rows, width), f32)] + scratch
    else:
        ends = [struct((rows, width), f32)]

    def kernel(bits, *refs):
        qk_refs, vo_refs, refs = refs[:2], refs[2:4], refs[4:]
        (*args, cosine, sine, ok), refs = refs[:7], refs[7:]
        more, refs = refs[: len(last)], refs[len(last) :]
        before, refs = refs[: len(extra)], refs[len(extra) :]
        qk_outs, refs = refs[: counts[0]], refs[counts[0] :]
        vo_outs, refs = refs[: counts[1]], refs[counts[1] :]
        *ends, total, project, qk_held, vo_held = refs
        step = pl.program_id(0)
        normed, middle_low, held, mixed = args
        qk_now = qk.load(bits[0], qk_refs, qk_held)
        vo_now = vo.load(bits[1], vo_refs, vo_held)
        qk_grad, vo_grad, term = back_piece(
            normed, middle_low, qk_now, vo_now, held, mixed, cosine, sine, ok, project
        )
        qk_halves.store(bits[0], before[:1], qk_outs, qk_grad)
        vo_halves.store(bits[1], before[1:], vo_outs, vo_grad)
        add_up(total, term, step)
        if last:
            ahead, hidden, middle_grad, scale = more
            sums, hidden_low = ends

            @pl.when(step == pl.num_programs(0) - 1)
            def _():
                grad = ahead[...] + total[...]
                normal, inverse = normalise(hidden[...])
                hidden_low[...] = (
                    middle_grad[...] + norm_back(normal, inverse, grad, scale[...])
                ).astype(low)
                sums[0:1, :] = jnp.sum(grad, axis=0, keepdims=True)
                sums[1:2, :] = jnp.sum(grad * normal, axis=0, keepdims=True)

    return line.run(
        kernel,
        [*outs, *ends],
        [*qk.ins(), *vo.ins(), *plain, *extra],
        grid=(2,),
        in_specs=[
            *qk.specs(),
            *vo.specs(),
            *(each(value) if value.ndim == 3 else whole(value) for value in plain),
            *qk_halves.in_specs(),
            *vo_halves.in_specs(),
        ],
        out_specs=out_specs + [whole(value) for value in ends],
        scratch=scratch,
        prefetch=[bits],
        flops=2 * rows * (16 * width * inner + 40 * rows * inner),
    )


def leave(line, blocks, hidden_low, bit, parts):
    count = len(blocks)
    length, width = hidden_low.shape
    depth = 2 * width
    half = width // 2

    def kernel(bit, *refs):
        blocks, hidden_low, outs, joined = refs[:count], refs[count], refs[count + 1 : count + 5], refs[-1]
        rows = blocks[0].shape[0]
        for place, block in enumerate(blocks):
            joined[place * rows : (place + 1) * rows, :] = block[:, :depth]
        mine = bit[0] == 1
        for place in range(2):
            sent, kept = outs[2 * place : 2 * place + 2]
            total = dg(joined[...], hidden_low[:, place * half : (place + 1) * half], 0, 0)
            total = total.reshape(sent.shape[0], 2, -1, half)
            sent[...] = jnp.where(mine, total[:, 0], total[:, 1]).astype(low)
            kept[...] = jnp.where(mine, total[:, 1], total[:, 0]).astype(low)

    return line.run(
        kernel,
        [struct((parts // 2, depth // parts, half), low)] * 4,
        [*blocks, hidden_low],
        prefetch=[bit],
        scratch=[pltpu.VMEM((length, depth), low)],
        flops=2 * length * width * depth,
    )


def inputs_back(line, blocks, pairs, bits):
    count = len(blocks)
    length, width = sum(block.shape[0] for block in blocks), blocks[0].shape[1]
    half = width // 2

    def kernel(bits, *refs):
        blocks, skips = refs[:count], refs[count : count + 4]
        frame_grad, skip_grad, hidden, *held = refs[count + 4 :]
        rows = blocks[0].shape[0]
        for place, block in enumerate(blocks):
            start = pl.multiple_of((bits[1] ^ place) * rows, rows)
            hidden[pl.ds(start, rows), :] = block[...]
        first, second = put_together(bits[0], (skips[:2], skips[2:]), held)
        for here, out in ((slice(0, width), frame_grad), (slice(width, 2 * width), skip_grad)):
            total = dg(hidden[:, :half], first[here, :], 1, 1)
            out[...] = total + dg(hidden[:, half:], second[here, :], 1, 1)

    return line.run(
        kernel,
        [struct((length, width), f32)] * 2,
        [*blocks, *pairs[0], *pairs[1]],
        prefetch=[bits],
        scratch=[pltpu.VMEM((length, width), low), *together(pairs)],
        flops=4 * length * width * width,
    )


def adam_update(master, first, second, grad, rate):
    first_new = beta_first * first + (1.0 - beta_first) * grad
    second_new = beta_second * second + (1.0 - beta_second) * grad * grad
    first_hat = first_new / (1.0 - beta_first**STEP)
    second_hat = second_new / (1.0 - beta_second**STEP)
    master_new = master - rate * (
        first_hat / (jnp.sqrt(second_hat) + adam_eps) + decay_rate * master
    )
    return (first_new, second_new, master_new, master_new.astype(low))


def added(pair):
    return pair[0][...].astype(f32) + pair[1][...].astype(f32)


def store_update(states, grad, rate, outs):
    for out, value in zip(outs, adam_update(*(state[...] for state in states), grad, rate)):
        out[...] = value


def update_outs(master):
    return [struct(master.shape, f32)] * 3 + [struct(master.shape, low)]


def update_feed(line, first, second, ups, downs):
    def kernel(*refs):
        pairs, ups, downs = (refs[:2], refs[2:4]), refs[4:7], refs[7:10]
        up_outs, down_outs = refs[10:14], refs[14:18]
        totals = [added(pair) for pair in pairs]
        half = totals[0].shape[1] // 2
        store_update(ups, jnp.concatenate([total[:, :half] for total in totals], axis=1), rates[4], up_outs)
        store_update(
            downs, jnp.concatenate([total[:, half:].T for total in totals], axis=0), rates[5], down_outs
        )

    return line.run(kernel, update_outs(ups[0]) + update_outs(downs[0]), [*first, *second, *ups, *downs])


def update_attention(line, qk, vo, inputs, outputs):
    def kernel(*refs):
        qk, vo, inputs, outputs = refs[:2], refs[2:4], refs[4:7], refs[7:10]
        input_outs, output_outs = refs[10:14], refs[14:18]
        qk, vo = added(qk), added(vo)
        inner = qk.shape[1] // 2
        for place, grad in enumerate((qk[:, :inner], qk[:, inner:], vo[:, :inner])):
            store_update(
                [state.at[place] for state in inputs], grad, rates[2], [out.at[place] for out in input_outs]
            )
        store_update(outputs, vo[:, inner:].T, rates[3], output_outs)

    return line.run(kernel, update_outs(inputs[0]) + update_outs(outputs[0]), [*qk, *vo, *inputs, *outputs])


def update_skip(line, first, second, skips):
    def kernel(*refs):
        grad = jnp.concatenate([added(refs[:2]), added(refs[2:4])], axis=1)
        store_update(refs[4:7], grad, rates[0], refs[7:11])

    return line.run(kernel, update_outs(skips[0]), [*first, *second, *skips])


def orders():
    dp_bits, tensor_bits = bits_of("dp"), bits_of("tensor")
    far = [("dp", mask) for mask in dp_bits[:-2]]
    near, next_near = ("dp", dp_bits[-1]), ("dp", dp_bits[-2])
    across = ("tensor", tensor_bits[0])
    return (
        far + [next_near, across, near],
        far + [next_near, near, across],
        far + [near, across, next_near],
    )


def body(
    frames,
    skip_frames,
    time_embed,
    lengths,
    out_grad,
    skip_weight,
    adapt_weight,
    input_weight,
    output_weight,
    up_weight,
    down_weight,
    skip_first,
    adapt_first,
    input_first,
    output_first,
    up_first,
    down_first,
    skip_second,
    adapt_second,
    input_second,
    output_second,
    up_second,
    down_second,
):
    micro, _, rows, width = frames.shape
    parts = lax.axis_size("tensor")
    groups = lax.axis_size("dp")
    me = lax.axis_index("tensor")
    inner = input_weight.shape[2]
    heads = inner // HEAD_DIM
    highest = lax.Precision.HIGHEST
    order_p, order_q, order_r = orders()
    core = ("tensor", bits_of("tensor")[-1])
    across = ("tensor", bits_of("tensor")[0])
    dims = [across] + [("dp", mask) for mask in bits_of("dp")]
    all_dims = dims[1:] + [across, core]
    core_bit = bit_array(*core)
    bits = jnp.concatenate([bit_of(order_p[-1], (across,)), bit_of(order_q[-1], (across,))])
    line = Line()

    skip_one, skip_two, qk_shard, vo_shard = pack_attention(
        line, skip_weight, input_weight.transpose(1, 0, 2), output_weight
    )
    skip_walks = (
        Gather(line, skip_one, order_p + [core], all_dims, ()),
        Gather(line, skip_two, order_r + [core], all_dims, ()),
    )
    blocks = to_owner(
        lambda index: jnp.concatenate(
            [pick(value, index, 0)[0] for value in (frames, skip_frames, out_grad)], axis=1
        )
    )
    attention_walks = (
        Gather(line, qk_shard, order_p, dims, (across,)),
        Gather(line, vo_shard, order_q, dims, (across,)),
    )
    adapt_low = adapt_weight.astype(low)
    time_values = time_embed[:, 0, :].astype(f32)
    time_low = jax.nn.silu(time_values).astype(low)
    time_all = line.tie(unflip(time_low, 0, "tensor"))[None]
    for mask in reversed(bits_of("dp")):
        time_all = jnp.concatenate([time_all, swap(time_all, "dp", mask)], axis=0)
    time_rows = time_all.reshape(groups * micro, width)
    adapt_mine = jnp.dot(time_rows, adapt_low, preferred_element_type=f32).reshape(groups, micro, -1)
    adapt_vector = unflip(unflip(exchange_all(adapt_mine), 0, "dp"), 1, "tensor").reshape(1, -1)
    shift_one, scale_one, shift_two, scale_two = jnp.split(adapt_vector, 4, axis=1)

    row_index = jnp.concatenate(
        [(me ^ step) * rows + jnp.arange(rows, dtype=jnp.int32) for step in range(parts)]
    )
    length = pick(lengths, me, 0)[0]
    keep = (row_index < length).astype(f32)[:, None]
    half = HEAD_DIM // 2
    frequency = 10000.0 ** (-jnp.arange(half).astype(f32) / half)
    angles = row_index.astype(f32)[:, None] * frequency[None, :]
    cosine = jnp.tile(jnp.cos(angles), (1, 2 * heads))
    sine = jnp.tile(jnp.concatenate([-jnp.sin(angles), jnp.sin(angles)], axis=1), (1, heads))

    more = range(len(bits_of("dp")) - 3)
    for _ in more:
        go(line, *skip_walks)
        go(line, *attention_walks)
    go(line, *skip_walks)
    go(line, *attention_walks)
    go(line, *skip_walks)
    go(line, *attention_walks)
    go(line, *skip_walks)
    feed_walks = [
        Gather(line, shard, order, dims, (across,))
        for shard, order in zip(pack_feed(line, up_weight, down_weight), (order_p, order_q))
    ]
    go(line, *skip_walks)
    go(line, *attention_walks)
    for _ in more:
        go(line, *feed_walks)
    go(line, *feed_walks)
    skip_pairs = [walk.pair() for walk in skip_walks]
    hidden, outer = enter(line, blocks, skip_pairs, core_bit, keep)
    go(line, *feed_walks)
    qk_own, vo_own = (Weights(walk.pair(), walk.step, across) for walk in attention_walks)
    qk_other, vo_other = qk_own.flip(core), vo_own.flip(core)
    held_own, mixed_own, attended, normed_one = attend(
        line, qk_own, vo_own, bits, cosine, sine, keep, hidden, shift_one, scale_one
    )
    go(line, *feed_walks)
    held_other, mixed_other, middle, normed_two = attend(
        line,
        qk_other,
        vo_other,
        bits,
        cosine,
        sine,
        keep,
        hidden,
        shift_two,
        scale_two,
        normed=normed_one,
        before=attended,
    )
    feed_own = [Weights(walk.pair(), walk.step, across) for walk in feed_walks]
    feed_other = [weights.flip(core) for weights in feed_own]
    fed, back, feed_arrived, feed_scatters = [], [], [], []
    for place, weights in enumerate(feed_other):
        grad, *ends = feed(line, normed_two, outer, weights, bits, place, Halves(weights))
        feed_arrived.append(swap(grad, *core))
        fed.append(ends[0])
        back.append(ends[1])
    for place, weights in enumerate(feed_own):
        kept, sent, *ends = feed(
            line, normed_two, outer, weights, bits, place, Halves(weights, feed_arrived[place])
        )
        feed_scatters.append(
            Scatter(line, kept, sent, (order_p, order_q)[place][::-1], dims, (across,))
        )
        fed.append(ends[0])
        back.append(ends[1])
    feed_one, feed_two = feed_scatters
    result, middle_grad, sums_two, middle_low = bend(line, middle, outer, keep, scale_two, fed, back)
    results = from_owner([result[step * rows : (step + 1) * rows] for step in range(parts)])
    results = unflip(jnp.stack(results), 0, "tensor")
    qk_grad, vo_grad, ahead = attend_back(
        line,
        normed_one,
        middle_low,
        qk_other,
        vo_other,
        bits,
        held_other,
        mixed_other,
        cosine,
        sine,
        keep,
        Halves(qk_other),
        Halves(vo_other),
    )
    qk_arrived, vo_arrived = swap(qk_grad, *core), swap(vo_grad, *core)
    go(line, feed_one)
    qk_kept, qk_sent, vo_kept, vo_sent, sums_one, hidden_low = attend_back(
        line,
        normed_one,
        middle_low,
        qk_own,
        vo_own,
        bits,
        held_own,
        mixed_own,
        cosine,
        sine,
        keep,
        Halves(qk_own, qk_arrived),
        Halves(vo_own, vo_arrived),
        last=(ahead, hidden, middle_grad, scale_one),
    )
    attention_scatters = [
        Scatter(line, qk_kept, qk_sent, order_p[::-1], dims, (across,)),
        Scatter(line, vo_kept, vo_sent, order_q[::-1], dims, (across,)),
    ]
    go(line, feed_one, feed_two)
    leaving = leave(line, blocks, hidden_low, core_bit, groups * parts)
    skip_scatters = [
        Scatter(line, kept, sent, [core] + order[::-1], all_dims, ())
        for sent, kept, order in zip(leaving[::2], leaving[1::2], (order_p, order_q))
    ]
    hidden_back = from_owner([hidden_low[step * rows : (step + 1) * rows] for step in range(parts)])
    go(line, *skip_scatters)
    go(line, *attention_scatters)
    frame_grads, skip_grads = inputs_back(
        line, hidden_back, skip_pairs, jnp.concatenate([core_bit, me.astype(jnp.int32)[None]])
    )
    frame_grads, skip_grads = frame_grads.reshape(frames.shape), skip_grads.reshape(frames.shape)
    go(line, feed_one, feed_two)
    go(line, *skip_scatters)
    go(line, *attention_scatters)
    go(line, feed_two)
    adapt_back = jnp.concatenate([sums_one.reshape(-1), sums_two.reshape(-1)]).reshape(
        groups, parts, -1
    )
    adapt_rows = exchange_all(unflip(unflip(adapt_back, 0, "dp"), 1, "tensor"))
    adapt_rows = adapt_rows.reshape(groups * micro, -1)
    adapt_sum = lax.dot_general(
        time_rows.astype(f32), adapt_rows, (((0,), (0,)), ((), ())), precision=highest
    )
    time_part = lax.dot_general(
        adapt_rows, adapt_low.astype(f32), (((1,), (1,)), ((), ())), precision=highest
    ).reshape(groups, micro, width)
    for mask in bits_of("dp"):
        time_part = time_part[:mask] + swap(time_part[mask:], "dp", mask)
    time_part = unflip(time_part[0], 0, "tensor")
    for mask in bits_of("tensor"):
        time_part = time_part + swap(time_part, "tensor", mask)
    sigmoid = jax.nn.sigmoid(time_values)
    time_grad = time_part * (sigmoid * (1.0 + time_values * (1.0 - sigmoid)))

    go(line, *skip_scatters)
    go(line, *attention_scatters)
    go(line, *skip_scatters)
    for _ in more:
        go(line, feed_one, feed_two)
        go(line, *attention_scatters)
        go(line, *skip_scatters)
    feed_new = update_feed(
        line,
        feed_one.terms,
        feed_two.terms,
        (up_weight, up_first, up_second),
        (down_weight, down_first, down_second),
    )
    attention_new = update_attention(
        line,
        attention_scatters[0].terms,
        attention_scatters[1].terms,
        [state.transpose(1, 0, 2) for state in (input_weight, input_first, input_second)],
        (output_weight, output_first, output_second),
    )
    skip_new = update_skip(
        line,
        skip_scatters[0].terms,
        skip_scatters[1].terms,
        (skip_weight, skip_first, skip_second),
    )
    adapt_new = adam_update(adapt_weight, adapt_first, adapt_second, adapt_sum, rates[1])
    return (
        results[:, None],
        frame_grads,
        skip_grads,
        time_grad[:, None, :],
        *skip_new,
        *adapt_new,
        *(value.transpose(1, 0, 2) for value in attention_new[:4]),
        *attention_new[4:],
        *feed_new,
    )


def solution(mesh):
    return jax.shard_map(
        body,
        mesh=mesh,
        in_specs=(
            P(None, "dp", "tensor", None),
            P(None, "dp", "tensor", None),
            P(None, "dp", None),
            P(None, "dp"),
            P(None, "dp", "tensor", None),
            P(("dp", "tensor"), None),
            P(None, ("dp", "tensor")),
            P("dp", None, "tensor"),
            P("tensor", "dp"),
            P("dp", "tensor"),
            P("tensor", "dp"),
            P(("dp", "tensor"), None),
            P(None, ("dp", "tensor")),
            P("dp", None, "tensor"),
            P("tensor", "dp"),
            P("dp", "tensor"),
            P("tensor", "dp"),
            P(("dp", "tensor"), None),
            P(None, ("dp", "tensor")),
            P("dp", None, "tensor"),
            P("tensor", "dp"),
            P("dp", "tensor"),
            P("tensor", "dp"),
        ),
        out_specs=(
            P(None, "dp", "tensor", None),
            P(None, "dp", "tensor", None),
            P(None, "dp", "tensor", None),
            P(None, "dp", None),
            P(("dp", "tensor"), None),
            P(("dp", "tensor"), None),
            P(("dp", "tensor"), None),
            P(("dp", "tensor"), None),
            P(None, ("dp", "tensor")),
            P(None, ("dp", "tensor")),
            P(None, ("dp", "tensor")),
            P(None, ("dp", "tensor")),
            P("dp", None, "tensor"),
            P("dp", None, "tensor"),
            P("dp", None, "tensor"),
            P("dp", None, "tensor"),
            P("tensor", "dp"),
            P("tensor", "dp"),
            P("tensor", "dp"),
            P("tensor", "dp"),
            P("dp", "tensor"),
            P("dp", "tensor"),
            P("dp", "tensor"),
            P("dp", "tensor"),
            P("tensor", "dp"),
            P("tensor", "dp"),
            P("tensor", "dp"),
            P("tensor", "dp"),
        ),
        check_vma=False,
    )
```

time: 833 us -> 580 us (0.70)
  Pallas kernels: 0 us -> 249 us
  waiting for transfers between devices: 374 us -> 195 us
  matrix products: 149 us -> 2.53 us
  local copies, waits for them, and re-layouts: 145 us -> 24.7 us
  other arithmetic: 78.4 us -> 15.6 us
  starting transfers between devices: 73.2 us -> 84.1 us
    pallas_call x0 -> x38, Pallas kernels: none -> 249 us  [run(): pl.pallas_call(inner, grid_spec=pltpu.PrefetchScalarGridSpec(num_scalar_p...]
    ppermute x85 -> x91, waiting for transfers between devices: 374 us -> 195 us  [swap(): return lax.ppermute(values, axis, [(i, i ^ mask) for i in range(count)])]
    dot_general x76 -> x1, matrix products: 145 us -> 0.16 us  [body(): jnp.dot(time_rows, adapt_low, preferred_element_type=f32)]
    convert_element_type x35 -> x1, other arithmetic: 43.2 us -> 1.56 us  [body(): keep = (row_index < length).astype(f32)[:, None]]
    ppermute x8 -> x0, local copies, waits for them, and re-layouts: 32.1 us -> none  [swap(): return lax.ppermute(values, axis, [(i, i ^ mask) for i in range(count)])]
    slice x22 -> x1, local copies, waits for them, and re-layouts: 26.3 us -> 0.89 us  [body(): hidden_low[step * rows:(step + 1) * rows]]
    concatenate x8 -> x3, local copies, waits for them, and re-layouts: 23.2 us -> 0.83 us  [body(): jnp.concatenate([sums_one.reshape(-1), sums_two.reshape(-1)])]
    ppermute x85 -> x91, starting transfers between devices: 73.2 us -> 84.1 us  [swap(): return lax.ppermute(values, axis, [(i, i ^ mask) for i in range(count)])]
  transfers between devices with their start and end apart: 85 -> 91, of which waited for: 35 -> 36; matrix products, arithmetic and copies ran while one was open for 35% -> 5% of each run, Pallas kernels for 0% -> 42%
where the time goes in v2:
time: 580 us; the launch traced here: 573 us
  Pallas kernels  249 us (43%)
  waiting for transfers between devices  195 us (34%)
  starting transfers between devices  84.1 us (14%)
  local copies, waits for them, and re-layouts  24.7 us (4%)
  other arithmetic  15.6 us (3%)
    pallas_call x38, Pallas kernels, run(): pl.pallas_call(inner, grid_spec=pltpu.PrefetchScalarGridSpec(num_scalar_p...  249 us
    ppermute x91, waiting for transfers between devices, swap(): return lax.ppermute(values, axis, [(i, i ^ mask) for i in range(count)])  195 us
    ppermute x91, starting transfers between devices, swap(): return lax.ppermute(values, axis, [(i, i ^ mask) for i in range(count)])  84.1 us
    unnamed x129, local copies, waits for them, and re-layouts  14.1 us
  transfers between devices with their start and end apart: 91, of which 36 were waited for; matrix products, arithmetic and copies ran while one was open for 5% of the time, Pallas kernels for 42%

profile of v2, /device:TPU:0, one launch (start us, length us, event | category | flops | bytes accessed | tf_op | source)
XLA Modules:
  0.0 573.0 jit_solution(4038832182393771159)
XLA Ops:
  84.0 5.9 %collective-permute-done.25 = bf16[128,1024]{1,0:T(8,128)(2,1)} collective-permute-done((bf16[128,1024]{1,0:T(8,128)(2,1)}, bf16[128,1024]{1,0:T(8,128)(2,1)}, u32[]{:S(2)}, u32[]{:S(2)}) %collective-permute-start.25) | collective-permute-done | bytes 262176 | tf_op jit(solution)/shard_map/ppermute | solution.py:37
  110.7 9.1 %collective-permute-done.22.refs_4_ = bf16[128,3072]{1,0:T(8,128)(2,1)S(1)} collective-permute-done((bf16[128,3072]{1,0:T(8,128)(2,1)}, bf16[128,3072]{1,0:T(8,128)(2,1)S(1)}, u32[]{:S(2)}, u32[]{:S(2)}) %collective-permute-start.22) | collective-permute-done | bytes 786464 | tf_op jit(solution)/shard_map/ppermute | solution.py:37
  122.5 7.3 %shard_map.448 = (f32[512,1024]{1,0:T(8,128)}, bf16[512,1024]{1,0:T(8,128)(2,1)}) custom-call(s32[1]{0:T(128)} %bitcast.56.refs_0_, bf16[128,3072]{1,0:T(8,128)(2,1)} %pad_maximum_fusion.1.refs_1_, bf16[128,3072]{1,0:T(8,128)(2,1)} %collective-permute-done.20.refs_2_, bf16[128,3072]{1,0:T(8,128)(2,1)} %copy-done.13, bf16[128,3072]{1,0:T(8,128)(2,1)} %copy-done.14, ...), custom_call_target="tpu_custom_call" | custom-call | flops 2147483648 | bytes 10487808 | tf_op jit(solution)/shard_map/pallas_call | solution.py:72
  147.0 14.7 %shard_map.450 = (bf16[2,512,768]{2,1,0:T(8,128)(2,1)}, bf16[2,512,256]{2,1,0:T(8,128)(2,1)}, f32[512,1024]{1,0:T(8,128)}, bf16[512,1024]{1,0:T(8,128)(2,1)}) custom-call(s32[2]{0:T(128)} %pad_add_fusion.refs_0_, bf16[2,4,128,512]{3,2,1,0:T(8,128)(2,1)} %bitcast.43.refs_1_, bf16[2,4,128,512]{3,2,1,0:T(8,128)(2,1)} %bitcast.45.refs_2_, ...), custom_call_target="tpu_custom_call" | custom-call | flops 4294967296 | bytes 12593152 | tf_op jit(solution)/shard_map/pallas_call | solution.py:72
  161.7 7.6 %collective-permute-done.38 = bf16[512,1024]{1,0:T(8,128)(2,1)S(1)} collective-permute-done((bf16[512,1024]{1,0:T(8,128)(2,1)}, bf16[512,1024]{1,0:T(8,128)(2,1)S(1)}, u32[]{:S(2)}, u32[]{:S(2)}) %collective-permute-start.38) | collective-permute-done | bytes 1048608 | tf_op jit(solution)/shard_map/ppermute | solution.py:37
  170.3 5.1 shard_map.451
  182.6 40.7 %collective-permute-done.40 = bf16[1024,1024]{1,0:T(8,128)(2,1)S(1)} collective-permute-done((bf16[1024,1024]{1,0:T(8,128)(2,1)}, bf16[1024,1024]{1,0:T(8,128)(2,1)S(1)}, u32[]{:S(2)}, u32[]{:S(2)}) %collective-permute-start.40) | collective-permute-done | bytes 2097184 | tf_op jit(solution)/shard_map/ppermute | solution.py:37
  225.0 8.6 %collective-permute-done.16.refs_2_ = bf16[2,4,128,512]{3,2,1,0:T(8,128)(2,1)S(1)} collective-permute-done((bf16[2,4,128,512]{3,2,1,0:T(8,128)(2,1)}, bf16[2,4,128,512]{3,2,1,0:T(8,128)(2,1)S(1)}, u32[]{:S(2)}, u32[]{:S(2)}) %collective-permute-start.16) | collective-permute-done | bytes 1048608 | tf_op jit(solution)/shard_map/ppermute | solution.py:37
  234.7 15.8 %shard_map.452 = (bf16[2,512,768]{2,1,0:T(8,128)(2,1)}, bf16[2,512,256]{2,1,0:T(8,128)(2,1)}, f32[512,1024]{1,0:T(8,128)}, bf16[512,1024]{1,0:T(8,128)(2,1)}) custom-call(s32[2]{0:T(128)} %pad_add_fusion.refs_0_, bf16[2,4,128,512]{3,2,1,0:T(8,128)(2,1)} %copy-done.58, bf16[2,4,128,512]{3,2,1,0:T(8,128)(2,1)} %copy-done.59, bf16[1,1024,512]{2,1,0:T(8,128)(2,1)} %copy-done.57, ...), custom_call_target="tpu_custom_call" | custom-call | flops 4294967296 | bytes 15738880 | tf_op jit(solution)/shard_map/pallas_call | solution.py:72
  250.5 13.7 %shard_map.453 = (bf16[2,1024,1024]{2,1,0:T(8,128)(2,1)}, bf16[512,1024]{1,0:T(8,128)(2,1)}, bf16[512,1024]{1,0:T(8,128)(2,1)}) custom-call(s32[2]{0:T(128)} %pad_add_fusion.refs_0_, bf16[2,4,128,1024]{3,2,1,0:T(8,128)(2,1)} %collective-permute-done.39.refs_1_, bf16[2,4,128,1024]{3,2,1,0:T(8,128)(2,1)} %collective-permute-done.41.refs_2_, ...), custom_call_target="tpu_custom_call" | custom-call | flops 6442450944 | bytes 12582912 | tf_op jit(solution)/shard_map/pallas_call | solution.py:72
  264.3 14.1 %shard_map.454 = (bf16[2,1024,1024]{2,1,0:T(8,128)(2,1)}, bf16[512,1024]{1,0:T(8,128)(2,1)}, bf16[512,1024]{1,0:T(8,128)(2,1)}) custom-call(s32[2]{0:T(128)} %pad_add_fusion.refs_0_, bf16[1,1024,1024]{2,1,0:T(8,128)(2,1)} %collective-permute-done.42.refs_1_, bf16[1,1024,1024]{2,1,0:T(8,128)(2,1)} %collective-permute-done.44.refs_2_, ...), custom_call_target="tpu_custom_call" | custom-call | flops 6442450944 | bytes 12582912 | tf_op jit(solution)/shard_map/pallas_call | solution.py:72
  278.8 15.1 %shard_map.455 = (bf16[2,4,128,1024]{3,2,1,0:T(8,128)(2,1)}, bf16[2,4,128,1024]{3,2,1,0:T(8,128)(2,1)}, bf16[512,1024]{1,0:T(8,128)(2,1)}, bf16[512,1024]{1,0:T(8,128)(2,1)}) custom-call(s32[2]{0:T(128)} %pad_add_fusion.refs_0_, bf16[2,4,128,1024]{3,2,1,0:T(8,128)(2,1)} %bitcast.372, bf16[2,4,128,1024]{3,2,1,0:T(8,128)(2,1)} %bitcast.374, ...), custom_call_target="tpu_custom_call" | custom-call | flops 6442450944 | bytes 16777216 | tf_op jit(solution)/shard_map/pallas_call | solution.py:72
  297.4 16.3 %shard_map.456 = (bf16[1024,1024]{1,0:T(8,128)(2,1)}, bf16[1024,1024]{1,0:T(8,128)(2,1)}, bf16[512,1024]{1,0:T(8,128)(2,1)}, bf16[512,1024]{1,0:T(8,128)(2,1)}) custom-call(s32[2]{0:T(128)} %pad_add_fusion.refs_0_, bf16[1,1024,1024]{2,1,0:T(8,128)(2,1)} %bitcast.367, bf16[1,1024,1024]{2,1,0:T(8,128)(2,1)} %bitcast.369, ...), custom_call_target="tpu_custom_call" | custom-call | flops 6442450944 | bytes 16777216 | tf_op jit(solution)/shard_map/pallas_call | solution.py:72
  313.7 8.8 %shard_map.457 = (bf16[512,1024]{1,0:T(8,128)(2,1)}, f32[512,1024]{1,0:T(8,128)}, f32[2,1024]{1,0:T(2,128)}, bf16[512,1024]{1,0:T(8,128)(2,1)}) custom-call(f32[512,1024]{1,0:T(8,128)} %get-tuple-element.188.refs_0_, bf16[512,1024]{1,0:T(8,128)(2,1)} %get-tuple-element.182.refs_5_.refs_4_.refs_1_, ...), custom_call_target="tpu_custom_call" | custom-call | bytes 15742976 | tf_op jit(solution)/shard_map/pallas_call | solution.py:72
  322.5 20.3 %shard_map.458 = (bf16[2,1024,512]{2,1,0:T(8,128)(2,1)}, bf16[2,1024,512]{2,1,0:T(8,128)(2,1)}, f32[512,1024]{1,0:T(8,128)}) custom-call(s32[2]{0:T(128)} %pad_add_fusion.refs_0_, bf16[2,4,128,512]{3,2,1,0:T(8,128)(2,1)} %copy-done.58, bf16[2,4,128,512]{3,2,1,0:T(8,128)(2,1)} %copy-done.59, bf16[1,1024,512]{2,1,0:T(8,128)(2,1)} %copy-done.57, ...), custom_call_target="tpu_custom_call" | custom-call | flops 9663676416 | bytes 15730688 | tf_op jit(solution)/shard_map/pallas_call | solution.py:72
  350.3 24.2 %shard_map.460 = (bf16[2,4,128,512]{3,2,1,0:T(8,128)(2,1)}, bf16[2,4,128,512]{3,2,1,0:T(8,128)(2,1)}, bf16[1024,512]{1,0:T(8,128)(2,1)}, bf16[1024,512]{1,0:T(8,...) custom-call(s32[2]{0:T(128)} %pad_add_fusion.refs_0_, bf16[2,4,128,512]{3,2,1,0:T(8,128)(2,1)} %bitcast.43.refs_1_, ...), custom_call_target="tpu_custom_call" | custom-call | flops 9663676416 | bytes 25180160 | tf_op jit(solution)/shard_map/pallas_call | solution.py:72
  388.8 25.1 %collective-permute-done.65 = f32[2,2,2,1,2,128]{5,4,3,2,1,0:T(2,128)S(1)} collective-permute-done((f32[2,2,2,1,2,128]{5,4,3,2,1,0:T(2,128)S(1)}, f32[2,2,2,1,2,128]{5,4,3,2,1,0:T(2,128)S(1)}, u32[]{:S(2)}, u32[]{:S(2)}) %collective-permute-start.65) | collective-permute-done | bytes 8224 | tf_op jit(solution)/shard_map/ppermute | solution.py:37
  422.8 5.8 %shard_map.461 = (bf16[2,128,1024]{2,1,0:T(8,128)(2,1)}, bf16[2,128,1024]{2,1,0:T(8,128)(2,1)}, bf16[4,128,1024]{2,1,0:T(8,128)(2,1)}, bf16[4,128,1024]{2,1,0:T(8,128)(2,1)}) custom-call(s32[2]{0:T(128)} %pad_add_fusion.4.refs_0_, bf16[2,2,128,1024]{3,2,1,0:T(8,128)(2,1)} %bitcast.285, bf16[2,2,128,1024]{3,2,1,0:T(8,128)(2,1)} %bitcast.120.refs_2_, ...), custom_call_target="tpu_custom_call" | custom-call | bytes 9437184 | tf_op jit(solution)/shard_map/pallas_call | solution.py:72
  428.6 6.0 %shard_map.462 = (bf16[16,64,512]{2,1,0:T(8,128)(2,1)}, bf16[16,64,512]{2,1,0:T(8,128)(2,1)}, bf16[16,64,512]{2,1,0:T(8,128)(2,1)}, bf16[16,64,512]{2,1,0:T(8,128)(2,1)}) custom-call(s32[1]{0:T(128)} %bitcast.56.refs_0_, bf16[128,3072]{1,0:T(8,128)(2,1)} %pad_maximum_fusion.1.refs_1_, bf16[128,3072]{1,0:T(8,128)(2,1)} %collective-permute-done.20.refs_2_, ...), custom_call_target="tpu_custom_call" | custom-call | flops 2147483648 | bytes 8388608 | tf_op jit(solution)/shard_map/pallas_call | solution.py:72
  438.9 9.5 %collective-permute-done.69 = f32[1,4,1024]{2,1,0:T(4,128)S(1)} collective-permute-done((f32[1,4,1024]{2,1,0:T(4,128)S(1)}, f32[1,4,1024]{2,1,0:T(4,128)S(1)}, u32[]{:S(2)}, u32[]{:S(2)}) %collective-permute-start.69) | collective-permute-done | bytes 16416 | tf_op jit(solution)/shard_map/ppermute | solution.py:37
  450.8 14.9 %collective-permute-done.55.refs_4_ = bf16[128,1024]{1,0:T(8,128)(2,1)S(1)} collective-permute-done((bf16[128,1024]{1,0:T(8,128)(2,1)S(1)}, bf16[128,1024]{1,0:T(8,128)(2,1)S(1)}, u32[]{:S(2)}, u32[]{:S(2)}) %collective-permute-start.55) | collective-permute-done | bytes 262176 | tf_op jit(solution)/shard_map/ppermute | solution.py:37
  484.8 7.0 %shard_map.465 = (f32[512,1024]{1,0:T(8,128)}, f32[512,1024]{1,0:T(8,128)}) custom-call(s32[2]{0:T(128)} %pad_add_fusion.3.refs_0_, bf16[128,1024]{1,0:T(8,128)(2,1)} %get-tuple-element.407.refs_1_, bf16[128,1024]{1,0:T(8,128)(2,1)} %collective-permute-done.53.refs_2_, bf16[128,1024]{1,0:T(8,128)(2,1)} %collective-permute-done.54.refs_3_, ...), custom_call_target="tpu_custom_call" | custom-call | flops 2147483648 | bytes 9437184 | tf_op jit(solution)/shard_map/pallas_call | solution.py:72
  497.1 6.0 %collective-permute-done.72 = bf16[512,512]{1,0:T(8,128)(2,1)S(1)} collective-permute-done((bf16[512,512]{1,0:T(8,128)(2,1)}, bf16[512,512]{1,0:T(8,128)(2,1)S(1)}, u32[]{:S(2)}, u32[]{:S(2)}) %collective-permute-start.72) | collective-permute-done | bytes 524320 | tf_op jit(solution)/shard_map/ppermute | solution.py:37
  532.2 6.6 %collective-permute-done.84 = bf16[256,512]{1,0:T(8,128)(2,1)S(1)} collective-permute-done((bf16[256,512]{1,0:T(8,128)(2,1)}, bf16[256,512]{1,0:T(8,128)(2,1)S(1)}, u32[]{:S(2)}, u32[]{:S(2)}) %collective-permute-start.84) | collective-permute-done | bytes 262176 | tf_op jit(solution)/shard_map/ppermute | solution.py:37
  (420 shorter events, 262.9 us)
Async XLA Ops:
  2.7 35.9 %collective-permute-start.1 = (bf16[128,512]{1,0:T(8,128)(2,1)}, bf16[128,512]{1,0:T(8,128)(2,1)S(1)}, u32[]{:S(2)}, u32[]{:S(2)}) collective-permute-start(bf16[128,512]{1,0:T(8,128)(2,1)} %get-tuple-element.159.refs_5_), channel_id=1, source_target_pairs={{0,16},{4,20},{8,24},{12,28},{16,0},{20,4},{24,8},{28,12},{1,17},{... | collective-permute-start | bytes 393224 | tf_op jit(solution)/shard_map/ppermute | solution.py:37
  68.9 30.3 %collective-permute-start.8 = (bf16[512,512]{1,0:T(8,128)(2,1)S(1)}, bf16[512,512]{1,0:T(8,128)(2,1)}, u32[]{:S(2)}, u32[]{:S(2)}) collective-permute-start(bf16[512,512]{1,0:T(8,128)(2,1)S(1)} %bitcast.299), channel_id=1, source_target_pairs={{0,2},{1,3},{2,0},{3,1},{4,6},{5,7},{6,4},{7,5},{8,10},{9,11},{10,... | collective-permute-start | bytes 1572872 | tf_op jit(solution)/shard_map/ppermute | solution.py:37
  83.1 37.8 %collective-permute-start.24 = (bf16[1024,512]{1,0:T(8,128)(2,1)}, bf16[1024,512]{1,0:T(8,128)(2,1)S(1)}, u32[]{:S(2)}, u32[]{:S(2)}) collective-permute-start(bf16[1024,512]{1,0:T(8,128)(2,1)} %bitcast.238), channel_id=1, source_target_pairs={{0,1},{1,0},{2,3},{3,2},{4,5},{5,4},{6,7},{7,6},{8,9},{9,8},{10,11... | collective-permute-start | bytes 3145736 | tf_op jit(solution)/shard_map/ppermute | solution.py:37
  93.2 29.2 %collective-permute-start.23 = (bf16[1024,512]{1,0:T(8,128)(2,1)}, bf16[1024,512]{1,0:T(8,128)(2,1)}, u32[]{:S(2)}, u32[]{:S(2)}) collective-permute-start(bf16[1024,512]{1,0:T(8,128)(2,1)} %bitcast.280), channel_id=1, source_target_pairs={{0,1},{1,0},{2,3},{3,2},{4,5},{5,4},{6,7},{7,6},{8,9},{9,8},{10,11... | collective-permute-start | bytes 3145736 | tf_op jit(solution)/shard_map/ppermute | solution.py:37
  138.4 30.9 %collective-permute-start.38 = (bf16[512,1024]{1,0:T(8,128)(2,1)}, bf16[512,1024]{1,0:T(8,128)(2,1)S(1)}, u32[]{:S(2)}, u32[]{:S(2)}) collective-permute-start(bf16[512,1024]{1,0:T(8,128)(2,1)} %bitcast.277), channel_id=1, source_target_pairs={{0,4},{4,0},{8,12},{12,8},{16,20},{20,16},{24,28},{28,24},{1,5},{5... | collective-permute-start | bytes 3145736 | tf_op jit(solution)/shard_map/ppermute | solution.py:37
  140.0 29.4 %collective-permute-start.37 = (bf16[512,1024]{1,0:T(8,128)(2,1)}, bf16[512,1024]{1,0:T(8,128)(2,1)}, u32[]{:S(2)}, u32[]{:S(2)}) collective-permute-start(bf16[512,1024]{1,0:T(8,128)(2,1)} %bitcast.275), channel_id=1, source_target_pairs={{0,2},{1,3},{2,0},{3,1},{4,6},{5,7},{6,4},{7,5},{8,10},{9,11},{10,... | collective-permute-start | bytes 3145736 | tf_op jit(solution)/shard_map/ppermute | solution.py:37
  175.4 47.9 %collective-permute-start.40 = (bf16[1024,1024]{1,0:T(8,128)(2,1)}, bf16[1024,1024]{1,0:T(8,128)(2,1)S(1)}, u32[]{:S(2)}, u32[]{:S(2)}) collective-permute-start(bf16[1024,1024]{1,0:T(8,128)(2,1)} %bitcast.370), channel_id=1, source_target_pairs={{0,4},{4,0},{8,12},{12,8},{16,20},{20,16},{24,28},{28,24},{1,5},{5... | collective-permute-start | bytes 6291464 | tf_op jit(solution)/shard_map/ppermute | solution.py:37
  176.7 47.8 %collective-permute-start.43 = (bf16[1024,1024]{1,0:T(8,128)(2,1)}, bf16[1024,1024]{1,0:T(8,128)(2,1)S(1)}, u32[]{:S(2)}, u32[]{:S(2)}) collective-permute-start(bf16[1024,1024]{1,0:T(8,128)(2,1)} %bitcast.365), channel_id=1, source_target_pairs={{0,2},{1,3},{2,0},{3,1},{4,6},{5,7},{6,4},{7,5},{8,10},{9,11},{10,... | collective-permute-start | bytes 6291464 | tf_op jit(solution)/shard_map/ppermute | solution.py:37
  178.4 44.9 %collective-permute-start.14 = (bf16[2,4,128,512]{3,2,1,0:T(8,128)(2,1)}, bf16[2,4,128,512]{3,2,1,0:T(8,128)(2,1)S(1)}, u32[]{:S(2)}, u32[]{:S(2)}) collective-permute-start(bf16[2,4,128,512]{3,2,1,0:T(8,128)(2,1)} %bitcast.43.refs_1_), channel_id=1, source_target_pairs={{0,1},{1,0},{2,3},{3,2},{4,5},{5,4},{6,7},{7,6},{8,9},{9,8},{10,11... | collective-permute-start | bytes 3145736 | tf_op jit(solution)/shard_map/ppermute | solution.py:37
  178.9 45.7 %collective-permute-start.19 = (bf16[1,1024,512]{2,1,0:T(8,128)(2,1)}, bf16[1,1024,512]{2,1,0:T(8,128)(2,1)}, u32[]{:S(2)}, u32[]{:S(2)}) collective-permute-start(bf16[1,1024,512]{2,1,0:T(8,128)(2,1)} %bitcast.48.refs_4_), channel_id=1, source_target_pairs={{0,1},{1,0},{2,3},{3,2},{4,5},{5,4},{6,7},{7,6},{8,9},{9,8},{10,11... | collective-permute-start | bytes 3145736 | tf_op jit(solution)/shard_map/ppermute | solution.py:37
  182.5 68.0 %collective-permute-start.39 = (bf16[2,4,128,1024]{3,2,1,0:T(8,128)(2,1)}, bf16[2,4,128,1024]{3,2,1,0:T(8,128)(2,1)}, u32[]{:S(2)}, u32[]{:S(2)}) collective-permute-start(bf16[2,4,128,1024]{3,2,1,0:T(8,128)(2,1)} %bitcast.371), channel_id=1, source_target_pairs={{0,1},{1,0},{2,3},{3,2},{4,5},{5,4},{6,7},{7,6},{8,9},{9,8},{10,11... | collective-permute-start | bytes 6291464 | tf_op jit(solution)/shard_map/ppermute | solution.py:37
  223.3 41.0 %collective-permute-start.42 = (bf16[1,1024,1024]{2,1,0:T(8,128)(2,1)}, bf16[1,1024,1024]{2,1,0:T(8,128)(2,1)}, u32[]{:S(2)}, u32[]{:S(2)}) collective-permute-start(bf16[1,1024,1024]{2,1,0:T(8,128)(2,1)} %bitcast.366), channel_id=1, source_target_pairs={{0,1},{1,0},{2,3},{3,2},{4,5},{5,4},{6,7},{7,6},{8,9},{9,8},{10,11... | collective-permute-start | bytes 6291464 | tf_op jit(solution)/shard_map/ppermute | solution.py:37
  224.5 39.8 %collective-permute-start.44 = (bf16[1,1024,1024]{2,1,0:T(8,128)(2,1)S(1)}, bf16[1,1024,1024]{2,1,0:T(8,128)(2,1)}, u32[]{:S(2)}, u32[]{:S(2)}) collective-permute-start(bf16[1,1024,1024]{2,1,0:T(8,128)(2,1)S(1)} %bitcast.368), channel_id=1, source_target_pairs={{0,1},{1,0},{2,3},{3,2},{4,5},{5,4},{6,7},{7,6},{8,9},{9,8},{10,11... | collective-permute-start | bytes 6291464 | tf_op jit(solution)/shard_map/ppermute | solution.py:37
  293.8 50.8 %collective-permute-start.52 = (bf16[1024,1024]{1,0:T(8,128)(2,1)}, bf16[1024,1024]{1,0:T(8,128)(2,1)S(1)}, u32[]{:S(2)}, u32[]{:S(2)}) collective-permute-start(bf16[1024,1024]{1,0:T(8,128)(2,1)} %bitcast.375), channel_id=1, source_target_pairs={{0,4},{4,0},{8,12},{12,8},{16,20},{20,16},{24,28},{28,24},{1,5},{5... | collective-permute-start | bytes 6291464 | tf_op jit(solution)/shard_map/ppermute | solution.py:37
  343.4 78.8 %collective-permute-start.59 = (bf16[1024,1024]{1,0:T(8,128)(2,1)}, bf16[1024,1024]{1,0:T(8,128)(2,1)}, u32[]{:S(2)}, u32[]{:S(2)}) collective-permute-start(bf16[1024,1024]{1,0:T(8,128)(2,1)} %get-tuple-element.221), channel_id=1, source_target_pairs={{0,2},{1,3},{2,0},{3,1},{4,6},{5,7},{6,4},{7,5},{8,10},{9,11},{10,... | collective-permute-start | bytes 6291464 | tf_op jit(solution)/shard_map/ppermute | solution.py:37
  384.4 38.3 %collective-permute-start.58 = (bf16[512,1024]{1,0:T(8,128)(2,1)}, bf16[512,1024]{1,0:T(8,128)(2,1)}, u32[]{:S(2)}, u32[]{:S(2)}) collective-permute-start(bf16[512,1024]{1,0:T(8,128)(2,1)} %bitcast.377), channel_id=1, source_target_pairs={{0,2},{1,3},{2,0},{3,1},{4,6},{5,7},{6,4},{7,5},{8,10},{9,11},{10,... | collective-permute-start | bytes 3145736 | tf_op jit(solution)/shard_map/ppermute | solution.py:37
  422.2 45.6 %collective-permute-start.56 = (bf16[1024,512]{1,0:T(8,128)(2,1)}, bf16[1024,512]{1,0:T(8,128)(2,1)S(1)}, u32[]{:S(2)}, u32[]{:S(2)}) collective-permute-start(bf16[1024,512]{1,0:T(8,128)(2,1)} %bitcast.376), channel_id=1, source_target_pairs={{0,4},{4,0},{8,12},{12,8},{16,20},{20,16},{24,28},{28,24},{1,5},{5... | collective-permute-start | bytes 3145736 | tf_op jit(solution)/shard_map/ppermute | solution.py:37
  434.7 35.0 %collective-permute-start.60 = (bf16[1024,512]{1,0:T(8,128)(2,1)}, bf16[1024,512]{1,0:T(8,128)(2,1)}, u32[]{:S(2)}, u32[]{:S(2)}) collective-permute-start(bf16[1024,512]{1,0:T(8,128)(2,1)} %bitcast.379), channel_id=1, source_target_pairs={{0,1},{1,0},{2,3},{3,2},{4,5},{5,4},{6,7},{7,6},{8,9},{9,8},{10,11... | collective-permute-start | bytes 3145736 | tf_op jit(solution)/shard_map/ppermute | solution.py:37
  434.9 36.0 %collective-permute-start.61 = (bf16[1024,512]{1,0:T(8,128)(2,1)}, bf16[1024,512]{1,0:T(8,128)(2,1)}, u32[]{:S(2)}, u32[]{:S(2)}) collective-permute-start(bf16[1024,512]{1,0:T(8,128)(2,1)} %bitcast.378), channel_id=1, source_target_pairs={{0,1},{1,0},{2,3},{3,2},{4,5},{5,4},{6,7},{7,6},{8,9},{9,8},{10,11... | collective-permute-start | bytes 3145736 | tf_op jit(solution)/shard_map/ppermute | solution.py:37
  435.2 40.3 %collective-permute-start.57 = (bf16[1024,512]{1,0:T(8,128)(2,1)}, bf16[1024,512]{1,0:T(8,128)(2,1)}, u32[]{:S(2)}, u32[]{:S(2)}) collective-permute-start(bf16[1024,512]{1,0:T(8,128)(2,1)} %get-tuple-element.218), channel_id=1, source_target_pairs={{0,2},{1,3},{2,0},{3,1},{4,6},{5,7},{6,4},{7,5},{8,10},{9,11},{10,... | collective-permute-start | bytes 3145736 | tf_op jit(solution)/shard_map/ppermute | solution.py:37
  483.3 31.1 %collective-permute-start.80 = (bf16[512,512]{1,0:T(8,128)(2,1)}, bf16[512,512]{1,0:T(8,128)(2,1)S(1)}, u32[]{:S(2)}, u32[]{:S(2)}) collective-permute-start(bf16[512,512]{1,0:T(8,128)(2,1)} %bitcast.380), channel_id=1, source_target_pairs={{0,4},{4,0},{8,12},{12,8},{16,20},{20,16},{24,28},{28,24},{1,5},{5... | collective-permute-start | bytes 1572872 | tf_op jit(solution)/shard_map/ppermute | solution.py:37
  521.8 31.7 %collective-permute-start.71 = (f32[4,1024]{1,0:T(4,128)S(1)}, f32[4,1024]{1,0:T(4,128)S(1)}, u32[]{:S(2)}, u32[]{:S(2)}) collective-permute-start(f32[4,1024]{1,0:T(4,128)S(1)} %add.207), channel_id=1, source_target_pairs={{0,1},{1,0},{2,3},{3,2},{4,5},{5,4},{6,7},{7,6},{8,9},{9,8},{10,11... | collective-permute-start | bytes 49160 | tf_op jit(solution)/shard_map/ppermute | solution.py:37
  524.6 30.5 %collective-permute-start.89 = (bf16[128,1024]{1,0:T(8,128)(2,1)S(1)}, bf16[128,1024]{1,0:T(8,128)(2,1)S(1)}, u32[]{:S(2)}, u32[]{:S(2)}) collective-permute-start(bf16[128,1024]{1,0:T(8,128)(2,1)S(1)} %bitcast.387), channel_id=1, source_target_pairs={{0,16},{4,20},{8,24},{12,28},{16,0},{20,4},{24,8},{28,12},{1,17},{... | collective-permute-start | bytes 786440 | tf_op jit(solution)/shard_map/ppermute | solution.py:37
  526.4 32.2 %collective-permute-start.90 = (bf16[128,1024]{1,0:T(8,128)(2,1)}, bf16[128,1024]{1,0:T(8,128)(2,1)S(1)}, u32[]{:S(2)}, u32[]{:S(2)}) collective-permute-start(bf16[128,1024]{1,0:T(8,128)(2,1)} %bitcast.388), channel_id=1, source_target_pairs={{0,16},{4,20},{8,24},{12,28},{16,0},{20,4},{24,8},{28,12},{1,17},{... | collective-permute-start | bytes 786440 | tf_op jit(solution)/shard_map/ppermute | solution.py:37
  (131 other events, 1582.2 us)

commit v3 on v2

v3 whole, which is shorter than its diff:
```python
import functools
import math

import jax
import jax.numpy as jnp
from jax import lax
from jax.experimental import pallas as pl
from jax.experimental.pallas import tpu as pltpu
from jax.sharding import Mesh
from jax.sharding import PartitionSpec as P

HEAD_DIM = 64
TENSOR = ("high", "low")
STEP = 10
MEBI = 1 << 20

norm_eps = 1e-06
neg_large = -1e30
rates = (0.04, 0.06, 0.06, 0.6, 0.06, 0.03)
beta_first = 0.9
beta_second = 0.999
decay_rate = 0.01
adam_eps = 1e-08
low = jnp.bfloat16
f32 = jnp.float32


def bits_of(axis):
    count = lax.axis_size(axis).bit_length() - 1
    return [1 << place for place in reversed(range(count))]


def my_bit(axis, mask):
    return (lax.axis_index(axis) // mask) % 2


def swap(values, axis, mask):
    count = lax.axis_size(axis)
    return lax.ppermute(values, axis, [(i, i ^ mask) for i in range(count)])


def pick(values, index, dim):
    return lax.dynamic_index_in_dim(values, index, dim, keepdims=False)


def struct(shape, dtype):
    return jax.ShapeDtypeStruct(shape, dtype)


class Whole:
    def __init__(self, array, each=False):
        self.each = each


def whole(array):
    return Whole(array)


def each(array):
    return Whole(array, each=True)


class Line:
    def __init__(self):
        self.last = ()
        steps = [("dp", mask) for mask in bits_of("dp")] + [(TENSOR, mask) for mask in bits_of(TENSOR)]
        self.place = {step: 2 + place for place, step in enumerate(steps)}
        me = lax.axis_index(TENSOR)
        self.bits = jnp.stack([jnp.zeros((), me.dtype), me] + [my_bit(*step) for step in steps])

    def run(self, kernel, outs, ins, *, grid=(1,), in_specs=None, out_specs=None, scratch=(), flops=0, limit=14):
        in_specs = [Whole(value) for value in ins] if in_specs is None else in_specs
        out_specs = [Whole(value) for value in outs] if out_specs is None else out_specs
        marks = [isinstance(spec, Whole) and spec.each for spec in (*in_specs, *out_specs)]
        in_specs, out_specs = (
            [pl.BlockSpec(memory_space=pltpu.VMEM) if isinstance(spec, Whole) else spec for spec in specs]
            for specs in (in_specs, out_specs)
        )
        deps = self.last
        skip = 1 + len(ins)

        def inner(*refs):
            bits, *refs = (*refs[:skip], *refs[skip + len(deps) :])
            parts = [ref.at[pl.program_id(0)] if mark else ref for ref, mark in zip(refs, marks)]
            kernel(bits, *parts, *refs[len(marks) :])

        moved = sum(value.size * value.dtype.itemsize for value in (*ins, *outs))
        results = pl.pallas_call(
            inner,
            grid_spec=pltpu.PrefetchScalarGridSpec(
                num_scalar_prefetch=1,
                grid=grid,
                in_specs=in_specs + [pl.BlockSpec(memory_space=pl.ANY)] * len(deps),
                out_specs=out_specs,
                scratch_shapes=list(scratch),
            ),
            out_shape=list(outs),
            cost_estimate=pl.CostEstimate(flops=flops, bytes_accessed=moved, transcendentals=0),
            compiler_params=pltpu.CompilerParams(vmem_limit_bytes=limit * MEBI),
        )(self.bits, *ins, *deps)
        self.last = (results[-1],)
        return results

    def need(self, *values):
        self.last += values

    def tie(self, values):
        return lax.optimization_barrier((values, self.last))[0]


def merge(line, pairs, places):
    count = len(pairs)

    def kernel(bits, *refs):
        for place in range(count):
            (mine, other), out = refs[2 * place : 2 * place + 2], refs[2 * count + place]
            bit = bits[places[place]]
            out[:, pl.ds(bit, 1)] = mine[...][:, None]
            out[:, pl.ds(1 - bit, 1)] = other[...][:, None]

    outs = [struct((mine.shape[0], 2) + mine.shape[1:], low) for mine, _ in pairs]
    return line.run(kernel, outs, [value for pair in pairs for value in pair])


def split(line, pairs, places):
    count = len(pairs)

    def kernel(bits, *refs):
        for place in range(count):
            terms, outs = refs[2 * place : 2 * place + 2], refs[2 * (count + place) : 2 * (count + place) + 2]
            bit = bits[places[place]]
            for index, out in zip((1 - bit, bit), outs):
                total = sum(term[:, pl.ds(index, 1)].astype(f32) for term in terms)
                out[...] = total[:, 0].astype(low)

    outs = [struct(pair[0].shape[:1] + pair[0].shape[2:], low) for pair in pairs for _ in range(2)]
    results = line.run(kernel, outs, [value for pair in pairs for value in pair])
    return list(zip(results[::2], results[1::2]))


class Gather:
    def __init__(self, line, shard, order, dims, relative):
        self.line, self.order, self.dims, self.relative = line, list(order), dims, relative
        self.sizes = {dim: 1 for dim in dims}
        self.columns = shard.shape[1]
        self.mine = line.tie(shard)
        self.begin()

    def begin(self):
        self.step = self.order.pop(0)
        self.arrived = swap(self.mine, *self.step)

    def pair(self):
        place = self.dims.index(self.step)
        outer = math.prod(self.sizes[dim] for dim in self.dims[:place])
        shape = (outer, -1, self.columns)
        return self.mine.reshape(shape), self.arrived.reshape(shape)

    def end(self, piece):
        self.mine = piece.reshape(-1, self.columns)
        self.sizes[self.step] = 2
        self.begin()


class Scatter:
    def __init__(self, line, kept, sent, order, dims, relative, arrived=None):
        self.line, self.order, self.dims, self.relative = line, list(order), dims, relative
        self.sizes = {dim: 2 if dim in self.order else 1 for dim in dims}
        self.columns = kept.shape[-1]
        self.begin(kept, sent, arrived)

    def begin(self, kept, sent, arrived=None):
        self.step = self.order.pop(0)
        self.sizes[self.step] = 1
        flat = (-1, self.columns)
        if arrived is None:
            arrived = swap(sent.reshape(flat), *self.step)
        self.terms = [kept.reshape(flat), arrived.reshape(flat)]

    def pair(self):
        place = self.dims.index(self.order[0])
        outer = math.prod(self.sizes[dim] for dim in self.dims[:place])
        return [term.reshape(outer, 2, -1, self.columns) for term in self.terms]

    def end(self, halves):
        sent, kept = halves
        self.begin(kept, sent)


def go(line, *walks):
    gathers = isinstance(walks[0], Gather)
    steps = [walk.step if gathers else walk.order[0] for walk in walks]
    places = [0 if step in walk.relative else line.place[step] for step, walk in zip(steps, walks)]
    results = (merge if gathers else split)(line, [walk.pair() for walk in walks], places)
    for walk, result in zip(walks, results):
        walk.end(result)


class Pieces:
    def __init__(self, line, walk, across, arrays=None):
        self.line, self.walk, self.across = line, walk, walk.step == across
        self.columns = walk.columns
        self.arrays = arrays
        if arrays is None:
            self.arrays = list(walk.pair())
            if not self.across:
                self.arrays = [value.reshape((2, -1) + value.shape[1:]) for value in self.arrays]

    def flip(self, core, tied=False):
        across = (TENSOR, bits_of(TENSOR)[0])
        arrays = self.line.tie(self.arrays) if tied else self.arrays
        return Pieces(self.line, self.walk, across, [swap(value, *core) for value in arrays])

    def specs(self):
        return [whole(value) if self.across else each(value) for value in self.arrays]

    def scratch(self):
        shape = self.arrays[0].shape[1:]
        return [pltpu.VMEM((1,) + shape if self.across else (shape[0], 2) + shape[1:], low)]

    def load(self, bits, refs, held):
        mine, arrived = refs
        if self.across:
            step = pl.program_id(0)

            @pl.when(step == 0)
            def _():
                held[0][...] = mine[...]

            @pl.when(step > 0)
            def _():
                held[0][...] = arrived[...]

            return held[0][...].reshape(-1, self.columns)
        return put_together(bits[self.line.place[self.walk.step]], mine, arrived, held[0])


class Both:
    def __init__(self, first, second):
        self.parts = first, second
        self.arrays = first.arrays + second.arrays
        self.columns = first.columns + second.columns

    def flip(self, core):
        return Both(*(part.flip(core) for part in self.parts))

    def specs(self):
        return [spec for part in self.parts for spec in part.specs()]

    def scratch(self):
        return [space for part in self.parts for space in part.scratch()]

    def load(self, bits, refs, held):
        first, second = self.parts
        return first.load(bits, refs[:2], held[:1]), second.load(bits, refs[2:], held[1:])


class Halves:
    def __init__(self, line, width, columns, step=None, dims=(), arrived=None, start=0):
        self.line, self.step, self.arrived, self.start, self.columns = line, step, arrived, start, columns
        self.across = step is not None and step == dims[0]
        if step is None:
            self.outs = [struct((2, width, columns), low)]
        elif self.across:
            self.outs = [struct((width, columns), low)] * 2
        else:
            outer = 1 << (dims.index(step) - 1)
            self.outs = [struct((2, outer, width // (2 * outer), columns), low)] * 2

    def specs(self):
        return [whole(value) if self.across else each(value) for value in self.outs]

    def store(self, bits, before, outs, total):
        if self.step is None:
            outs[0][...] = total.astype(low)
            return
        kept, sent = outs
        arrived = before[:, self.start : self.start + self.columns]
        total = (total + arrived.astype(f32)).astype(low)
        if self.across:
            step = pl.program_id(0)

            @pl.when(step == 0)
            def _():
                kept[...] = total

            @pl.when(step > 0)
            def _():
                sent[...] = total

        else:
            mine = bits[self.line.place[self.step]] == 1
            total = total.reshape(kept.shape[0], 2, *kept.shape[1:])
            kept[...] = jnp.where(mine, total[:, 1], total[:, 0])
            sent[...] = jnp.where(mine, total[:, 0], total[:, 1])


def from_owner(blocks):
    return [block if step == 0 else swap(block, TENSOR, step) for step, block in enumerate(blocks)]


def unflip(values, dim, axis):
    masks = bits_of(axis)
    shape = values.shape
    values = values.reshape(shape[:dim] + (2,) * len(masks) + shape[dim + 1 :])
    for place, mask in enumerate(masks):
        values = jnp.where(
            my_bit(axis, mask) == 1, jnp.flip(values, dim + place), values
        )
    return values.reshape(shape)


def exchange_steps(line, values):
    shape = values.shape
    dims = [("dp", mask) for mask in bits_of("dp")]
    dims += [(TENSOR, mask) for mask in bits_of(TENSOR)]
    values = values.reshape((2,) * len(dims) + shape[2:])
    for dim, (axis, mask) in enumerate(dims):
        values = line.tie(values)
        kept = lax.slice_in_dim(values, 0, 1, axis=dim)
        arrived = swap(lax.slice_in_dim(values, 1, 2, axis=dim), axis, mask)
        values = jnp.concatenate([kept, arrived], axis=dim)
        line.need(values)
        yield None
    yield values.reshape(shape)


def mean_last(values):
    return jnp.mean(values, axis=-1, keepdims=True)


def normalise(values):
    center = values - mean_last(values)
    inverse = lax.rsqrt(mean_last(center * center) + norm_eps)
    return center * inverse, inverse


def norm_back(normal, inverse, grad, scale):
    scaled = grad * (1.0 + scale)
    return inverse * (scaled - mean_last(scaled) - normal * mean_last(scaled * normal))


def dg(left, right, left_dim, right_dim):
    return lax.dot_general(
        left, right, (((left_dim,), (right_dim,)), ((), ())), preferred_element_type=f32
    )


def pack(line, skip, inputs, output, up, down):
    inner, block = inputs.shape[2], up.shape[1] // 2

    def kernel(bits, skip, inputs, output, up, down, skip_out, qk, vo, *feeds):
        skip_out[...] = skip[...].astype(low)
        qk[:, :inner] = inputs[0].astype(low)
        qk[:, inner:] = inputs[1].astype(low)
        vo[:, :inner] = inputs[2].astype(low)
        vo[:, inner:] = output[...].T.astype(low)
        for place, out in enumerate(feeds):
            here = slice(place * block, (place + 1) * block)
            out[:, :block] = up[:, here].astype(low)
            out[:, block:] = down[here, :].T.astype(low)

    outs = [struct(skip.shape, low)] + [struct((inputs.shape[1], 2 * inner), low)] * 2 + [struct(up.shape, low)] * 2
    return line.run(kernel, outs, [skip, inputs, output, up, down])


def cut(line, arrays):
    count, _, rows, width = arrays[0].shape

    def kernel(bits, *refs):
        for place in range(count):

            @pl.when(pl.program_id(0) == place)
            def _():
                for index in range(len(arrays)):
                    here = slice(index * width, (index + 1) * width)
                    refs[len(arrays) + place][:, here] = refs[index][0, 0]

    out = struct((rows, len(arrays) * width), low)
    return line.run(
        kernel,
        [out] * count,
        list(arrays),
        grid=(count,),
        in_specs=[pl.BlockSpec((1, 1, rows, width), lambda i, bits: (bits[1] ^ i, 0, 0, 0))] * len(arrays),
    )


def put_together(bit, mine, arrived, held):
    held[:, pl.ds(bit, 1)] = mine[...][:, None]
    held[:, pl.ds(1 - bit, 1)] = arrived[...][:, None]
    return held[...].reshape(-1, held.shape[-1])


def together(pair):
    return pltpu.VMEM((pair[0].shape[0], 2) + pair[0].shape[1:], low)


def enter(line, blocks, pair, place, keep):
    count = len(blocks)
    length, width = sum(block.shape[0] for block in blocks), pair[0].shape[-1]
    depth = 2 * width

    def kernel(bits, *refs):
        blocks, skips, keep = refs[:count], refs[count : count + 2], refs[count + 2]
        hidden, outer, joined, held = refs[count + 3 :]
        rows = blocks[0].shape[0]
        for index, block in enumerate(blocks):
            here = slice(index * rows, (index + 1) * rows)
            joined[here, :] = block[:, :depth]
            outer[here, :] = (keep[here, :] * block[:, depth:].astype(f32)).astype(low)
        put_together(bits[place], *skips, held)
        half = width // 2
        for here in (slice(0, half), slice(half, width)):
            hidden[:, here] = dg(joined[...], held[:, :, :, here].reshape(depth, half), 1, 0)

    return line.run(
        kernel,
        [struct((length, width), f32), struct((length, width), low)],
        [*blocks, *pair, keep],
        scratch=[pltpu.VMEM((length, depth), low), together(pair)],
        flops=2 * length * width * depth,
        limit=14,
    )


def half_turn(values):
    lanes = lax.broadcasted_iota(jnp.int32, values.shape, 1) % HEAD_DIM
    width = values.shape[1]
    half = HEAD_DIM // 2
    return jnp.where(
        lanes < half, pltpu.roll(values, width - half, 1), pltpu.roll(values, half, 1)
    )


def shares_of(keys, queries, ok):
    scores = jnp.where(ok > 0, dg(keys, queries, 1, 1), neg_large)
    weights = jnp.exp(scores - jnp.max(scores, axis=0, keepdims=True))
    return weights * (1.0 / jnp.sum(weights, axis=0, keepdims=True))


def attend_piece(normed, qk, vo, cosine, sine, ok, held, mixed):
    inner = qk.shape[1] // 2
    rows = normed.shape[0]
    for part in range(3):
        weight = (qk[:, :inner], qk[:, inner:], vo[:, :inner])[part]
        project = dg(normed[...], weight, 1, 0)
        if part < 2:
            project = project * cosine[...] + half_turn(project) * sine[...]
        if part == 0:
            project = project * HEAD_DIM**-0.5
        held[:, part * inner : (part + 1) * inner] = project.astype(low)
    queries = held[:, :inner]
    keys = held[:, inner : 2 * inner]
    values = held[:, 2 * inner :]
    owner = lax.broadcasted_iota(jnp.int32, (rows, inner), 1) // HEAD_DIM
    zero = jnp.zeros((), low)
    total = None
    for head in range(inner // HEAD_DIM):
        mine = owner == head
        shares = shares_of(keys, jnp.where(mine, queries, zero), ok[...]).astype(low)
        term = dg(shares, jnp.where(mine, values, zero), 0, 0)
        total = term if total is None else total + term
    mixed[...] = total.astype(low)
    return dg(mixed[...], vo[:, inner:], 1, 1).astype(low).astype(f32)


def add_up(total, term, step):
    @pl.when(step == 0)
    def _():
        total[...] = term

    @pl.when(step > 0)
    def _():
        total[...] += term


def attend(line, weights, cosine, sine, ok, hidden, shift, scale, normed=None, before=None):
    rows, width = hidden.shape
    inner = weights.columns // 4
    total = struct((rows, width), f32)
    outs = [struct((2, rows, 3 * inner), low), struct((2, rows, inner), low), total, struct((rows, width), low)]
    plain = [cosine, sine, ok, hidden, shift, scale]
    plain += [] if before is None else [normed, before]
    arrays = weights.arrays

    def kernel(bits, *refs):
        tables, refs = refs[: len(arrays)], refs[len(arrays) :]
        (cosine, sine, ok, hidden, shift, scale, *more), refs = refs[: len(plain)], refs[len(plain) :]
        held, mixed, out, after, *scratch = refs
        step = pl.program_id(0)

        def modulate(values):
            normal, _ = normalise(values)
            after[...] = (normal * (1.0 + scale[...]) + shift[...]).astype(low)

        if not more:

            @pl.when(step == 0)
            def _():
                modulate(hidden[...])

        qk, vo = weights.load(bits, tables, scratch)
        normed = more[0] if more else after
        term = attend_piece(normed, qk, vo, cosine, sine, ok, held, mixed)
        add_up(out, term, step)
        if more:

            @pl.when(step == pl.num_programs(0) - 1)
            def _():
                total = hidden[...] + (more[1][...] + out[...])
                out[...] = total
                modulate(total)

    return line.run(
        kernel,
        outs,
        [*arrays, *plain],
        grid=(2,),
        in_specs=[*weights.specs(), *(whole(value) for value in plain)],
        out_specs=[each(outs[0]), each(outs[1]), whole(total), whole(total)],
        scratch=weights.scratch(),
        flops=2 * rows * (8 * width * inner + 16 * rows * inner),
        limit=20,
    )


def gelu_pair(values):
    root = math.sqrt(2.0 / math.pi)
    cube = 0.044715 * values * values
    slope = jnp.tanh(root * values * (1.0 + cube))
    gate = 0.5 * (1.0 + slope)
    back = gate + 0.5 * values * (1.0 - slope * slope) * root * (1.0 + 3.0 * cube)
    return values * gate, back


def feed(line, normed, outer, weights, halves, before=None):
    rows, width = normed.shape
    half = weights.columns // 2
    end = struct((rows, width), low)
    arrays = weights.arrays
    extra = [] if before is None else [before]

    def kernel(bits, *refs):
        tables, (normed, outer, *refs) = refs[: len(arrays)], refs[len(arrays) :]
        before, refs = refs[: len(extra)], refs[len(extra) :]
        outs, (fed, back, fed_total, back_total, *scratch) = refs[: len(halves.outs)], refs[len(halves.outs) :]
        step = pl.program_id(0)
        now = weights.load(bits, tables, scratch)
        up, down = now[:, :half], now[:, half:]
        value, slope = gelu_pair(dg(normed[...], up, 1, 0))
        gated = value.astype(low)
        lifted = (dg(outer[...], down, 1, 0) * slope).astype(low)
        grad = jnp.concatenate([dg(normed[...], lifted, 0, 0), dg(outer[...], gated, 0, 0)], axis=1)
        halves.store(bits, *(before or (None,)), outs, grad)
        add_up(fed_total, dg(gated, down, 1, 1), step)
        add_up(back_total, dg(lifted, up, 1, 1), step)

        @pl.when(step == pl.num_programs(0) - 1)
        def _():
            fed[...] = fed_total[...].astype(low)
            back[...] = back_total[...].astype(low)

    return line.run(
        kernel,
        [*halves.outs, end, end],
        [*arrays, normed, outer, *extra],
        grid=(2,),
        in_specs=[*weights.specs(), whole(normed), whole(outer), *(each(value) for value in extra)],
        out_specs=[*halves.specs(), whole(end), whole(end)],
        scratch=[pltpu.VMEM((rows, width), f32)] * 2 + weights.scratch(),
        flops=24 * rows * width * half,
        limit=22,
    )


def bend_kernel(middle, outer, keep, scale, *refs):
    *parts, result, middle_grad, middle_low, sums = refs
    count = len(parts) // 2
    fed = sum(part[...].astype(f32) for part in parts[:count])
    grad = sum(part[...].astype(f32) for part in parts[count:])
    result[...] = (keep[...] * (middle[...] + fed)).astype(low)
    normal, inverse = normalise(middle[...])
    total = outer[...].astype(f32) + norm_back(normal, inverse, grad, scale[...])
    middle_grad[...] = total
    middle_low[...] = total.astype(low)
    sums[0:1, :] = jnp.sum(grad, axis=0, keepdims=True)
    sums[1:2, :] = jnp.sum(grad * normal, axis=0, keepdims=True)


def bend(line, middle, outer, keep, scale, fed, back):
    shape = middle.shape
    outs = [struct(shape, low), struct(shape, f32), struct((2, shape[1]), f32), struct(shape, low)]

    def kernel(bits, *refs):
        *refs, sums, middle_low = refs
        bend_kernel(*refs, middle_low, sums)

    return line.run(kernel, outs, [middle, outer, keep, scale, *fed, *back], limit=14)


def back_piece(normed, middle_low, qk, vo, held, mixed, cosine, sine, ok, project):
    inner = qk.shape[1] // 2
    rows = normed.shape[0]
    queries = held[:, :inner]
    keys = held[:, inner : 2 * inner]
    values = held[:, 2 * inner :]
    above = dg(middle_low[...], vo[:, inner:], 1, 0).astype(low)
    owner = lax.broadcasted_iota(jnp.int32, (rows, inner), 1) // HEAD_DIM
    zero = jnp.zeros((), low)
    query_grad = key_grad = value_grad = jnp.zeros((rows, inner), f32)
    for head in range(inner // HEAD_DIM):
        mine = owner == head
        queries_here = jnp.where(mine, queries, zero)
        above_here = jnp.where(mine, above, zero)
        shares = shares_of(keys, queries_here, ok[...])
        share_grad = dg(values, above_here, 1, 1)
        inside = jnp.sum(share_grad * shares, axis=0, keepdims=True)
        score_grad = (shares * (share_grad - inside)).astype(low)
        value_grad += dg(shares.astype(low), above_here, 1, 0)
        key_grad += dg(score_grad, queries_here, 1, 0)
        query_grad += dg(score_grad, jnp.where(mine, keys, zero), 0, 0)
    query_grad = query_grad * HEAD_DIM**-0.5
    for place, grad in enumerate((query_grad, key_grad)):
        turned = grad * cosine[...] - half_turn(grad) * sine[...]
        project[:, place * inner : (place + 1) * inner] = turned.astype(low)
    project[:, 2 * inner :] = value_grad.astype(low)
    qk_grad = dg(normed[...], project[:, : 2 * inner], 0, 0)
    vo_grad = jnp.concatenate(
        [dg(normed[...], project[:, 2 * inner :], 0, 0), dg(middle_low[...], mixed[...], 0, 0)], axis=1
    )
    term = dg(project[:, : 2 * inner], qk, 1, 1)
    term += dg(project[:, 2 * inner :], vo[:, :inner], 1, 1)
    return qk_grad, vo_grad, term.astype(low).astype(f32)


def attend_back(line, normed, middle_low, weights, held, mixed, cosine, sine, ok, parts, before=None, last=()):
    rows, width = normed.shape
    inner = weights.columns // 4
    arrays = weights.arrays
    plain = [normed, middle_low, held, mixed, cosine, sine, ok, *last]
    extra = [] if before is None else [before]
    scratch = [pltpu.VMEM((rows, 3 * inner), low), *weights.scratch()]
    if last:
        ends = [struct((2, width), f32), struct((rows, width), low)]
        scratch = [pltpu.VMEM((rows, width), f32)] + scratch
    else:
        ends = [struct((rows, width), f32)]

    def kernel(bits, *refs):
        tables, refs = refs[: len(arrays)], refs[len(arrays) :]
        (*args, cosine, sine, ok), refs = refs[:7], refs[7:]
        more, refs = refs[: len(last)], refs[len(last) :]
        before, refs = refs[: len(extra)], refs[len(extra) :]
        outs = []
        for part in parts:
            outs.append(refs[: len(part.outs)])
            refs = refs[len(part.outs) :]
        marks, (total, project, *scratch) = (refs[:2], refs[2:]) if last else ((), refs)
        step = pl.program_id(0)
        normed, middle_low, held, mixed = args
        qk, vo = weights.load(bits, tables, scratch)
        *grads, term = back_piece(
            normed, middle_low, qk, vo, held, mixed, cosine, sine, ok, project
        )
        if len(parts) == 1:
            grads = [jnp.concatenate(grads, axis=1)]
        for part, out, grad in zip(parts, outs, grads):
            part.store(bits, *(before or (None,)), out, grad)
        add_up(total, term, step)
        if last:
            ahead, hidden, middle_grad, scale = more
            sums, hidden_low = marks

            @pl.when(step == pl.num_programs(0) - 1)
            def _():
                grad = ahead[...] + total[...]
                normal, inverse = normalise(hidden[...])
                hidden_low[...] = (
                    middle_grad[...] + norm_back(normal, inverse, grad, scale[...])
                ).astype(low)
                sums[0:1, :] = jnp.sum(grad, axis=0, keepdims=True)
                sums[1:2, :] = jnp.sum(grad * normal, axis=0, keepdims=True)

    outs = [value for part in parts for value in part.outs]
    return line.run(
        kernel,
        [*outs, *ends],
        [*arrays, *plain, *extra],
        grid=(2,),
        in_specs=[
            *weights.specs(),
            *(each(value) if value.ndim == 3 else whole(value) for value in plain),
            *(each(value) for value in extra),
        ],
        out_specs=[spec for part in parts for spec in part.specs()] + [whole(value) for value in ends],
        scratch=scratch,
        flops=2 * rows * (16 * width * inner + 40 * rows * inner),
        limit=24,
    )


def leave(line, blocks, hidden_low, place, parts):
    count = len(blocks)
    length, width = hidden_low.shape
    depth = 2 * width

    def kernel(bits, *refs):
        blocks, hidden_low, sent, kept, joined = refs[:count], *refs[count:]
        rows = blocks[0].shape[0]
        for index, block in enumerate(blocks):
            joined[index * rows : (index + 1) * rows, :] = block[:, :depth]
        mine = bits[place] == 1
        half = width // 2
        for here in (slice(0, half), slice(half, width)):
            total = dg(joined[...], hidden_low[:, here], 0, 0)
            total = total.reshape(sent.shape[0], 2, -1, half)
            sent[:, :, here] = jnp.where(mine, total[:, 0], total[:, 1]).astype(low)
            kept[:, :, here] = jnp.where(mine, total[:, 1], total[:, 0]).astype(low)

    return line.run(
        kernel,
        [struct((parts // 2, depth // parts, width), low)] * 2,
        [*blocks, hidden_low],
        scratch=[pltpu.VMEM((length, depth), low)],
        flops=2 * length * width * depth,
        limit=16,
    )


def inputs_back(line, blocks, results, pair, place):
    count = len(blocks)
    length, width = sum(block.shape[0] for block in blocks), blocks[0].shape[1]

    def kernel(bits, *refs):
        blocks, results, skips = refs[:count], refs[count : 2 * count], refs[2 * count : 2 * count + 2]
        frame_grad, skip_grad, result, hidden, held = refs[2 * count + 2 :]
        rows = blocks[0].shape[0]
        for index in range(count):
            start = pl.multiple_of((bits[1] ^ index) * rows, rows)
            hidden[pl.ds(start, rows), :] = blocks[index][...]
            result[pl.ds(start, rows), :] = results[index][...]
        skip = put_together(bits[place], *skips, held)
        frame_grad[...] = dg(hidden[...], skip[:width], 1, 1)
        skip_grad[...] = dg(hidden[...], skip[width:], 1, 1)

    return line.run(
        kernel,
        [struct((length, width), f32)] * 2 + [struct((length, width), low)],
        [*blocks, *results, *pair],
        scratch=[pltpu.VMEM((length, width), low), together(pair)],
        flops=4 * length * width * width,
        limit=14,
    )


def adam_update(master, first, second, grad, rate):
    first_new = beta_first * first + (1.0 - beta_first) * grad
    second_new = beta_second * second + (1.0 - beta_second) * grad * grad
    first_hat = first_new / (1.0 - beta_first**STEP)
    second_hat = second_new / (1.0 - beta_second**STEP)
    master_new = master - rate * (
        first_hat / (jnp.sqrt(second_hat) + adam_eps) + decay_rate * master
    )
    return (first_new, second_new, master_new, master_new.astype(low))


def added(pair):
    return pair[0][...].astype(f32) + pair[1][...].astype(f32)


def store_update(states, grad, rate, outs):
    for out, value in zip(outs, adam_update(*(state[...] for state in states), grad, rate)):
        out[...] = value


def update_outs(master):
    return [struct(master.shape, f32)] * 3 + [struct(master.shape, low)]


def update_feed(line, first, second, ups, downs):
    def kernel(bits, *refs):
        pairs, ups, downs = (refs[:2], refs[2:4]), refs[4:7], refs[7:10]
        up_outs, down_outs = refs[10:14], refs[14:18]
        totals = [added(pair) for pair in pairs]
        half = totals[0].shape[1] // 2
        store_update(ups, jnp.concatenate([total[:, :half] for total in totals], axis=1), rates[4], up_outs)
        store_update(
            downs, jnp.concatenate([total[:, half:].T for total in totals], axis=0), rates[5], down_outs
        )

    return line.run(kernel, update_outs(ups[0]) + update_outs(downs[0]), [*first, *second, *ups, *downs], limit=10)


def update_attention(line, qk, vo, inputs, outputs):
    def kernel(bits, *refs):
        qk, vo, inputs, outputs = refs[:2], refs[2:4], refs[4:7], refs[7:10]
        input_outs, output_outs = refs[10:14], refs[14:18]
        qk, vo = added(qk), added(vo)
        inner = qk.shape[1] // 2
        for place, grad in enumerate((qk[:, :inner], qk[:, inner:], vo[:, :inner])):
            store_update(
                [state.at[place] for state in inputs], grad, rates[2], [out.at[place] for out in input_outs]
            )
        store_update(outputs, vo[:, inner:].T, rates[3], output_outs)

    return line.run(kernel, update_outs(inputs[0]) + update_outs(outputs[0]), [*qk, *vo, *inputs, *outputs], limit=10)


def update_skip(line, pair, skips):
    def kernel(bits, *refs):
        store_update(refs[2:5], added(refs[:2]), rates[0], refs[5:9])

    return line.run(kernel, update_outs(skips[0]), [*pair, *skips], limit=8)


def orders():
    dp_bits, tensor_bits = bits_of("dp"), bits_of(TENSOR)
    far = [("dp", mask) for mask in dp_bits[:-2]]
    y, z = ("dp", dp_bits[-1]), ("dp", dp_bits[-2])
    x = (TENSOR, tensor_bits[0])
    return {
        "xzy": far + [x, z, y],
        "yzx": far + [y, z, x],
        "zxy": far + [z, x, y],
        "zyx": far + [z, y, x],
        "yxz": far + [y, x, z],
        "xyz": far + [x, y, z],
    }


def body(
    frames,
    skip_frames,
    time_embed,
    lengths,
    out_grad,
    skip_weight,
    adapt_weight,
    input_weight,
    output_weight,
    up_weight,
    down_weight,
    skip_first,
    adapt_first,
    input_first,
    output_first,
    up_first,
    down_first,
    skip_second,
    adapt_second,
    input_second,
    output_second,
    up_second,
    down_second,
):
    micro, _, rows, width = frames.shape
    parts = lax.axis_size(TENSOR)
    groups = lax.axis_size("dp")
    me = lax.axis_index(TENSOR)
    inner = input_weight.shape[2]
    heads = inner // HEAD_DIM
    highest = lax.Precision.HIGHEST
    order = orders()
    skip_order, skip_back_order = order["xzy"], order["zyx"]
    attention_orders, attention_back_orders = (order["xyz"], order["xzy"]), (order["xzy"], order["yzx"])
    feed_orders, feed_back_orders = (order["yzx"], order["zxy"]), (order["zxy"], order["zyx"])
    core = (TENSOR, bits_of(TENSOR)[-1])
    across = (TENSOR, bits_of(TENSOR)[0])
    dims = [across] + [("dp", mask) for mask in bits_of("dp")]
    all_dims = dims[1:] + [across, core]
    line = Line()

    adapt_low = adapt_weight.astype(low)
    time_values = time_embed[:, 0, :].astype(f32)
    time_low = jax.nn.silu(time_values).astype(low)

    def modulation():
        time_all = unflip(time_low, 0, TENSOR)[None]
        for mask in reversed(bits_of("dp")):
            time_all = line.tie(time_all)
            time_all = jnp.concatenate([time_all, swap(time_all, "dp", mask)], axis=0)
            line.need(time_all)
            yield None
        time_rows = time_all.reshape(groups * micro, width)
        adapt_mine = jnp.dot(time_rows, adapt_low, preferred_element_type=f32).reshape(groups, micro, -1)
        for adapt_all in exchange_steps(line, adapt_mine):
            yield time_rows, adapt_all

    modulate = modulation()

    row_index = jnp.concatenate(
        [(me ^ step) * rows + jnp.arange(rows, dtype=jnp.int32) for step in range(parts)]
    )
    length = pick(lengths, me, 0)[0]
    keep = (row_index < length).astype(f32)[:, None]
    half = HEAD_DIM // 2
    frequency = 10000.0 ** (-jnp.arange(half).astype(f32) / half)
    angles = row_index.astype(f32)[:, None] * frequency[None, :]
    cosine = jnp.tile(jnp.cos(angles), (1, 2 * heads))
    sine = jnp.tile(jnp.concatenate([-jnp.sin(angles), jnp.sin(angles)], axis=1), (1, heads))

    next(modulate)
    skip_shard, qk_shard, vo_shard, *feed_shards = pack(
        line, skip_weight, input_weight.transpose(1, 0, 2), output_weight, up_weight, down_weight
    )
    skip_walk = Gather(line, skip_shard, skip_order + [core], all_dims, ())
    attention_walks = [
        Gather(line, shard, each_order, dims, (across,))
        for shard, each_order in zip((qk_shard, vo_shard), attention_orders)
    ]
    next(modulate)
    blocks = list(cut(line, (frames, skip_frames, out_grad)))
    blocks[2] = swap(blocks[2], TENSOR, 2)
    feed_walks = [
        Gather(line, shard, each_order, dims, (across,))
        for shard, each_order in zip(feed_shards, feed_orders)
    ]
    next(modulate)
    more = range(len(bits_of("dp")) - 3)
    for _ in more:
        go(line, skip_walk)
        go(line, *attention_walks)
        go(line, *feed_walks)
    go(line, skip_walk)
    next(modulate)
    go(line, *attention_walks)
    next(modulate)
    go(line, skip_walk)
    next(modulate)
    go(line, *feed_walks)
    next(modulate)
    line.need(blocks[2])
    blocks[3] = swap(line.tie(blocks[3]), TENSOR, 3)
    go(line, *attention_walks)
    for time_rows, adapt_all in modulate:
        pass
    go(line, skip_walk)
    adapt_vector = unflip(unflip(adapt_all, 0, "dp"), 1, TENSOR).reshape(1, -1)
    shift_one, scale_one, shift_two, scale_two = jnp.split(adapt_vector, 4, axis=1)
    go(line, *feed_walks)
    line.need(blocks[3])
    blocks[1] = swap(line.tie(blocks[1]), TENSOR, 1)
    go(line, *attention_walks)
    go(line, skip_walk)
    skip_pair = skip_walk.pair()
    hidden, outer = enter(line, blocks, skip_pair, line.place[core], keep)
    go(line, *feed_walks)
    attention_own = Both(*(Pieces(line, walk, across) for walk in attention_walks))
    held_own, mixed_own, attended, normed_one = attend(
        line, attention_own, cosine, sine, keep, hidden, shift_one, scale_one
    )
    attention_other = attention_own.flip(core)
    held_other, mixed_other, middle, normed_two = attend(
        line, attention_other, cosine, sine, keep, hidden, shift_two, scale_two, normed=normed_one, before=attended
    )
    fed, back, feed_arrived, feed_scatters = [], [], [], []
    feed_own = [Pieces(line, walk, across) for walk in feed_walks]
    columns = feed_shards[0].shape[1]
    feed_other = [pieces.flip(core, tied=True) for pieces in feed_own]
    for pieces in feed_other:
        grad, *ends = feed(line, normed_two, outer, pieces, Halves(line, width, columns))
        feed_arrived.append(swap(grad, *core))
        fed.append(ends[0])
        back.append(ends[1])
    for pieces, arrived, each_order in zip(feed_own, feed_arrived, feed_back_orders):
        halves = Halves(line, width, columns, each_order[-1], dims, arrived)
        kept, sent, *ends = feed(line, normed_two, outer, pieces, halves, arrived)
        feed_scatters.append(Scatter(line, kept, sent, each_order[::-1], dims, (across,)))
        fed.append(ends[0])
        back.append(ends[1])
    feed_one, feed_two = feed_scatters
    result, middle_grad, sums_two, middle_low = bend(line, middle, outer, keep, scale_two, fed, back)
    results = from_owner([result[step * rows : (step + 1) * rows] for step in range(parts)])
    qk_other, vo_other, ahead = attend_back(
        line,
        normed_one,
        middle_low,
        attention_other,
        held_other,
        mixed_other,
        cosine,
        sine,
        keep,
        [Halves(line, width, 2 * inner)] * 2,
    )
    attention_arrived = [swap(grad, *core) for grad in (qk_other, vo_other)]
    go(line, feed_one)
    go(line, feed_two)
    qk_grad, vo_grad, sums_one, hidden_low = attend_back(
        line,
        normed_one,
        middle_low,
        attention_own,
        held_own,
        mixed_own,
        cosine,
        sine,
        keep,
        [Halves(line, width, 2 * inner)] * 2,
        last=(ahead, hidden, middle_grad, scale_one),
    )
    attention_scatters = [
        Scatter(line, grad, None, [core] + each_order[::-1], dims, (across,), arrived)
        for grad, arrived, each_order in zip((qk_grad, vo_grad), attention_arrived, attention_back_orders)
    ]
    go(line, *attention_scatters)
    go(line, feed_one, feed_two)
    line.need(*results[1:])
    skip_sent, skip_kept = leave(line, blocks, hidden_low, line.place[core], groups * parts)
    skip_scatter = Scatter(line, skip_kept, skip_sent, [core] + skip_back_order[::-1], all_dims, ())
    hidden_back = from_owner([hidden_low[step * rows : (step + 1) * rows] for step in range(parts)])

    def modulation_back():
        adapt_back = jnp.concatenate([sums_one.reshape(-1), sums_two.reshape(-1)]).reshape(
            groups, parts, -1
        )
        for adapt_rows in exchange_steps(line, unflip(unflip(adapt_back, 0, "dp"), 1, TENSOR)):
            yield None
        adapt_rows = adapt_rows.reshape(groups * micro, -1)
        adapt_sum = lax.dot_general(
            time_rows.astype(f32), adapt_rows, (((0,), (0,)), ((), ())), precision=highest
        )
        time_part = lax.dot_general(
            adapt_rows, adapt_low.astype(f32), (((1,), (1,)), ((), ())), precision=highest
        ).reshape(groups, micro, width)
        for mask in bits_of("dp"):
            time_part = line.tie(time_part)
            time_part = time_part[:mask] + swap(time_part[mask:], "dp", mask)
            yield None
        time_part = unflip(time_part[0], 0, TENSOR)
        for mask in bits_of(TENSOR):
            time_part = line.tie(time_part)
            time_part = time_part + swap(time_part, TENSOR, mask)
            yield None
        yield adapt_sum, time_part

    modulate_back = modulation_back()
    go(line, skip_scatter)
    next(modulate_back)
    go(line, *attention_scatters)
    next(modulate_back)
    go(line, feed_one, feed_two)
    next(modulate_back)
    go(line, skip_scatter)
    next(modulate_back)
    go(line, *attention_scatters)
    next(modulate_back)
    line.need(feed_one.terms[1], feed_two.terms[1])
    line.need(*hidden_back[1:])
    frame_grads, skip_grads, results = inputs_back(
        line, hidden_back, results, skip_pair, line.place[core]
    )
    frame_grads, skip_grads = frame_grads.reshape(frames.shape), skip_grads.reshape(frames.shape)
    next(modulate_back)
    go(line, skip_scatter)
    next(modulate_back)
    go(line, *attention_scatters)
    next(modulate_back)
    go(line, skip_scatter)
    for _ in more:
        go(line, feed_one, feed_two)
        go(line, *attention_scatters)
        go(line, skip_scatter)
    next(modulate_back)
    line.need(*(walk.terms[1] for walk in attention_scatters))
    feed_new = update_feed(
        line,
        feed_one.terms,
        feed_two.terms,
        (up_weight, up_first, up_second),
        (down_weight, down_first, down_second),
    )
    for ends in modulate_back:
        pass
    adapt_sum, time_part = ends
    sigmoid = jax.nn.sigmoid(time_values)
    time_grad = time_part * (sigmoid * (1.0 + time_values * (1.0 - sigmoid)))
    attention_new = update_attention(
        line,
        attention_scatters[0].terms,
        attention_scatters[1].terms,
        [state.transpose(1, 0, 2) for state in (input_weight, input_first, input_second)],
        (output_weight, output_first, output_second),
    )
    skip_new = update_skip(line, skip_scatter.terms, (skip_weight, skip_first, skip_second))
    adapt_new = adam_update(adapt_weight, adapt_first, adapt_second, adapt_sum, rates[1])
    return (
        results.reshape(frames.shape),
        frame_grads,
        skip_grads,
        time_grad[:, None, :],
        *skip_new,
        *adapt_new,
        *(value.transpose(1, 0, 2) for value in attention_new[:4]),
        *attention_new[4:],
        *feed_new,
    )


def solution(mesh):
    groups, parts = mesh.devices.shape
    split_mesh = Mesh(mesh.devices.reshape(groups, parts // 2, 2), ("dp", *TENSOR))
    return jax.shard_map(
        body,
        mesh=split_mesh,
        in_specs=(
            P(None, "dp", TENSOR, None),
            P(None, "dp", TENSOR, None),
            P(None, "dp", None),
            P(None, "dp"),
            P(None, "dp", TENSOR, None),
            P(("dp", *TENSOR), None),
            P(None, ("dp", *TENSOR)),
            P("dp", None, TENSOR),
            P(TENSOR, "dp"),
            P("dp", TENSOR),
            P(TENSOR, "dp"),
            P(("dp", *TENSOR), None),
            P(None, ("dp", *TENSOR)),
            P("dp", None, TENSOR),
            P(TENSOR, "dp"),
            P("dp", TENSOR),
            P(TENSOR, "dp"),
            P(("dp", *TENSOR), None),
            P(None, ("dp", *TENSOR)),
            P("dp", None, TENSOR),
            P(TENSOR, "dp"),
            P("dp", TENSOR),
            P(TENSOR, "dp"),
        ),
        out_specs=(
            P(None, "dp", TENSOR, None),
            P(None, "dp", TENSOR, None),
            P(None, "dp", TENSOR, None),
            P(None, "dp", None),
            P(("dp", *TENSOR), None),
            P(("dp", *TENSOR), None),
            P(("dp", *TENSOR), None),
            P(("dp", *TENSOR), None),
            P(None, ("dp", *TENSOR)),
            P(None, ("dp", *TENSOR)),
            P(None, ("dp", *TENSOR)),
            P(None, ("dp", *TENSOR)),
            P("dp", None, TENSOR),
            P("dp", None, TENSOR),
            P("dp", None, TENSOR),
            P("dp", None, TENSOR),
            P(TENSOR, "dp"),
            P(TENSOR, "dp"),
            P(TENSOR, "dp"),
            P(TENSOR, "dp"),
            P("dp", TENSOR),
            P("dp", TENSOR),
            P("dp", TENSOR),
            P("dp", TENSOR),
            P(TENSOR, "dp"),
            P(TENSOR, "dp"),
            P(TENSOR, "dp"),
            P(TENSOR, "dp"),
        ),
        check_vma=False,
    )
```

time: 580 us -> 497 us (0.86)
  Pallas kernels: 249 us -> 160 us
  waiting for transfers between devices: 195 us -> 213 us
  local copies, waits for them, and re-layouts: 24.7 us -> 40.7 us
  starting transfers between devices: 84.1 us -> 68.2 us
  other arithmetic: 15.6 us -> 1.44 us
    pallas_call x38 -> x39, Pallas kernels: 249 us -> 160 us  [run(): pl.pallas_call(inner, grid_spec=pltpu.PrefetchScalarGridSpec(num_scalar_p...]
    ppermute x91 -> x81, waiting for transfers between devices: 195 us -> 213 us  [swap(): return lax.ppermute(values, axis, [(i, i ^ mask) for i in range(count)])]
    unnamed x129 -> x175, local copies, waits for them, and re-layouts: 14.1 us -> 31 us
    ppermute x91 -> x81, starting transfers between devices: 84.1 us -> 68.2 us  [swap(): return lax.ppermute(values, axis, [(i, i ^ mask) for i in range(count)])]
    concatenate x28 -> x11, other arithmetic: 10.5 us -> 0.12 us  [the longest x10 0.11 us: exchange_steps(): values = jnp.concatenate([kept, arrived], axis=dim)]
  transfers between devices with their start and end apart: 91 -> 81, of which waited for: 36 -> 38; matrix products, arithmetic and copies ran while one was open for 5% -> 3% of each run, Pallas kernels for 42% -> 31%
where the time goes in v3:
time: 497 us; the launch traced here: 490 us
  waiting for transfers between devices  213 us (43%)
  Pallas kernels  160 us (32%)
  starting transfers between devices  68.2 us (14%)
  local copies, waits for them, and re-layouts  40.7 us (8%)
    ppermute x81, waiting for transfers between devices, swap(): return lax.ppermute(values, axis, [(i, i ^ mask) for i in range(count)])  213 us
    pallas_call x39, Pallas kernels, run(): pl.pallas_call(inner, grid_spec=pltpu.PrefetchScalarGridSpec(num_scalar_p...  160 us
    ppermute x81, starting transfers between devices, swap(): return lax.ppermute(values, axis, [(i, i ^ mask) for i in range(count)])  68.2 us
    unnamed x175, local copies, waits for them, and re-layouts  31 us
  transfers between devices with their start and end apart: 81, of which 38 were waited for; matrix products, arithmetic and copies ran while one was open for 3% of the time, Pallas kernels for 31%

profile of v3, /device:TPU:0, one launch (start us, length us, event | category | flops | bytes accessed | tf_op | source)
XLA Modules:
  0.0 489.6 jit_solution(10597123644157685364)
XLA Ops:
  25.4 9.0 %collective-permute-done.5 = bf16[4,4,1024]{2,1,0:T(4,128)(2,1)S(1)} collective-permute-done((bf16[4,4,1024]{2,1,0:T(4,128)(2,1)S(1)}, bf16[4,4,1024]{2,1,0:T(4,128)(2,1)S(1)}, u32[]{:S(2)}, u32[]{:S(2)}) %collective-permute-start.5) | collective-permute-done | bytes 32800 | tf_op jit(solution)/shard_map/ppermute | solution.py:39
  50.2 10.1 %collective-permute-done.9 = bf16[128,1024]{1,0:T(8,128)(2,1)S(1)} collective-permute-done((bf16[128,1024]{1,0:T(8,128)(2,1)S(1)}, bf16[128,1024]{1,0:T(8,128)(2,1)S(1)}, u32[]{:S(2)}, u32[]{:S(2)}) %collective-permute-start.9) | collective-permute-done | bytes 262176 | tf_op jit(solution)/shard_map/ppermute | solution.py:39
  79.4 8.1 %collective-permute-done.19 = bf16[256,1024]{1,0:T(8,128)(2,1)S(1)} collective-permute-done((bf16[256,1024]{1,0:T(8,128)(2,1)S(1)}, bf16[256,1024]{1,0:T(8,128)(2,1)S(1)}, u32[]{:S(2)}, u32[]{:S(2)}) %collective-permute-start.19) | collective-permute-done | bytes 524320 | tf_op jit(solution)/shard_map/ppermute | solution.py:39
  89.0 24.9 %collective-permute-done.18 = bf16[256,1024]{1,0:T(8,128)(2,1)S(1)} collective-permute-done((bf16[256,1024]{1,0:T(8,128)(2,1)S(1)}, bf16[256,1024]{1,0:T(8,128)(2,1)S(1)}, u32[]{:S(2)}, u32[]{:S(2)}) %collective-permute-start.18) | collective-permute-done | bytes 524320 | tf_op jit(solution)/shard_map/ppermute | solution.py:39
  116.0 8.2 %collective-permute-done.16 = bf16[512,512]{1,0:T(8,128)(2,1)S(1)} collective-permute-done((bf16[512,512]{1,0:T(8,128)(2,1)S(1)}, bf16[512,512]{1,0:T(8,128)(2,1)S(1)}, u32[]{:S(2)}, u32[]{:S(2)}) %collective-permute-start.16) | collective-permute-done | bytes 524320 | tf_op jit(solution)/shard_map/ppermute | solution.py:39
  162.5 14.0 %collective-permute-done.23 = bf16[1024,512]{1,0:T(8,128)(2,1)} collective-permute-done((bf16[1024,512]{1,0:T(8,128)(2,1)}, bf16[1024,512]{1,0:T(8,128)(2,1)}, u32[]{:S(2)}, u32[]{:S(2)}) %collective-permute-start.23) | collective-permute-done | bytes 1048608 | tf_op jit(solution)/shard_map/ppermute | solution.py:39
  180.8 12.2 %shard_map.451 = (bf16[2,512,768]{2,1,0:T(8,128)(2,1)S(1)}, bf16[2,512,256]{2,1,0:T(8,128)(2,1)S(1)}, f32[512,1024]{1,0:T(8,128)S(1)}, bf16[512,1024]{1,0:T(8,128)(2,1)S(1)}) custom-call(s32[7]{0:T(128)S(1)} %stack.27.refs_0_, bf16[2,2,256,512]{3,2,1,0:T(8,128)(2,1)} %bitcast.43.refs_1_, bf16[2,2,256,512]{3,2,1,0:T(8,128)(2,1)} %bitcast.45.refs_2_, ...), custom_call_target="tpu_custom_call" | custom-call | flops 4294967296 | bytes 12593152 | tf_op jit(solution)/shard_map/pallas_call | solution.py:88
  194.2 12.0 %shard_map.452 = (bf16[2,512,768]{2,1,0:T(8,128)(2,1)S(1)}, bf16[2,512,256]{2,1,0:T(8,128)(2,1)S(1)}, f32[512,1024]{1,0:T(8,128)S(1)}, bf16[512,1024]{1,0:T(8,128)(2,1)S(1)}) custom-call(s32[7]{0:T(128)S(1)} %stack.27.refs_0_, bf16[2,2,256,512]{3,2,1,0:T(8,128)(2,1)} %collective-permute-done.30.refs_1_, ...), custom_call_target="tpu_custom_call" | custom-call | flops 4294967296 | bytes 15738880 | tf_op jit(solution)/shard_map/pallas_call | solution.py:88
  214.4 9.4 %shard_map.453 = (bf16[2,1024,1024]{2,1,0:T(8,128)(2,1)S(1)}, bf16[512,1024]{1,0:T(8,128)(2,1)S(1)}, bf16[512,1024]{1,0:T(8,128)(2,1)S(1)}) custom-call(s32[7]{0:T(128)S(1)} %stack.27.refs_0_, bf16[1,1024,1024]{2,1,0:T(8,128)(2,1)S(1)} %collective-permute-done.35.refs_1_, bf16[1,1024,1024]{2,1,0:T(8,128)(2,1)S(1)} %collective-permute-done.36.refs_2_, ...), custom_call_target="tpu_custom_call" | custom-call | flops 6442450944 | bytes 12582912 | tf_op jit(solution)/shard_map/pallas_call | solution.py:88
  224.1 9.3 %shard_map.454 = (bf16[2,1024,1024]{2,1,0:T(8,128)(2,1)S(1)}, bf16[512,1024]{1,0:T(8,128)(2,1)S(1)}, bf16[512,1024]{1,0:T(8,128)(2,1)S(1)}) custom-call(s32[7]{0:T(128)S(1)} %stack.27.refs_0_, bf16[2,4,128,1024]{3,2,1,0:T(8,128)(2,1)S(1)} %collective-permute-done.38.refs_1_, bf16[2,4,128,1024]{3,2,1,0:T(8,128)(2,1)S(1)} %collective-permute-done.39.refs_2_, ...), custom_call_target="tpu_custom_call" | custom-call | flops 6442450944 | bytes 12582912 | tf_op jit(solution)/shard_map/pallas_call | solution.py:88
  233.8 13.3 %shard_map.455 = (bf16[2,4,128,1024]{3,2,1,0:T(8,128)(2,1)S(1)}, bf16[2,4,128,1024]{3,2,1,0:T(8,128)(2,1)}, bf16[512,1024]{1,0:T(8,128)(2,1)S(1)}, bf16[512,1024]{1,0:T(8,128)(2,1)S(1)}) custom-call(s32[7]{0:T(128)S(1)} %stack.27.refs_0_, bf16[1,1024,1024]{2,1,0:T(8,128)(2,1)} %bitcast.71.refs_1_, bf16[1,1024,1024]{2,1,0:T(8,128)(2,1)} %bitcast.73.refs_2_, ...), custom_call_target="tpu_custom_call" | custom-call | flops 6442450944 | bytes 16777216 | tf_op jit(solution)/shard_map/pallas_call | solution.py:88
  249.8 12.4 %shard_map.456 = (bf16[1024,1024]{1,0:T(8,128)(2,1)S(1)}, bf16[1024,1024]{1,0:T(8,128)(2,1)S(1)}, bf16[512,1024]{1,0:T(8,128)(2,1)S(1)}, bf16[512,1024]{1,0:T(8,128)(2,1)S(1)}) custom-call(s32[7]{0:T(128)S(1)} %stack.27.refs_0_, bf16[2,4,128,1024]{3,2,1,0:T(8,128)(2,1)} %bitcast.74.refs_1_, bf16[2,4,128,1024]{3,2,1,0:T(8,128)(2,1)} %bitcast.76.refs_2_, ...), custom_call_target="tpu_custom_call" | custom-call | flops 6442450944 | bytes 16777216 | tf_op jit(solution)/shard_map/pallas_call | solution.py:88
  266.0 17.2 %shard_map.458 = (bf16[2,1024,512]{2,1,0:T(8,128)(2,1)S(1)}, bf16[2,1024,512]{2,1,0:T(8,128)(2,1)S(1)}, f32[512,1024]{1,0:T(8,128)S(1)}) custom-call(s32[7]{0:T(128)S(1)} %stack.27.refs_0_, bf16[2,2,256,512]{3,2,1,0:T(8,128)(2,1)} %collective-permute-done.30.refs_1_, bf16[2,2,256,512]{3,2,1,0:T(8,128)(2,1)} %collective-permute-done.31.refs_2_, ...), custom_call_target="tpu_custom_call" | custom-call | flops 9663676416 | bytes 15730688 | tf_op jit(solution)/shard_map/pallas_call | solution.py:88
  283.9 11.1 %collective-permute-done.43 = bf16[1024,1024]{1,0:T(8,128)(2,1)S(1)} collective-permute-done((bf16[1024,1024]{1,0:T(8,128)(2,1)}, bf16[1024,1024]{1,0:T(8,128)(2,1)S(1)}, u32[]{:S(2)}, u32[]{:S(2)}) %collective-permute-start.43) | collective-permute-done | bytes 2097184 | tf_op jit(solution)/shard_map/ppermute | solution.py:39
  296.7 14.1 %collective-permute-done.42 = bf16[1024,1024]{1,0:T(8,128)(2,1)S(1)} collective-permute-done((bf16[1024,1024]{1,0:T(8,128)(2,1)S(1)}, bf16[1024,1024]{1,0:T(8,128)(2,1)S(1)}, u32[]{:S(2)}, u32[]{:S(2)}) %collective-permute-start.42) | collective-permute-done | bytes 2097184 | tf_op jit(solution)/shard_map/ppermute | solution.py:39
  315.0 19.2 %shard_map.461 = (bf16[2,1024,512]{2,1,0:T(8,128)(2,1)S(1)}, bf16[2,1024,512]{2,1,0:T(8,128)(2,1)S(1)}, f32[2,1024]{1,0:T(2,128)S(1)}, bf16[512,1024]{1,0:T(8,128)(2,1)S(1)}) custom-call(s32[7]{0:T(128)S(1)} %stack.27.refs_0_, bf16[2,2,256,512]{3,2,1,0:T(8,128)(2,1)} %bitcast.43.refs_1_, bf16[2,2,256,512]{3,2,1,0:T(8,128)(2,1)} %bitcast.45.refs_2_, ...), custom_call_target="tpu_custom_call" | custom-call | flops 9663676416 | bytes 20985856 | tf_op jit(solution)/shard_map/pallas_call | solution.py:88
  363.5 11.5 %collective-permute-done.52 = bf16[1024,512]{1,0:T(8,128)(2,1)} collective-permute-done((bf16[1024,512]{1,0:T(8,128)(2,1)}, bf16[1024,512]{1,0:T(8,128)(2,1)}, u32[]{:S(2)}, u32[]{:S(2)}) %collective-permute-start.52) | collective-permute-done | bytes 1048608 | tf_op jit(solution)/shard_map/ppermute | solution.py:39
  378.9 5.9 %collective-permute-done.63 = f32[2,1,2,2,2,128]{5,4,3,2,1,0:T(2,128)S(1)} collective-permute-done((f32[2,1,2,2,2,128]{5,4,3,2,1,0:T(2,128)S(1)}, f32[2,1,2,2,2,128]{5,4,3,2,1,0:T(2,128)S(1)}, u32[]{:S(2)}, u32[]{:S(2)}) %collective-permute-start.63) | collective-permute-done | bytes 8224 | tf_op jit(solution)/shard_map/ppermute | solution.py:39
  389.4 8.2 %collective-permute-done.60 = bf16[512,1024]{1,0:T(8,128)(2,1)S(1)} collective-permute-done((bf16[512,1024]{1,0:T(8,128)(2,1)S(1)}, bf16[512,1024]{1,0:T(8,128)(2,1)S(1)}, u32[]{:S(2)}, u32[]{:S(2)}) %collective-permute-start.60) | collective-permute-done | bytes 1048608 | tf_op jit(solution)/shard_map/ppermute | solution.py:39
  402.2 7.7 %collective-permute-done.59 = bf16[512,512]{1,0:T(8,128)(2,1)S(1)} collective-permute-done((bf16[512,512]{1,0:T(8,128)(2,1)S(1)}, bf16[512,512]{1,0:T(8,128)(2,1)S(1)}, u32[]{:S(2)}, u32[]{:S(2)}) %collective-permute-start.59) | collective-permute-done | bytes 524320 | tf_op jit(solution)/shard_map/ppermute | solution.py:39
  422.5 11.2 %collective-permute-done.68.refs_14_.refs_4_ = bf16[128,1024]{1,0:T(8,128)(2,1)S(1)} collective-permute-done((bf16[128,1024]{1,0:T(8,128)(2,1)S(1)}, bf16[128,1024]{1,0:T(8,128)(2,1)S(1)}, u32[]{:S(2)}, u32[]{:S(2)}) %collective-permute-start.68) | collective-permute-done | bytes 262176 | tf_op jit(solution)/shard_map/ppermute | solution.py:39
  433.7 5.0 %collective-permute-done.67.refs_13_.refs_2_ = bf16[128,1024]{1,0:T(8,128)(2,1)S(1)} collective-permute-done((bf16[128,1024]{1,0:T(8,128)(2,1)S(1)}, bf16[128,1024]{1,0:T(8,128)(2,1)S(1)}, u32[]{:S(2)}, u32[]{:S(2)}) %collective-permute-start.67) | collective-permute-done | bytes 262176 | tf_op jit(solution)/shard_map/ppermute | solution.py:39
  438.8 6.5 %shard_map.470 = (f32[512,1024]{1,0:T(8,128)}, f32[512,1024]{1,0:T(8,128)}, bf16[512,1024]{1,0:T(8,128)(2,1)}) custom-call(s32[7]{0:T(128)S(1)} %stack.27.refs_0_, bf16[128,1024]{1,0:T(8,128)(2,1)S(1)} %get-tuple-element.441.refs_1_, bf16[128,1024]{1,0:T(8,128)(2,1)S(1)} %collective-permute-done.44.refs_2_.refs_15_, ...), custom_call_target="tpu_custom_call" | custom-call | flops 2147483648 | bytes 11534336 | tf_op jit(solution)/shard_map/pallas_call | solution.py:88
  480.8 5.8 %collective-permute-done.80.refs_2_ = bf16[64,1024]{1,0:T(8,128)(2,1)S(1)} collective-permute-done((bf16[64,1024]{1,0:T(8,128)(2,1)S(1)}, bf16[64,1024]{1,0:T(8,128)(2,1)S(1)}, u32[]{:S(2)}, u32[]{:S(2)}) %collective-permute-start.80) | collective-permute-done | bytes 131104 | tf_op jit(solution)/shard_map/ppermute | solution.py:39
  (435 shorter events, 220.5 us)
Async XLA Ops:
  43.8 28.2 %collective-permute-start.15 = (bf16[128,3072]{1,0:T(8,128)(2,1)S(1)}, bf16[128,3072]{1,0:T(8,128)(2,1)S(1)}, u32[]{:S(2)}, u32[]{:S(2)}) collective-permute-start(bf16[128,3072]{1,0:T(8,128)(2,1)S(1)} %get-tuple-element.193), channel_id=1, source_target_pairs={{0,2},{1,3},{2,0},{3,1},{4,6},{5,7},{6,4},{7,5},{8,10},{9,11},{10,... | collective-permute-start | bytes 2359304 | tf_op jit(solution)/shard_map/ppermute | solution.py:39
  76.6 49.6 %collective-permute-start.26 = (bf16[512,1024]{1,0:T(8,128)(2,1)S(1)}, bf16[512,1024]{1,0:T(8,128)(2,1)S(1)}, u32[]{:S(2)}, u32[]{:S(2)}) collective-permute-start(bf16[512,1024]{1,0:T(8,128)(2,1)S(1)} %bitcast.192), channel_id=1, source_target_pairs={{0,4},{4,0},{8,12},{12,8},{16,20},{20,16},{24,28},{28,24},{1,5},{5... | collective-permute-start | bytes 3145736 | tf_op jit(solution)/shard_map/ppermute | solution.py:39
  78.2 46.0 %collective-permute-start.22 = (bf16[128,3072]{1,0:T(8,128)(2,1)S(1)}, bf16[128,3072]{1,0:T(8,128)(2,1)S(1)}, u32[]{:S(2)}, u32[]{:S(2)}) collective-permute-start(bf16[128,3072]{1,0:T(8,128)(2,1)S(1)} %get-tuple-element.199.refs_3_), channel_id=1, source_target_pairs={{0,3},{1,2},{2,1},{3,0},{4,7},{5,6},{6,5},{7,4},{8,11},{9,10},{10,... | collective-permute-start | bytes 2359304 | tf_op jit(solution)/shard_map/ppermute | solution.py:39
  78.9 35.0 %collective-permute-start.18 = (bf16[256,1024]{1,0:T(8,128)(2,1)S(1)}, bf16[256,1024]{1,0:T(8,128)(2,1)S(1)}, u32[]{:S(2)}, u32[]{:S(2)}) collective-permute-start(bf16[256,1024]{1,0:T(8,128)(2,1)S(1)} %bitcast.239), channel_id=1, source_target_pairs={{0,4},{4,0},{8,12},{12,8},{16,20},{20,16},{24,28},{28,24},{1,5},{5... | collective-permute-start | bytes 1572872 | tf_op jit(solution)/shard_map/ppermute | solution.py:39
  79.4 36.6 %collective-permute-start.17 = (bf16[512,512]{1,0:T(8,128)(2,1)S(1)}, bf16[512,512]{1,0:T(8,128)(2,1)S(1)}, u32[]{:S(2)}, u32[]{:S(2)}) collective-permute-start(bf16[512,512]{1,0:T(8,128)(2,1)S(1)} %bitcast.211), channel_id=1, source_target_pairs={{0,8},{4,12},{8,0},{12,4},{16,24},{20,28},{24,16},{28,20},{1,9},{5... | collective-permute-start | bytes 1572872 | tf_op jit(solution)/shard_map/ppermute | solution.py:39
  87.5 36.7 %collective-permute-start.16 = (bf16[512,512]{1,0:T(8,128)(2,1)S(1)}, bf16[512,512]{1,0:T(8,128)(2,1)S(1)}, u32[]{:S(2)}, u32[]{:S(2)}) collective-permute-start(bf16[512,512]{1,0:T(8,128)(2,1)S(1)} %bitcast.230), channel_id=1, source_target_pairs={{0,4},{4,0},{8,12},{12,8},{16,20},{20,16},{24,28},{28,24},{1,5},{5... | collective-permute-start | bytes 1572872 | tf_op jit(solution)/shard_map/ppermute | solution.py:39
  129.8 32.6 %collective-permute-start.24 = (bf16[1024,512]{1,0:T(8,128)(2,1)}, bf16[1024,512]{1,0:T(8,128)(2,1)}, u32[]{:S(2)}, u32[]{:S(2)}) collective-permute-start(bf16[1024,512]{1,0:T(8,128)(2,1)} %bitcast.47), channel_id=1, source_target_pairs={{0,4},{4,0},{8,12},{12,8},{16,20},{20,16},{24,28},{28,24},{1,5},{5... | collective-permute-start | bytes 3145736 | tf_op jit(solution)/shard_map/ppermute | solution.py:39
  132.0 44.5 %collective-permute-start.23 = (bf16[1024,512]{1,0:T(8,128)(2,1)}, bf16[1024,512]{1,0:T(8,128)(2,1)}, u32[]{:S(2)}, u32[]{:S(2)}) collective-permute-start(bf16[1024,512]{1,0:T(8,128)(2,1)} %bitcast.44), channel_id=1, source_target_pairs={{0,8},{4,12},{8,0},{12,4},{16,24},{20,28},{24,16},{28,20},{1,9},{5... | collective-permute-start | bytes 3145736 | tf_op jit(solution)/shard_map/ppermute | solution.py:39
  133.4 43.1 %collective-permute-start.32 = (bf16[2,4,128,512]{3,2,1,0:T(8,128)(2,1)}, bf16[2,4,128,512]{3,2,1,0:T(8,128)(2,1)}, u32[]{:S(2)}, u32[]{:S(2)}) collective-permute-start(bf16[2,4,128,512]{3,2,1,0:T(8,128)(2,1)} %bitcast.46.refs_3_), channel_id=1, source_target_pairs={{0,1},{1,0},{2,3},{3,2},{4,5},{5,4},{6,7},{7,6},{8,9},{9,8},{10,11... | collective-permute-start | bytes 3145736 | tf_op jit(solution)/shard_map/ppermute | solution.py:39
  160.1 46.9 %collective-permute-start.34 = (bf16[1024,1024]{1,0:T(8,128)(2,1)}, bf16[1024,1024]{1,0:T(8,128)(2,1)}, u32[]{:S(2)}, u32[]{:S(2)}) collective-permute-start(bf16[1024,1024]{1,0:T(8,128)(2,1)} %bitcast.72), channel_id=1, source_target_pairs={{0,2},{1,3},{2,0},{3,1},{4,6},{5,7},{6,4},{7,5},{8,10},{9,11},{10,... | collective-permute-start | bytes 6291464 | tf_op jit(solution)/shard_map/ppermute | solution.py:39
  160.8 46.8 %collective-permute-start.37 = (bf16[1024,1024]{1,0:T(8,128)(2,1)}, bf16[1024,1024]{1,0:T(8,128)(2,1)}, u32[]{:S(2)}, u32[]{:S(2)}) collective-permute-start(bf16[1024,1024]{1,0:T(8,128)(2,1)} %bitcast.75), channel_id=1, source_target_pairs={{0,4},{4,0},{8,12},{12,8},{16,20},{20,16},{24,28},{28,24},{1,5},{5... | collective-permute-start | bytes 6291464 | tf_op jit(solution)/shard_map/ppermute | solution.py:39
  162.4 31.8 %collective-permute-start.30 = (bf16[2,2,256,512]{3,2,1,0:T(8,128)(2,1)}, bf16[2,2,256,512]{3,2,1,0:T(8,128)(2,1)}, u32[]{:S(2)}, u32[]{:S(2)}) collective-permute-start(bf16[2,2,256,512]{3,2,1,0:T(8,128)(2,1)} %bitcast.43.refs_1_), channel_id=1, source_target_pairs={{0,1},{1,0},{2,3},{3,2},{4,5},{5,4},{6,7},{7,6},{8,9},{9,8},{10,11... | collective-permute-start | bytes 3145736 | tf_op jit(solution)/shard_map/ppermute | solution.py:39
  247.1 47.9 %collective-permute-start.43 = (bf16[1024,1024]{1,0:T(8,128)(2,1)}, bf16[1024,1024]{1,0:T(8,128)(2,1)S(1)}, u32[]{:S(2)}, u32[]{:S(2)}) collective-permute-start(bf16[1024,1024]{1,0:T(8,128)(2,1)} %bitcast.80), channel_id=1, source_target_pairs={{0,4},{4,0},{8,12},{12,8},{16,20},{20,16},{24,28},{28,24},{1,5},{5... | collective-permute-start | bytes 6291464 | tf_op jit(solution)/shard_map/ppermute | solution.py:39
  262.2 48.6 %collective-permute-start.42 = (bf16[1024,1024]{1,0:T(8,128)(2,1)S(1)}, bf16[1024,1024]{1,0:T(8,128)(2,1)S(1)}, u32[]{:S(2)}, u32[]{:S(2)}) collective-permute-start(bf16[1024,1024]{1,0:T(8,128)(2,1)S(1)} %get-tuple-element.236), channel_id=1, source_target_pairs={{0,2},{1,3},{2,0},{3,1},{4,6},{5,7},{6,4},{7,5},{8,10},{9,11},{10,... | collective-permute-start | bytes 6291464 | tf_op jit(solution)/shard_map/ppermute | solution.py:39
  283.3 29.8 %collective-permute-start.50 = (bf16[2,1024,512]{2,1,0:T(8,128)(2,1)S(1)}, bf16[2,1024,512]{2,1,0:T(8,128)(2,1)S(1)}, u32[]{:S(2)}, u32[]{:S(2)}) collective-permute-start(bf16[2,1024,512]{2,1,0:T(8,128)(2,1)S(1)} %get-tuple-element.244), channel_id=1, source_target_pairs={{0,1},{1,0},{2,3},{3,2},{4,5},{5,4},{6,7},{7,6},{8,9},{9,8},{10,11... | collective-permute-start | bytes 6291464 | tf_op jit(solution)/shard_map/ppermute | solution.py:39
  283.4 30.4 %collective-permute-start.51 = (bf16[2,1024,512]{2,1,0:T(8,128)(2,1)S(1)}, bf16[2,1024,512]{2,1,0:T(8,128)(2,1)S(1)}, u32[]{:S(2)}, u32[]{:S(2)}) collective-permute-start(bf16[2,1024,512]{2,1,0:T(8,128)(2,1)S(1)} %get-tuple-element.246), channel_id=1, source_target_pairs={{0,1},{1,0},{2,3},{3,2},{4,5},{5,4},{6,7},{7,6},{8,9},{9,8},{10,11... | collective-permute-start | bytes 6291464 | tf_op jit(solution)/shard_map/ppermute | solution.py:39
  296.0 41.8 %collective-permute-start.54 = (bf16[512,1024]{1,0:T(8,128)(2,1)S(1)}, bf16[512,1024]{1,0:T(8,128)(2,1)S(1)}, u32[]{:S(2)}, u32[]{:S(2)}) collective-permute-start(bf16[512,1024]{1,0:T(8,128)(2,1)S(1)} %bitcast.278), channel_id=1, source_target_pairs={{0,2},{1,3},{2,0},{3,1},{4,6},{5,7},{6,4},{7,5},{8,10},{9,11},{10,... | collective-permute-start | bytes 3145736 | tf_op jit(solution)/shard_map/ppermute | solution.py:39
  313.1 27.5 %collective-permute-start.49 = (bf16[128,1024]{1,0:T(8,128)(2,1)S(1)}, bf16[128,1024]{1,0:T(8,128)(2,1)S(1)}, u32[]{:S(2)}, u32[]{:S(2)}) collective-permute-start(bf16[128,1024]{1,0:T(8,128)(2,1)S(1)} %get-tuple-element.434), channel_id=1, source_target_pairs={{0,3},{1,2},{2,1},{3,0},{4,7},{5,6},{6,5},{7,4},{8,11},{9,10},{10,... | collective-permute-start | bytes 786440 | tf_op jit(solution)/shard_map/ppermute | solution.py:39
  313.1 30.2 %collective-permute-start.48 = (bf16[128,1024]{1,0:T(8,128)(2,1)S(1)}, bf16[128,1024]{1,0:T(8,128)(2,1)S(1)}, u32[]{:S(2)}, u32[]{:S(2)}) collective-permute-start(bf16[128,1024]{1,0:T(8,128)(2,1)S(1)} %get-tuple-element.435), channel_id=1, source_target_pairs={{0,2},{1,3},{2,0},{3,1},{4,6},{5,7},{6,4},{7,5},{8,10},{9,11},{10,... | collective-permute-start | bytes 786440 | tf_op jit(solution)/shard_map/ppermute | solution.py:39
  313.8 29.6 %collective-permute-start.47 = (bf16[128,1024]{1,0:T(8,128)(2,1)S(1)}, bf16[128,1024]{1,0:T(8,128)(2,1)S(1)}, u32[]{:S(2)}, u32[]{:S(2)}) collective-permute-start(bf16[128,1024]{1,0:T(8,128)(2,1)S(1)} %get-tuple-element.436), channel_id=1, source_target_pairs={{0,1},{1,0},{2,3},{3,2},{4,5},{5,4},{6,7},{7,6},{8,9},{9,8},{10,11... | collective-permute-start | bytes 786440 | tf_op jit(solution)/shard_map/ppermute | solution.py:39
  358.0 39.6 %collective-permute-start.60 = (bf16[512,1024]{1,0:T(8,128)(2,1)S(1)}, bf16[512,1024]{1,0:T(8,128)(2,1)S(1)}, u32[]{:S(2)}, u32[]{:S(2)}) collective-permute-start(bf16[512,1024]{1,0:T(8,128)(2,1)S(1)} %bitcast.277), channel_id=1, source_target_pairs={{0,2},{1,3},{2,0},{3,1},{4,6},{5,7},{6,4},{7,5},{8,10},{9,11},{10,... | collective-permute-start | bytes 3145736 | tf_op jit(solution)/shard_map/ppermute | solution.py:39
  415.4 29.9 %collective-permute-start.69 = (bf16[256,1024]{1,0:T(8,128)(2,1)S(1)}, bf16[256,1024]{1,0:T(8,128)(2,1)S(1)}, u32[]{:S(2)}, u32[]{:S(2)}) collective-permute-start(bf16[256,1024]{1,0:T(8,128)(2,1)S(1)} %bitcast.282), channel_id=1, source_target_pairs={{0,4},{4,0},{8,12},{12,8},{16,20},{20,16},{24,28},{28,24},{1,5},{5... | collective-permute-start | bytes 1572872 | tf_op jit(solution)/shard_map/ppermute | solution.py:39
  419.4 30.0 %collective-permute-start.71 = (bf16[256,512]{1,0:T(8,128)(2,1)S(1)}, bf16[256,512]{1,0:T(8,128)(2,1)S(1)}, u32[]{:S(2)}, u32[]{:S(2)}) collective-permute-start(bf16[256,512]{1,0:T(8,128)(2,1)S(1)} %bitcast.288), channel_id=1, source_target_pairs={{0,2},{1,3},{2,0},{3,1},{4,6},{5,7},{6,4},{7,5},{8,10},{9,11},{10,... | collective-permute-start | bytes 786440 | tf_op jit(solution)/shard_map/ppermute | solution.py:39
  420.9 28.5 %collective-permute-start.72 = (bf16[256,512]{1,0:T(8,128)(2,1)S(1)}, bf16[256,512]{1,0:T(8,128)(2,1)S(1)}, u32[]{:S(2)}, u32[]{:S(2)}) collective-permute-start(bf16[256,512]{1,0:T(8,128)(2,1)S(1)} %bitcast.287), channel_id=1, source_target_pairs={{0,4},{4,0},{8,12},{12,8},{16,20},{20,16},{24,28},{28,24},{1,5},{5... | collective-permute-start | bytes 786440 | tf_op jit(solution)/shard_map/ppermute | solution.py:39
  (143 other events, 1595.6 us)

commit v4 on v3

--- a/solution.py
+++ b/solution.py
@@ -310,17 +310,22 @@
     return values.reshape(shape)
 
 
-def exchange_steps(line, values):
+def exchange_steps(line, values, needed=False):
     shape = values.shape
     dims = [("dp", mask) for mask in bits_of("dp")]
     dims += [(TENSOR, mask) for mask in bits_of(TENSOR)]
     values = values.reshape((2,) * len(dims) + shape[2:])
-    for dim, (axis, mask) in enumerate(dims):
+    turns = list(range(len(dims)))
+    if not needed:
+        turns = turns[-1:] + turns[-3:-1][::-1] + turns[:-3]
+        turns = turns[:1] + turns[2:] + turns[1:2]
+    for dim, (axis, mask) in [(dim, dims[dim]) for dim in turns]:
         values = line.tie(values)
         kept = lax.slice_in_dim(values, 0, 1, axis=dim)
         arrived = swap(lax.slice_in_dim(values, 1, 2, axis=dim), axis, mask)
         values = jnp.concatenate([kept, arrived], axis=dim)
-        line.need(values)
+        if needed:
+            line.need(values)
         yield None
     yield values.reshape(shape)
 
@@ -862,9 +867,9 @@
     heads = inner // HEAD_DIM
     highest = lax.Precision.HIGHEST
     order = orders()
-    skip_order, skip_back_order = order["xzy"], order["zyx"]
-    attention_orders, attention_back_orders = (order["xyz"], order["xzy"]), (order["xzy"], order["yzx"])
-    feed_orders, feed_back_orders = (order["yzx"], order["zxy"]), (order["zxy"], order["zyx"])
+    skip_order, skip_back_order = order["xyz"], order["yzx"]
+    attention_orders, attention_back_orders = (order["xyz"], order["xzy"]), (order["xyz"], order["zxy"])
+    feed_orders, feed_back_orders = (order["yzx"], order["zxy"]), (order["zxy"], order["xyz"])
     core = (TENSOR, bits_of(TENSOR)[-1])
     across = (TENSOR, bits_of(TENSOR)[0])
     dims = [across] + [("dp", mask) for mask in bits_of("dp")]
@@ -876,15 +881,16 @@
     time_low = jax.nn.silu(time_values).astype(low)
 
     def modulation():
-        time_all = unflip(time_low, 0, TENSOR)[None]
-        for mask in reversed(bits_of("dp")):
+        dp_bits = bits_of("dp")
+        time_all = unflip(time_low, 0, TENSOR).reshape((1,) * len(dp_bits) + time_low.shape)
+        for dim, mask in enumerate(dp_bits):
             time_all = line.tie(time_all)
-            time_all = jnp.concatenate([time_all, swap(time_all, "dp", mask)], axis=0)
+            time_all = jnp.concatenate([time_all, swap(time_all, "dp", mask)], axis=dim)
             line.need(time_all)
             yield None
         time_rows = time_all.reshape(groups * micro, width)
         adapt_mine = jnp.dot(time_rows, adapt_low, preferred_element_type=f32).reshape(groups, micro, -1)
-        for adapt_all in exchange_steps(line, adapt_mine):
+        for adapt_all in exchange_steps(line, adapt_mine, needed=True):
             yield time_rows, adapt_all
 
     modulate = modulation()
@@ -911,7 +917,6 @@
     ]
     next(modulate)
     blocks = list(cut(line, (frames, skip_frames, out_grad)))
-    blocks[2] = swap(blocks[2], TENSOR, 2)
     feed_walks = [
         Gather(line, shard, each_order, dims, (across,))
         for shard, each_order in zip(feed_shards, feed_orders)
@@ -922,26 +927,28 @@
         go(line, skip_walk)
         go(line, *attention_walks)
         go(line, *feed_walks)
+    line.need(cosine, sine, keep)
+    go(line, skip_walk)
+    next(modulate)
+    go(line, *attention_walks)
+    blocks[2] = swap(line.tie(blocks[2]), TENSOR, 2)
+    next(modulate)
     go(line, skip_walk)
     next(modulate)
     go(line, *attention_walks)
     next(modulate)
-    go(line, skip_walk)
-    next(modulate)
     go(line, *feed_walks)
-    next(modulate)
-    line.need(blocks[2])
-    blocks[3] = swap(line.tie(blocks[3]), TENSOR, 3)
-    go(line, *attention_walks)
     for time_rows, adapt_all in modulate:
         pass
+    blocks[3] = swap(line.tie(blocks[3]), TENSOR, 3)
     go(line, skip_walk)
+    go(line, *feed_walks)
     adapt_vector = unflip(unflip(adapt_all, 0, "dp"), 1, TENSOR).reshape(1, -1)
     shift_one, scale_one, shift_two, scale_two = jnp.split(adapt_vector, 4, axis=1)
-    go(line, *feed_walks)
+    line.need(blocks[2])
+    go(line, *attention_walks)
+    blocks[1] = swap(line.tie(blocks[1]), TENSOR, 1)
     line.need(blocks[3])
-    blocks[1] = swap(line.tie(blocks[1]), TENSOR, 1)
-    go(line, *attention_walks)
     go(line, skip_walk)
     skip_pair = skip_walk.pair()
     hidden, outer = enter(line, blocks, skip_pair, line.place[core], keep)
@@ -985,8 +992,7 @@
         [Halves(line, width, 2 * inner)] * 2,
     )
     attention_arrived = [swap(grad, *core) for grad in (qk_other, vo_other)]
-    go(line, feed_one)
-    go(line, feed_two)
+    line.need(*results[1:])
     qk_grad, vo_grad, sums_one, hidden_low = attend_back(
         line,
         normed_one,
@@ -1004,9 +1010,7 @@
         Scatter(line, grad, None, [core] + each_order[::-1], dims, (across,), arrived)
         for grad, arrived, each_order in zip((qk_grad, vo_grad), attention_arrived, attention_back_orders)
     ]
-    go(line, *attention_scatters)
     go(line, feed_one, feed_two)
-    line.need(*results[1:])
     skip_sent, skip_kept = leave(line, blocks, hidden_low, line.place[core], groups * parts)
     skip_scatter = Scatter(line, skip_kept, skip_sent, [core] + skip_back_order[::-1], all_dims, ())
     hidden_back = from_owner([hidden_low[step * rows : (step + 1) * rows] for step in range(parts)])
@@ -1036,28 +1040,28 @@
         yield adapt_sum, time_part
 
     modulate_back = modulation_back()
+    go(line, *attention_scatters)
     go(line, skip_scatter)
+    next(modulate_back)
+    go(line, feed_one, feed_two)
     next(modulate_back)
     go(line, *attention_scatters)
     next(modulate_back)
+    go(line, skip_scatter)
+    next(modulate_back)
     go(line, feed_one, feed_two)
+    next(modulate_back)
+    go(line, *attention_scatters)
     next(modulate_back)
     go(line, skip_scatter)
     next(modulate_back)
     go(line, *attention_scatters)
+    go(line, skip_scatter)
     next(modulate_back)
-    line.need(feed_one.terms[1], feed_two.terms[1])
-    line.need(*hidden_back[1:])
     frame_grads, skip_grads, results = inputs_back(
         line, hidden_back, results, skip_pair, line.place[core]
     )
     frame_grads, skip_grads = frame_grads.reshape(frames.shape), skip_grads.reshape(frames.shape)
-    next(modulate_back)
-    go(line, skip_scatter)
-    next(modulate_back)
-    go(line, *attention_scatters)
-    next(modulate_back)
-    go(line, skip_scatter)
     for _ in more:
         go(line, feed_one, feed_two)
         go(line, *attention_scatters)

time: 497 us -> 461 us (0.928)
  waiting for transfers between devices: 213 us -> 157 us
  local copies, waits for them, and re-layouts: 40.7 us -> 48.9 us
  Pallas kernels: 160 us -> 166 us
    ppermute x81, waiting for transfers between devices: 213 us -> 157 us  [swap(): return lax.ppermute(values, axis, [(i, i ^ mask) for i in range(count)])]
    unnamed x175 -> x197, local copies, waits for them, and re-layouts: 31 us -> 42.6 us
    pallas_call x39 -> x38, Pallas kernels: 160 us -> 166 us  [run(): pl.pallas_call(inner, grid_spec=pltpu.PrefetchScalarGridSpec(num_scalar_p...]
  transfers between devices with their start and end apart: 81 -> 81, of which waited for: 38 -> 36; matrix products, arithmetic and copies ran while one was open for 3% -> 2% of each run, Pallas kernels for 31% -> 36%
where the time goes in v4:
time: 461 us; the launch traced here: 454 us
  Pallas kernels  166 us (36%)
  waiting for transfers between devices  157 us (34%)
  starting transfers between devices  72.6 us (16%)
  local copies, waits for them, and re-layouts  48.9 us (11%)
  matrix products  4.82 us (1%)
    pallas_call x38, Pallas kernels, run(): pl.pallas_call(inner, grid_spec=pltpu.PrefetchScalarGridSpec(num_scalar_p...  166 us
    ppermute x81, waiting for transfers between devices, swap(): return lax.ppermute(values, axis, [(i, i ^ mask) for i in range(count)])  157 us
    ppermute x81, starting transfers between devices, swap(): return lax.ppermute(values, axis, [(i, i ^ mask) for i in range(count)])  72.6 us
    unnamed x197, local copies, waits for them, and re-layouts  42.6 us
  transfers between devices with their start and end apart: 81, of which 36 were waited for; matrix products, arithmetic and copies ran while one was open for 2% of the time, Pallas kernels for 36%

profile of v4, /device:TPU:0, one launch (start us, length us, event | category | flops | bytes accessed | tf_op | source)
XLA Modules:
  0.0 454.0 jit_solution(4657437201961986145)
XLA Ops:
  56.5 5.9 %collective-permute-done.14 = bf16[128,1024]{1,0:T(8,128)(2,1)S(1)} collective-permute-done((bf16[128,1024]{1,0:T(8,128)(2,1)S(1)}, bf16[128,1024]{1,0:T(8,128)(2,1)S(1)}, u32[]{:S(2)}, u32[]{:S(2)}) %collective-permute-start.14) | collective-permute-done | bytes 262176 | tf_op jit(solution)/shard_map/ppermute | solution.py:39
  62.3 5.5 %collective-permute-done.15 = bf16[128,1024]{1,0:T(8,128)(2,1)S(1)} collective-permute-done((bf16[128,1024]{1,0:T(8,128)(2,1)S(1)}, bf16[128,1024]{1,0:T(8,128)(2,1)S(1)}, u32[]{:S(2)}, u32[]{:S(2)}) %collective-permute-start.15) | collective-permute-done | bytes 262176 | tf_op jit(solution)/shard_map/ppermute | solution.py:39
  73.3 10.0 %collective-permute-done.18 = bf16[256,1024]{1,0:T(8,128)(2,1)S(1)} collective-permute-done((bf16[256,1024]{1,0:T(8,128)(2,1)S(1)}, bf16[256,1024]{1,0:T(8,128)(2,1)S(1)}, u32[]{:S(2)}, u32[]{:S(2)}) %collective-permute-start.18) | collective-permute-done | bytes 524320 | tf_op jit(solution)/shard_map/ppermute | solution.py:39
  85.9 30.7 %collective-permute-done.13 = bf16[512,512]{1,0:T(8,128)(2,1)S(1)} collective-permute-done((bf16[512,512]{1,0:T(8,128)(2,1)S(1)}, bf16[512,512]{1,0:T(8,128)(2,1)S(1)}, u32[]{:S(2)}, u32[]{:S(2)}) %collective-permute-start.13) | collective-permute-done | bytes 524320 | tf_op jit(solution)/shard_map/ppermute | solution.py:39
  137.9 8.0 %collective-permute-done.29 = bf16[512,1024]{1,0:T(8,128)(2,1)} collective-permute-done((bf16[512,1024]{1,0:T(8,128)(2,1)}, bf16[512,1024]{1,0:T(8,128)(2,1)}, u32[]{:S(2)}, u32[]{:S(2)}) %collective-permute-start.29) | collective-permute-done | bytes 1048608 | tf_op jit(solution)/shard_map/ppermute | solution.py:39
  147.8 4.9 %shard_map.450 = (bf16[2,2,256,1024]{3,2,1,0:T(8,128)(2,1)}, bf16[1,2,512,1024]{3,2,1,0:T(8,128)(2,1)}) custom-call(s32[7]{0:T(128)S(1)} %stack.27.refs_0_, bf16[2,256,1024]{2,1,0:T(8,128)(2,1)} %bitcast.65.refs_1_, bf16[2,256,1024]{2,1,0:T(8,128)(2,1)} %bitcast.67.refs_2_, bf16[1,512,1024]{2,1,0:T(8,128)(2,1)} %bitcast.68.refs_3_, ...), custom_call_target="tpu_custom_call" | custom-call | bytes 8388608 | tf_op jit(solution)/shard_map/pallas_call | solution.py:88
  153.9 15.7 %collective-permute-done.22 = bf16[1024,512]{1,0:T(8,128)(2,1)} collective-permute-done((bf16[1024,512]{1,0:T(8,128)(2,1)}, bf16[1024,512]{1,0:T(8,128)(2,1)}, u32[]{:S(2)}, u32[]{:S(2)}) %collective-permute-start.22) | collective-permute-done | bytes 1048608 | tf_op jit(solution)/shard_map/ppermute | solution.py:39
  173.9 12.4 %shard_map.451 = (bf16[2,512,768]{2,1,0:T(8,128)(2,1)S(1)}, bf16[2,512,256]{2,1,0:T(8,128)(2,1)S(1)}, f32[512,1024]{1,0:T(8,128)S(1)}, bf16[512,1024]{1,0:T(8,128)(2,1)S(1)}) custom-call(s32[7]{0:T(128)S(1)} %stack.27.refs_0_, bf16[2,2,256,512]{3,2,1,0:T(8,128)(2,1)} %bitcast.50.refs_1_, bf16[2,2,256,512]{3,2,1,0:T(8,128)(2,1)} %bitcast.52.refs_2_, ...), custom_call_target="tpu_custom_call" | custom-call | flops 4294967296 | bytes 12593152 | tf_op jit(solution)/shard_map/pallas_call | solution.py:88
  186.3 12.1 %shard_map.452 = (bf16[2,512,768]{2,1,0:T(8,128)(2,1)S(1)}, bf16[2,512,256]{2,1,0:T(8,128)(2,1)S(1)}, f32[512,1024]{1,0:T(8,128)S(1)}, bf16[512,1024]{1,0:T(8,128)(2,1)S(1)}) custom-call(s32[7]{0:T(128)S(1)} %stack.27.refs_0_, bf16[2,2,256,512]{3,2,1,0:T(8,128)(2,1)} %collective-permute-done.30.refs_1_, ...), custom_call_target="tpu_custom_call" | custom-call | flops 4294967296 | bytes 15738880 | tf_op jit(solution)/shard_map/pallas_call | solution.py:88
  206.7 9.4 %shard_map.453 = (bf16[2,1024,1024]{2,1,0:T(8,128)(2,1)S(1)}, bf16[512,1024]{1,0:T(8,128)(2,1)S(1)}, bf16[512,1024]{1,0:T(8,128)(2,1)S(1)}) custom-call(s32[7]{0:T(128)S(1)} %stack.27.refs_0_, bf16[1,1024,1024]{2,1,0:T(8,128)(2,1)S(1)} %collective-permute-done.35.refs_1_, bf16[1,1024,1024]{2,1,0:T(8,128)(2,1)S(1)} %collective-permute-done.36.refs_2_, ...), custom_call_target="tpu_custom_call" | custom-call | flops 6442450944 | bytes 12582912 | tf_op jit(solution)/shard_map/pallas_call | solution.py:88
  216.3 9.2 %shard_map.454 = (bf16[2,1024,1024]{2,1,0:T(8,128)(2,1)S(1)}, bf16[512,1024]{1,0:T(8,128)(2,1)S(1)}, bf16[512,1024]{1,0:T(8,128)(2,1)S(1)}) custom-call(s32[7]{0:T(128)S(1)} %stack.27.refs_0_, bf16[2,4,128,1024]{3,2,1,0:T(8,128)(2,1)S(1)} %collective-permute-done.38.refs_1_, bf16[2,4,128,1024]{3,2,1,0:T(8,128)(2,1)S(1)} %collective-permute-done.39.refs_2_, ...), custom_call_target="tpu_custom_call" | custom-call | flops 6442450944 | bytes 12582912 | tf_op jit(solution)/shard_map/pallas_call | solution.py:88
  226.0 13.1 %shard_map.455 = (bf16[2,4,128,1024]{3,2,1,0:T(8,128)(2,1)S(1)}, bf16[2,4,128,1024]{3,2,1,0:T(8,128)(2,1)}, bf16[512,1024]{1,0:T(8,128)(2,1)S(1)}, bf16[512,1024]{1,0:T(8,128)(2,1)S(1)}) custom-call(s32[7]{0:T(128)S(1)} %stack.27.refs_0_, bf16[1,1024,1024]{2,1,0:T(8,128)(2,1)} %bitcast.71.refs_1_, bf16[1,1024,1024]{2,1,0:T(8,128)(2,1)} %bitcast.73.refs_2_, ...), custom_call_target="tpu_custom_call" | custom-call | flops 6442450944 | bytes 16777216 | tf_op jit(solution)/shard_map/pallas_call | solution.py:88
  239.5 13.0 %shard_map.456 = (bf16[2,2,256,1024]{3,2,1,0:T(8,128)(2,1)S(1)}, bf16[2,2,256,1024]{3,2,1,0:T(8,128)(2,1)}, bf16[512,1024]{1,0:T(8,128)(2,1)S(1)}, bf16[512,1024]{1,0:T(8,128)(2,1)S(1)}) custom-call(s32[7]{0:T(128)S(1)} %stack.27.refs_0_, bf16[2,4,128,1024]{3,2,1,0:T(8,128)(2,1)} %bitcast.74.refs_1_, bf16[2,4,128,1024]{3,2,1,0:T(8,128)(2,1)} %bitcast.76.refs_2_, ...), custom_call_target="tpu_custom_call" | custom-call | flops 6442450944 | bytes 16777216 | tf_op jit(solution)/shard_map/pallas_call | solution.py:88
  258.6 19.3 %shard_map.458 = (bf16[2,1024,512]{2,1,0:T(8,128)(2,1)}, bf16[2,1024,512]{2,1,0:T(8,128)(2,1)}, f32[512,1024]{1,0:T(8,128)S(1)}) custom-call(s32[7]{0:T(128)S(1)} %stack.27.refs_0_, bf16[2,2,256,512]{3,2,1,0:T(8,128)(2,1)} %collective-permute-done.30.refs_1_, bf16[2,2,256,512]{3,2,1,0:T(8,128)(2,1)} %collective-permute-done.31.refs_2_, ...), custom_call_target="tpu_custom_call" | custom-call | flops 9663676416 | bytes 15730688 | tf_op jit(solution)/shard_map/pallas_call | solution.py:88
  281.4 19.3 %shard_map.459 = (bf16[2,1024,512]{2,1,0:T(8,128)(2,1)S(1)}, bf16[2,1024,512]{2,1,0:T(8,128)(2,1)S(1)}, f32[2,1024]{1,0:T(2,128)S(1)}, bf16[512,1024]{1,0:T(8,128)(2,1)S(1)}) custom-call(s32[7]{0:T(128)S(1)} %stack.27.refs_0_, bf16[2,2,256,512]{3,2,1,0:T(8,128)(2,1)} %bitcast.50.refs_1_, bf16[2,2,256,512]{3,2,1,0:T(8,128)(2,1)} %bitcast.52.refs_2_, ...), custom_call_target="tpu_custom_call" | custom-call | flops 9663676416 | bytes 20985856 | tf_op jit(solution)/shard_map/pallas_call | solution.py:88
  305.9 4.3 shard_map.461
  318.8 5.0 %shard_map.462 = (bf16[4,256,512]{2,1,0:T(8,128)(2,1)}, bf16[4,256,512]{2,1,0:T(8,128)(2,1)S(1)}, bf16[8,128,512]{2,1,0:T(8,128)(2,1)}, bf16[8,128,512]{2,1,0:T(8,128)(2,1)S(1)}) custom-call(s32[7]{0:T(128)S(1)} %stack.27.refs_0_, bf16[4,2,256,512]{3,2,1,0:T(8,128)(2,1)S(1)} %bitcast.214, bf16[4,2,256,512]{3,2,1,0:T(8,128)(2,1)} %bitcast.87.refs_2_, ...), custom_call_target="tpu_custom_call" | custom-call | bytes 12582912 | tf_op jit(solution)/shard_map/pallas_call | solution.py:88
  344.8 7.3 %collective-permute-done.54 = bf16[1024,512]{1,0:T(8,128)(2,1)} collective-permute-done((bf16[1024,512]{1,0:T(8,128)(2,1)}, bf16[1024,512]{1,0:T(8,128)(2,1)}, u32[]{:S(2)}, u32[]{:S(2)}) %collective-permute-start.54) | collective-permute-done | bytes 1048608 | tf_op jit(solution)/shard_map/ppermute | solution.py:39
  353.5 7.0 %collective-permute-done.55 = bf16[1024,512]{1,0:T(8,128)(2,1)} collective-permute-done((bf16[1024,512]{1,0:T(8,128)(2,1)}, bf16[1024,512]{1,0:T(8,128)(2,1)}, u32[]{:S(2)}, u32[]{:S(2)}) %collective-permute-start.55) | collective-permute-done | bytes 1048608 | tf_op jit(solution)/shard_map/ppermute | solution.py:39
  377.7 4.9 %collective-permute-done.60 = bf16[512,512]{1,0:T(8,128)(2,1)S(1)} collective-permute-done((bf16[512,512]{1,0:T(8,128)(2,1)S(1)}, bf16[512,512]{1,0:T(8,128)(2,1)S(1)}, u32[]{:S(2)}, u32[]{:S(2)}) %collective-permute-start.60) | collective-permute-done | bytes 524320 | tf_op jit(solution)/shard_map/ppermute | solution.py:39
  406.2 5.2 %shard_map.472 = (f32[512,1024]{1,0:T(8,128)}, f32[512,1024]{1,0:T(8,128)}, bf16[512,1024]{1,0:T(8,128)(2,1)}) custom-call(s32[7]{0:T(128)S(1)} %stack.27.refs_0_, bf16[128,1024]{1,0:T(8,128)(2,1)S(1)} %get-tuple-element.443.refs_1_, bf16[128,1024]{1,0:T(8,128)(2,1)S(1)} %collective-permute-done.45.refs_2_, ...), custom_call_target="tpu_custom_call" | custom-call | flops 2147483648 | bytes 11534336 | tf_op jit(solution)/shard_map/pallas_call | solution.py:88
  414.3 6.0 %collective-permute-done.74.refs_2_ = bf16[128,1024]{1,0:T(8,128)(2,1)S(1)} collective-permute-done((bf16[128,1024]{1,0:T(8,128)(2,1)S(1)}, bf16[128,1024]{1,0:T(8,128)(2,1)S(1)}, u32[]{:S(2)}, u32[]{:S(2)}) %collective-permute-start.74) | collective-permute-done | bytes 262176 | tf_op jit(solution)/shard_map/ppermute | solution.py:39
  420.2 5.6 %collective-permute-done.75.refs_4_ = bf16[128,1024]{1,0:T(8,128)(2,1)S(1)} collective-permute-done((bf16[128,1024]{1,0:T(8,128)(2,1)S(1)}, bf16[128,1024]{1,0:T(8,128)(2,1)S(1)}, u32[]{:S(2)}, u32[]{:S(2)}) %collective-permute-start.75) | collective-permute-done | bytes 262176 | tf_op jit(solution)/shard_map/ppermute | solution.py:39
  446.1 5.3 %collective-permute-done.80.refs_2_ = bf16[64,1024]{1,0:T(8,128)(2,1)S(1)} collective-permute-done((bf16[64,1024]{1,0:T(8,128)(2,1)S(1)}, bf16[64,1024]{1,0:T(8,128)(2,1)S(1)}, u32[]{:S(2)}, u32[]{:S(2)}) %collective-permute-start.80) | collective-permute-done | bytes 131104 | tf_op jit(solution)/shard_map/ppermute | solution.py:39
  (457 shorter events, 212.7 us)
Async XLA Ops:
  70.3 48.3 %collective-permute-start.26 = (bf16[512,1024]{1,0:T(8,128)(2,1)S(1)}, bf16[512,1024]{1,0:T(8,128)(2,1)S(1)}, u32[]{:S(2)}, u32[]{:S(2)}) collective-permute-start(bf16[512,1024]{1,0:T(8,128)(2,1)S(1)} %bitcast.194), channel_id=1, source_target_pairs={{0,8},{4,12},{8,0},{12,4},{16,24},{20,28},{24,16},{28,20},{1,9},{5... | collective-permute-start | bytes 3145736 | tf_op jit(solution)/shard_map/ppermute | solution.py:39
  71.8 44.8 %collective-permute-start.21 = (bf16[128,3072]{1,0:T(8,128)(2,1)S(1)}, bf16[128,3072]{1,0:T(8,128)(2,1)S(1)}, u32[]{:S(2)}, u32[]{:S(2)}) collective-permute-start(bf16[128,3072]{1,0:T(8,128)(2,1)S(1)} %copy-done.85), channel_id=1, source_target_pairs={{0,2},{1,3},{2,0},{3,1},{4,6},{5,7},{6,4},{7,5},{8,10},{9,11},{10,... | collective-permute-start | bytes 2359304 | tf_op jit(solution)/shard_map/ppermute | solution.py:39
  73.3 45.3 %collective-permute-start.25 = (bf16[128,3072]{1,0:T(8,128)(2,1)S(1)}, bf16[128,3072]{1,0:T(8,128)(2,1)S(1)}, u32[]{:S(2)}, u32[]{:S(2)}) collective-permute-start(bf16[128,3072]{1,0:T(8,128)(2,1)S(1)} %copy-done.53), channel_id=1, source_target_pairs={{0,3},{1,2},{2,1},{3,0},{4,7},{5,6},{6,5},{7,4},{8,11},{9,10},{10,... | collective-permute-start | bytes 2359304 | tf_op jit(solution)/shard_map/ppermute | solution.py:39
  83.3 33.3 %collective-permute-start.13 = (bf16[512,512]{1,0:T(8,128)(2,1)S(1)}, bf16[512,512]{1,0:T(8,128)(2,1)S(1)}, u32[]{:S(2)}, u32[]{:S(2)}) collective-permute-start(bf16[512,512]{1,0:T(8,128)(2,1)S(1)} %bitcast.209), channel_id=1, source_target_pairs={{0,8},{4,12},{8,0},{12,4},{16,24},{20,28},{24,16},{28,20},{1,9},{5... | collective-permute-start | bytes 1572872 | tf_op jit(solution)/shard_map/ppermute | solution.py:39
  83.4 33.2 %collective-permute-start.12 = (bf16[512,512]{1,0:T(8,128)(2,1)S(1)}, bf16[512,512]{1,0:T(8,128)(2,1)S(1)}, u32[]{:S(2)}, u32[]{:S(2)}) collective-permute-start(bf16[512,512]{1,0:T(8,128)(2,1)S(1)} %bitcast.232), channel_id=1, source_target_pairs={{0,4},{4,0},{8,12},{12,8},{16,20},{20,16},{24,28},{28,24},{1,5},{5... | collective-permute-start | bytes 1572872 | tf_op jit(solution)/shard_map/ppermute | solution.py:39
  121.8 32.0 %collective-permute-start.23 = (bf16[1024,512]{1,0:T(8,128)(2,1)}, bf16[1024,512]{1,0:T(8,128)(2,1)}, u32[]{:S(2)}, u32[]{:S(2)}) collective-permute-start(bf16[1024,512]{1,0:T(8,128)(2,1)} %bitcast.54), channel_id=1, source_target_pairs={{0,4},{4,0},{8,12},{12,8},{16,20},{20,16},{24,28},{28,24},{1,5},{5... | collective-permute-start | bytes 3145736 | tf_op jit(solution)/shard_map/ppermute | solution.py:39
  125.7 43.9 %collective-permute-start.22 = (bf16[1024,512]{1,0:T(8,128)(2,1)}, bf16[1024,512]{1,0:T(8,128)(2,1)}, u32[]{:S(2)}, u32[]{:S(2)}) collective-permute-start(bf16[1024,512]{1,0:T(8,128)(2,1)} %bitcast.51), channel_id=1, source_target_pairs={{0,8},{4,12},{8,0},{12,4},{16,24},{20,28},{24,16},{28,20},{1,9},{5... | collective-permute-start | bytes 3145736 | tf_op jit(solution)/shard_map/ppermute | solution.py:39
  127.2 42.4 %collective-permute-start.32 = (bf16[2,4,128,512]{3,2,1,0:T(8,128)(2,1)}, bf16[2,4,128,512]{3,2,1,0:T(8,128)(2,1)}, u32[]{:S(2)}, u32[]{:S(2)}) collective-permute-start(bf16[2,4,128,512]{3,2,1,0:T(8,128)(2,1)} %bitcast.53.refs_3_), channel_id=1, source_target_pairs={{0,1},{1,0},{2,3},{3,2},{4,5},{5,4},{6,7},{7,6},{8,9},{9,8},{10,11... | collective-permute-start | bytes 3145736 | tf_op jit(solution)/shard_map/ppermute | solution.py:39
  152.7 46.6 %collective-permute-start.34 = (bf16[1024,1024]{1,0:T(8,128)(2,1)}, bf16[1024,1024]{1,0:T(8,128)(2,1)}, u32[]{:S(2)}, u32[]{:S(2)}) collective-permute-start(bf16[1024,1024]{1,0:T(8,128)(2,1)} %bitcast.72), channel_id=1, source_target_pairs={{0,2},{1,3},{2,0},{3,1},{4,6},{5,7},{6,4},{7,5},{8,10},{9,11},{10,... | collective-permute-start | bytes 6291464 | tf_op jit(solution)/shard_map/ppermute | solution.py:39
  153.3 46.5 %collective-permute-start.37 = (bf16[1024,1024]{1,0:T(8,128)(2,1)}, bf16[1024,1024]{1,0:T(8,128)(2,1)}, u32[]{:S(2)}, u32[]{:S(2)}) collective-permute-start(bf16[1024,1024]{1,0:T(8,128)(2,1)} %bitcast.75), channel_id=1, source_target_pairs={{0,4},{4,0},{8,12},{12,8},{16,20},{20,16},{24,28},{28,24},{1,5},{5... | collective-permute-start | bytes 6291464 | tf_op jit(solution)/shard_map/ppermute | solution.py:39
  153.8 32.4 %collective-permute-start.30 = (bf16[2,2,256,512]{3,2,1,0:T(8,128)(2,1)}, bf16[2,2,256,512]{3,2,1,0:T(8,128)(2,1)}, u32[]{:S(2)}, u32[]{:S(2)}) collective-permute-start(bf16[2,2,256,512]{3,2,1,0:T(8,128)(2,1)} %bitcast.50.refs_1_), channel_id=1, source_target_pairs={{0,1},{1,0},{2,3},{3,2},{4,5},{5,4},{6,7},{7,6},{8,9},{9,8},{10,11... | collective-permute-start | bytes 3145736 | tf_op jit(solution)/shard_map/ppermute | solution.py:39
  239.1 61.8 %collective-permute-start.48 = (bf16[1024,1024]{1,0:T(8,128)(2,1)}, bf16[1024,1024]{1,0:T(8,128)(2,1)S(1)}, u32[]{:S(2)}, u32[]{:S(2)}) collective-permute-start(bf16[1024,1024]{1,0:T(8,128)(2,1)} %bitcast.78), channel_id=1, source_target_pairs={{0,4},{4,0},{8,12},{12,8},{16,20},{20,16},{24,28},{28,24},{1,5},{5... | collective-permute-start | bytes 6291464 | tf_op jit(solution)/shard_map/ppermute | solution.py:39
  252.5 48.4 %collective-permute-start.49 = (bf16[1024,1024]{1,0:T(8,128)(2,1)}, bf16[1024,1024]{1,0:T(8,128)(2,1)S(1)}, u32[]{:S(2)}, u32[]{:S(2)}) collective-permute-start(bf16[1024,1024]{1,0:T(8,128)(2,1)} %bitcast.81), channel_id=1, source_target_pairs={{0,8},{4,12},{8,0},{12,4},{16,24},{20,28},{24,16},{28,20},{1,9},{5... | collective-permute-start | bytes 6291464 | tf_op jit(solution)/shard_map/ppermute | solution.py:39
  279.2 34.8 %collective-permute-start.51 = (bf16[2,1024,512]{2,1,0:T(8,128)(2,1)}, bf16[2,1024,512]{2,1,0:T(8,128)(2,1)}, u32[]{:S(2)}, u32[]{:S(2)}) collective-permute-start(bf16[2,1024,512]{2,1,0:T(8,128)(2,1)} %get-tuple-element.247), channel_id=1, source_target_pairs={{0,1},{1,0},{2,3},{3,2},{4,5},{5,4},{6,7},{7,6},{8,9},{9,8},{10,11... | collective-permute-start | bytes 6291464 | tf_op jit(solution)/shard_map/ppermute | solution.py:39
  279.3 34.7 %collective-permute-start.52 = (bf16[2,1024,512]{2,1,0:T(8,128)(2,1)}, bf16[2,1024,512]{2,1,0:T(8,128)(2,1)}, u32[]{:S(2)}, u32[]{:S(2)}) collective-permute-start(bf16[2,1024,512]{2,1,0:T(8,128)(2,1)} %get-tuple-element.249), channel_id=1, source_target_pairs={{0,1},{1,0},{2,3},{3,2},{4,5},{5,4},{6,7},{7,6},{8,9},{9,8},{10,11... | collective-permute-start | bytes 6291464 | tf_op jit(solution)/shard_map/ppermute | solution.py:39
  311.7 26.3 %collective-permute-start.56 = (bf16[512,1024]{1,0:T(8,128)(2,1)}, bf16[512,1024]{1,0:T(8,128)(2,1)}, u32[]{:S(2)}, u32[]{:S(2)}) collective-permute-start(bf16[512,1024]{1,0:T(8,128)(2,1)} %bitcast.271), channel_id=1, source_target_pairs={{0,2},{1,3},{2,0},{3,1},{4,6},{5,7},{6,4},{7,5},{8,10},{9,11},{10,... | collective-permute-start | bytes 3145736 | tf_op jit(solution)/shard_map/ppermute | solution.py:39
  325.7 26.4 %collective-permute-start.54 = (bf16[1024,512]{1,0:T(8,128)(2,1)}, bf16[1024,512]{1,0:T(8,128)(2,1)}, u32[]{:S(2)}, u32[]{:S(2)}) collective-permute-start(bf16[1024,512]{1,0:T(8,128)(2,1)} %bitcast.94), channel_id=1, source_target_pairs={{0,8},{4,12},{8,0},{12,4},{16,24},{20,28},{24,16},{28,20},{1,9},{5... | collective-permute-start | bytes 3145736 | tf_op jit(solution)/shard_map/ppermute | solution.py:39
  327.4 33.0 %collective-permute-start.55 = (bf16[1024,512]{1,0:T(8,128)(2,1)}, bf16[1024,512]{1,0:T(8,128)(2,1)}, u32[]{:S(2)}, u32[]{:S(2)}) collective-permute-start(bf16[1024,512]{1,0:T(8,128)(2,1)} %bitcast.97), channel_id=1, source_target_pairs={{0,4},{4,0},{8,12},{12,8},{16,20},{20,16},{24,28},{28,24},{1,5},{5... | collective-permute-start | bytes 3145736 | tf_op jit(solution)/shard_map/ppermute | solution.py:39
  333.4 35.7 %collective-permute-start.53 = (bf16[512,1024]{1,0:T(8,128)(2,1)S(1)}, bf16[512,1024]{1,0:T(8,128)(2,1)S(1)}, u32[]{:S(2)}, u32[]{:S(2)}) collective-permute-start(bf16[512,1024]{1,0:T(8,128)(2,1)S(1)} %bitcast.269), channel_id=1, source_target_pairs={{0,2},{1,3},{2,0},{3,1},{4,6},{5,7},{6,4},{7,5},{8,10},{9,11},{10,... | collective-permute-start | bytes 3145736 | tf_op jit(solution)/shard_map/ppermute | solution.py:39
  343.1 28.7 %collective-permute-start.61 = (bf16[256,1024]{1,0:T(8,128)(2,1)S(1)}, bf16[256,1024]{1,0:T(8,128)(2,1)S(1)}, u32[]{:S(2)}, u32[]{:S(2)}) collective-permute-start(bf16[256,1024]{1,0:T(8,128)(2,1)S(1)} %bitcast.273), channel_id=1, source_target_pairs={{0,8},{4,12},{8,0},{12,4},{16,24},{20,28},{24,16},{28,20},{1,9},{5... | collective-permute-start | bytes 1572872 | tf_op jit(solution)/shard_map/ppermute | solution.py:39
  393.3 26.9 %collective-permute-start.74 = (bf16[128,1024]{1,0:T(8,128)(2,1)S(1)}, bf16[128,1024]{1,0:T(8,128)(2,1)S(1)}, u32[]{:S(2)}, u32[]{:S(2)}) collective-permute-start(bf16[128,1024]{1,0:T(8,128)(2,1)S(1)} %bitcast.278), channel_id=1, source_target_pairs={{0,16},{4,20},{8,24},{12,28},{16,0},{20,4},{24,8},{28,12},{1,17},{... | collective-permute-start | bytes 786440 | tf_op jit(solution)/shard_map/ppermute | solution.py:39
  395.3 30.6 %collective-permute-start.75 = (bf16[128,1024]{1,0:T(8,128)(2,1)S(1)}, bf16[128,1024]{1,0:T(8,128)(2,1)S(1)}, u32[]{:S(2)}, u32[]{:S(2)}) collective-permute-start(bf16[128,1024]{1,0:T(8,128)(2,1)S(1)} %bitcast.277), channel_id=1, source_target_pairs={{0,16},{4,20},{8,24},{12,28},{16,0},{20,4},{24,8},{28,12},{1,17},{... | collective-permute-start | bytes 786440 | tf_op jit(solution)/shard_map/ppermute | solution.py:39
  397.4 31.2 %collective-permute-start.77 = (bf16[128,512]{1,0:T(8,128)(2,1)S(1)}, bf16[128,512]{1,0:T(8,128)(2,1)S(1)}, u32[]{:S(2)}, u32[]{:S(2)}) collective-permute-start(bf16[128,512]{1,0:T(8,128)(2,1)S(1)} %bitcast.284), channel_id=1, source_target_pairs={{0,16},{4,20},{8,24},{12,28},{16,0},{20,4},{24,8},{28,12},{1,17},{... | collective-permute-start | bytes 393224 | tf_op jit(solution)/shard_map/ppermute | solution.py:39
  403.1 28.0 %collective-permute-start.76 = (bf16[128,512]{1,0:T(8,128)(2,1)S(1)}, bf16[128,512]{1,0:T(8,128)(2,1)S(1)}, u32[]{:S(2)}, u32[]{:S(2)}) collective-permute-start(bf16[128,512]{1,0:T(8,128)(2,1)S(1)} %bitcast.283), channel_id=1, source_target_pairs={{0,16},{4,20},{8,24},{12,28},{16,0},{20,4},{24,8},{28,12},{1,17},{... | collective-permute-start | bytes 393224 | tf_op jit(solution)/shard_map/ppermute | solution.py:39
  (154 other events, 1430.8 us)

commit v5 on v4

--- a/solution.py
+++ b/solution.py
@@ -1067,7 +1067,7 @@
         go(line, *attention_scatters)
         go(line, skip_scatter)
     next(modulate_back)
-    line.need(*(walk.terms[1] for walk in attention_scatters))
+    line.need(*(walk.terms[1] for walk in (*attention_scatters, skip_scatter)))
     feed_new = update_feed(
         line,
         feed_one.terms,

time: 461 us -> 481 us (1.043)
  waiting for transfers between devices: 157 us -> 174 us
    ppermute x81, waiting for transfers between devices: 157 us -> 174 us  [swap(): return lax.ppermute(values, axis, [(i, i ^ mask) for i in range(count)])]
    unnamed x197 -> x201, local copies, waits for them, and re-layouts: 42.6 us -> 46.4 us
  transfers between devices with their start and end apart: 81 -> 81, of which waited for: 36 -> 36; matrix products, arithmetic and copies ran while one was open for 2% -> 2% of each run, Pallas kernels for 36% -> 34%
where the time goes in v5:
time: 481 us; the launch traced here: 474 us
  waiting for transfers between devices  174 us (36%)
  Pallas kernels  168 us (35%)
  starting transfers between devices  70 us (15%)
  local copies, waits for them, and re-layouts  52.7 us (11%)
  matrix products  4.98 us (1%)
    ppermute x81, waiting for transfers between devices, swap(): return lax.ppermute(values, axis, [(i, i ^ mask) for i in range(count)])  174 us
    pallas_call x38, Pallas kernels, run(): pl.pallas_call(inner, grid_spec=pltpu.PrefetchScalarGridSpec(num_scalar_p...  168 us
    ppermute x81, starting transfers between devices, swap(): return lax.ppermute(values, axis, [(i, i ^ mask) for i in range(count)])  70 us
    unnamed x201, local copies, waits for them, and re-layouts  46.4 us
  transfers between devices with their start and end apart: 81, of which 36 were waited for; matrix products, arithmetic and copies ran while one was open for 2% of the time, Pallas kernels for 34%

profile of v5, /device:TPU:0, one launch (start us, length us, event | category | flops | bytes accessed | tf_op | source)
XLA Modules:
  0.0 473.8 jit_solution(17412879401781279537)
XLA Ops:
  55.2 6.8 %collective-permute-done.14 = bf16[128,1024]{1,0:T(8,128)(2,1)S(1)} collective-permute-done((bf16[128,1024]{1,0:T(8,128)(2,1)S(1)}, bf16[128,1024]{1,0:T(8,128)(2,1)S(1)}, u32[]{:S(2)}, u32[]{:S(2)}) %collective-permute-start.14) | collective-permute-done | bytes 262176 | tf_op jit(solution)/shard_map/ppermute | solution.py:39
  62.0 5.4 %collective-permute-done.15 = bf16[128,1024]{1,0:T(8,128)(2,1)S(1)} collective-permute-done((bf16[128,1024]{1,0:T(8,128)(2,1)S(1)}, bf16[128,1024]{1,0:T(8,128)(2,1)S(1)}, u32[]{:S(2)}, u32[]{:S(2)}) %collective-permute-start.15) | collective-permute-done | bytes 262176 | tf_op jit(solution)/shard_map/ppermute | solution.py:39
  72.9 10.0 %collective-permute-done.18 = bf16[256,1024]{1,0:T(8,128)(2,1)S(1)} collective-permute-done((bf16[256,1024]{1,0:T(8,128)(2,1)S(1)}, bf16[256,1024]{1,0:T(8,128)(2,1)S(1)}, u32[]{:S(2)}, u32[]{:S(2)}) %collective-permute-start.18) | collective-permute-done | bytes 524320 | tf_op jit(solution)/shard_map/ppermute | solution.py:39
  85.4 30.7 %collective-permute-done.13 = bf16[512,512]{1,0:T(8,128)(2,1)S(1)} collective-permute-done((bf16[512,512]{1,0:T(8,128)(2,1)S(1)}, bf16[512,512]{1,0:T(8,128)(2,1)S(1)}, u32[]{:S(2)}, u32[]{:S(2)}) %collective-permute-start.13) | collective-permute-done | bytes 524320 | tf_op jit(solution)/shard_map/ppermute | solution.py:39
  137.5 8.0 %collective-permute-done.29 = bf16[512,1024]{1,0:T(8,128)(2,1)} collective-permute-done((bf16[512,1024]{1,0:T(8,128)(2,1)}, bf16[512,1024]{1,0:T(8,128)(2,1)}, u32[]{:S(2)}, u32[]{:S(2)}) %collective-permute-start.29) | collective-permute-done | bytes 1048608 | tf_op jit(solution)/shard_map/ppermute | solution.py:39
  147.4 4.9 %shard_map.450 = (bf16[2,2,256,1024]{3,2,1,0:T(8,128)(2,1)}, bf16[1,2,512,1024]{3,2,1,0:T(8,128)(2,1)}) custom-call(s32[7]{0:T(128)S(1)} %stack.27.refs_0_, bf16[2,256,1024]{2,1,0:T(8,128)(2,1)} %bitcast.65.refs_1_, bf16[2,256,1024]{2,1,0:T(8,128)(2,1)} %bitcast.67.refs_2_, bf16[1,512,1024]{2,1,0:T(8,128)(2,1)} %bitcast.68.refs_3_, ...), custom_call_target="tpu_custom_call" | custom-call | bytes 8388608 | tf_op jit(solution)/shard_map/pallas_call | solution.py:88
  153.5 15.7 %collective-permute-done.22 = bf16[1024,512]{1,0:T(8,128)(2,1)} collective-permute-done((bf16[1024,512]{1,0:T(8,128)(2,1)}, bf16[1024,512]{1,0:T(8,128)(2,1)}, u32[]{:S(2)}, u32[]{:S(2)}) %collective-permute-start.22) | collective-permute-done | bytes 1048608 | tf_op jit(solution)/shard_map/ppermute | solution.py:39
  173.4 12.4 %shard_map.451 = (bf16[2,512,768]{2,1,0:T(8,128)(2,1)S(1)}, bf16[2,512,256]{2,1,0:T(8,128)(2,1)S(1)}, f32[512,1024]{1,0:T(8,128)S(1)}, bf16[512,1024]{1,0:T(8,128)(2,1)S(1)}) custom-call(s32[7]{0:T(128)S(1)} %stack.27.refs_0_, bf16[2,2,256,512]{3,2,1,0:T(8,128)(2,1)} %bitcast.50.refs_1_, bf16[2,2,256,512]{3,2,1,0:T(8,128)(2,1)} %bitcast.52.refs_2_, ...), custom_call_target="tpu_custom_call" | custom-call | flops 4294967296 | bytes 12593152 | tf_op jit(solution)/shard_map/pallas_call | solution.py:88
  185.8 12.1 %shard_map.452 = (bf16[2,512,768]{2,1,0:T(8,128)(2,1)S(1)}, bf16[2,512,256]{2,1,0:T(8,128)(2,1)S(1)}, f32[512,1024]{1,0:T(8,128)S(1)}, bf16[512,1024]{1,0:T(8,128)(2,1)S(1)}) custom-call(s32[7]{0:T(128)S(1)} %stack.27.refs_0_, bf16[2,2,256,512]{3,2,1,0:T(8,128)(2,1)} %collective-permute-done.30.refs_1_, ...), custom_call_target="tpu_custom_call" | custom-call | flops 4294967296 | bytes 15738880 | tf_op jit(solution)/shard_map/pallas_call | solution.py:88
  206.2 9.4 %shard_map.453 = (bf16[2,1024,1024]{2,1,0:T(8,128)(2,1)S(1)}, bf16[512,1024]{1,0:T(8,128)(2,1)S(1)}, bf16[512,1024]{1,0:T(8,128)(2,1)S(1)}) custom-call(s32[7]{0:T(128)S(1)} %stack.27.refs_0_, bf16[1,1024,1024]{2,1,0:T(8,128)(2,1)S(1)} %collective-permute-done.35.refs_1_, bf16[1,1024,1024]{2,1,0:T(8,128)(2,1)S(1)} %collective-permute-done.36.refs_2_, ...), custom_call_target="tpu_custom_call" | custom-call | flops 6442450944 | bytes 12582912 | tf_op jit(solution)/shard_map/pallas_call | solution.py:88
  215.8 9.2 %shard_map.454 = (bf16[2,1024,1024]{2,1,0:T(8,128)(2,1)S(1)}, bf16[512,1024]{1,0:T(8,128)(2,1)S(1)}, bf16[512,1024]{1,0:T(8,128)(2,1)S(1)}) custom-call(s32[7]{0:T(128)S(1)} %stack.27.refs_0_, bf16[2,4,128,1024]{3,2,1,0:T(8,128)(2,1)S(1)} %collective-permute-done.38.refs_1_, bf16[2,4,128,1024]{3,2,1,0:T(8,128)(2,1)S(1)} %collective-permute-done.39.refs_2_, ...), custom_call_target="tpu_custom_call" | custom-call | flops 6442450944 | bytes 12582912 | tf_op jit(solution)/shard_map/pallas_call | solution.py:88
  225.5 13.1 %shard_map.455 = (bf16[2,4,128,1024]{3,2,1,0:T(8,128)(2,1)S(1)}, bf16[2,4,128,1024]{3,2,1,0:T(8,128)(2,1)}, bf16[512,1024]{1,0:T(8,128)(2,1)S(1)}, bf16[512,1024]{1,0:T(8,128)(2,1)S(1)}) custom-call(s32[7]{0:T(128)S(1)} %stack.27.refs_0_, bf16[1,1024,1024]{2,1,0:T(8,128)(2,1)} %bitcast.71.refs_1_, bf16[1,1024,1024]{2,1,0:T(8,128)(2,1)} %bitcast.73.refs_2_, ...), custom_call_target="tpu_custom_call" | custom-call | flops 6442450944 | bytes 16777216 | tf_op jit(solution)/shard_map/pallas_call | solution.py:88
  239.1 13.0 %shard_map.456 = (bf16[2,2,256,1024]{3,2,1,0:T(8,128)(2,1)S(1)}, bf16[2,2,256,1024]{3,2,1,0:T(8,128)(2,1)}, bf16[512,1024]{1,0:T(8,128)(2,1)S(1)}, bf16[512,1024]{1,0:T(8,128)(2,1)S(1)}) custom-call(s32[7]{0:T(128)S(1)} %stack.27.refs_0_, bf16[2,4,128,1024]{3,2,1,0:T(8,128)(2,1)} %bitcast.74.refs_1_, bf16[2,4,128,1024]{3,2,1,0:T(8,128)(2,1)} %bitcast.76.refs_2_, ...), custom_call_target="tpu_custom_call" | custom-call | flops 6442450944 | bytes 16777216 | tf_op jit(solution)/shard_map/pallas_call | solution.py:88
  258.2 19.3 %shard_map.458 = (bf16[2,1024,512]{2,1,0:T(8,128)(2,1)}, bf16[2,1024,512]{2,1,0:T(8,128)(2,1)}, f32[512,1024]{1,0:T(8,128)S(1)}) custom-call(s32[7]{0:T(128)S(1)} %stack.27.refs_0_, bf16[2,2,256,512]{3,2,1,0:T(8,128)(2,1)} %collective-permute-done.30.refs_1_, bf16[2,2,256,512]{3,2,1,0:T(8,128)(2,1)} %collective-permute-done.31.refs_2_, ...), custom_call_target="tpu_custom_call" | custom-call | flops 9663676416 | bytes 15730688 | tf_op jit(solution)/shard_map/pallas_call | solution.py:88
  281.0 19.3 %shard_map.459 = (bf16[2,1024,512]{2,1,0:T(8,128)(2,1)S(1)}, bf16[2,1024,512]{2,1,0:T(8,128)(2,1)S(1)}, f32[2,1024]{1,0:T(2,128)S(1)}, bf16[512,1024]{1,0:T(8,128)(2,1)S(1)}) custom-call(s32[7]{0:T(128)S(1)} %stack.27.refs_0_, bf16[2,2,256,512]{3,2,1,0:T(8,128)(2,1)} %bitcast.50.refs_1_, bf16[2,2,256,512]{3,2,1,0:T(8,128)(2,1)} %bitcast.52.refs_2_, ...), custom_call_target="tpu_custom_call" | custom-call | flops 9663676416 | bytes 20985856 | tf_op jit(solution)/shard_map/pallas_call | solution.py:88
  305.4 4.3 shard_map.461
  318.3 5.0 %shard_map.462 = (bf16[4,256,512]{2,1,0:T(8,128)(2,1)}, bf16[4,256,512]{2,1,0:T(8,128)(2,1)S(1)}, bf16[8,128,512]{2,1,0:T(8,128)(2,1)}, bf16[8,128,512]{2,1,0:T(8,128)(2,1)S(1)}) custom-call(s32[7]{0:T(128)S(1)} %stack.27.refs_0_, bf16[4,2,256,512]{3,2,1,0:T(8,128)(2,1)S(1)} %bitcast.214, bf16[4,2,256,512]{3,2,1,0:T(8,128)(2,1)} %bitcast.87.refs_2_, ...), custom_call_target="tpu_custom_call" | custom-call | bytes 12582912 | tf_op jit(solution)/shard_map/pallas_call | solution.py:88
  344.3 7.3 %collective-permute-done.54 = bf16[1024,512]{1,0:T(8,128)(2,1)} collective-permute-done((bf16[1024,512]{1,0:T(8,128)(2,1)}, bf16[1024,512]{1,0:T(8,128)(2,1)}, u32[]{:S(2)}, u32[]{:S(2)}) %collective-permute-start.54) | collective-permute-done | bytes 1048608 | tf_op jit(solution)/shard_map/ppermute | solution.py:39
  353.0 7.0 %collective-permute-done.55 = bf16[1024,512]{1,0:T(8,128)(2,1)} collective-permute-done((bf16[1024,512]{1,0:T(8,128)(2,1)}, bf16[1024,512]{1,0:T(8,128)(2,1)}, u32[]{:S(2)}, u32[]{:S(2)}) %collective-permute-start.55) | collective-permute-done | bytes 1048608 | tf_op jit(solution)/shard_map/ppermute | solution.py:39
  376.2 5.9 %collective-permute-done.60 = bf16[512,512]{1,0:T(8,128)(2,1)S(1)} collective-permute-done((bf16[512,512]{1,0:T(8,128)(2,1)S(1)}, bf16[512,512]{1,0:T(8,128)(2,1)S(1)}, u32[]{:S(2)}, u32[]{:S(2)}) %collective-permute-start.60) | collective-permute-done | bytes 524320 | tf_op jit(solution)/shard_map/ppermute | solution.py:39
  396.8 5.6 %collective-permute-done.46.refs_3_ = bf16[128,1024]{1,0:T(8,128)(2,1)S(1)} collective-permute-done((bf16[128,1024]{1,0:T(8,128)(2,1)S(1)}, bf16[128,1024]{1,0:T(8,128)(2,1)S(1)}, u32[]{:S(2)}, u32[]{:S(2)}) %collective-permute-start.46) | collective-permute-done | bytes 262176 | tf_op jit(solution)/shard_map/ppermute | solution.py:39
  402.5 5.1 %shard_map.472 = (f32[512,1024]{1,0:T(8,128)}, f32[512,1024]{1,0:T(8,128)}, bf16[512,1024]{1,0:T(8,128)(2,1)}) custom-call(s32[7]{0:T(128)S(1)} %stack.27.refs_0_, bf16[128,1024]{1,0:T(8,128)(2,1)S(1)} %get-tuple-element.443.refs_1_, bf16[128,1024]{1,0:T(8,128)(2,1)S(1)} %collective-permute-done.45.refs_2_, ...), custom_call_target="tpu_custom_call" | custom-call | flops 2147483648 | bytes 11534336 | tf_op jit(solution)/shard_map/pallas_call | solution.py:88
  417.4 20.3 %collective-permute-done.74.refs_2_ = bf16[128,1024]{1,0:T(8,128)(2,1)S(1)} collective-permute-done((bf16[128,1024]{1,0:T(8,128)(2,1)}, bf16[128,1024]{1,0:T(8,128)(2,1)S(1)}, u32[]{:S(2)}, u32[]{:S(2)}) %collective-permute-start.74) | collective-permute-done | bytes 262176 | tf_op jit(solution)/shard_map/ppermute | solution.py:39
  437.7 5.6 %collective-permute-done.75.refs_4_ = bf16[128,1024]{1,0:T(8,128)(2,1)S(1)} collective-permute-done((bf16[128,1024]{1,0:T(8,128)(2,1)}, bf16[128,1024]{1,0:T(8,128)(2,1)S(1)}, u32[]{:S(2)}, u32[]{:S(2)}) %collective-permute-start.75) | collective-permute-done | bytes 262176 | tf_op jit(solution)/shard_map/ppermute | solution.py:39
  (461 shorter events, 216.2 us)
Async XLA Ops:
  69.9 48.3 %collective-permute-start.26 = (bf16[512,1024]{1,0:T(8,128)(2,1)S(1)}, bf16[512,1024]{1,0:T(8,128)(2,1)S(1)}, u32[]{:S(2)}, u32[]{:S(2)}) collective-permute-start(bf16[512,1024]{1,0:T(8,128)(2,1)S(1)} %bitcast.194), channel_id=1, source_target_pairs={{0,8},{4,12},{8,0},{12,4},{16,24},{20,28},{24,16},{28,20},{1,9},{5... | collective-permute-start | bytes 3145736 | tf_op jit(solution)/shard_map/ppermute | solution.py:39
  71.4 44.7 %collective-permute-start.21 = (bf16[128,3072]{1,0:T(8,128)(2,1)S(1)}, bf16[128,3072]{1,0:T(8,128)(2,1)S(1)}, u32[]{:S(2)}, u32[]{:S(2)}) collective-permute-start(bf16[128,3072]{1,0:T(8,128)(2,1)S(1)} %copy-done.88), channel_id=1, source_target_pairs={{0,2},{1,3},{2,0},{3,1},{4,6},{5,7},{6,4},{7,5},{8,10},{9,11},{10,... | collective-permute-start | bytes 2359304 | tf_op jit(solution)/shard_map/ppermute | solution.py:39
  72.9 45.2 %collective-permute-start.25 = (bf16[128,3072]{1,0:T(8,128)(2,1)S(1)}, bf16[128,3072]{1,0:T(8,128)(2,1)S(1)}, u32[]{:S(2)}, u32[]{:S(2)}) collective-permute-start(bf16[128,3072]{1,0:T(8,128)(2,1)S(1)} %get-tuple-element.206.refs_3_), channel_id=1, source_target_pairs={{0,3},{1,2},{2,1},{3,0},{4,7},{5,6},{6,5},{7,4},{8,11},{9,10},{10,... | collective-permute-start | bytes 2359304 | tf_op jit(solution)/shard_map/ppermute | solution.py:39
  82.8 33.3 %collective-permute-start.13 = (bf16[512,512]{1,0:T(8,128)(2,1)S(1)}, bf16[512,512]{1,0:T(8,128)(2,1)S(1)}, u32[]{:S(2)}, u32[]{:S(2)}) collective-permute-start(bf16[512,512]{1,0:T(8,128)(2,1)S(1)} %bitcast.209), channel_id=1, source_target_pairs={{0,8},{4,12},{8,0},{12,4},{16,24},{20,28},{24,16},{28,20},{1,9},{5... | collective-permute-start | bytes 1572872 | tf_op jit(solution)/shard_map/ppermute | solution.py:39
  82.9 33.2 %collective-permute-start.12 = (bf16[512,512]{1,0:T(8,128)(2,1)S(1)}, bf16[512,512]{1,0:T(8,128)(2,1)S(1)}, u32[]{:S(2)}, u32[]{:S(2)}) collective-permute-start(bf16[512,512]{1,0:T(8,128)(2,1)S(1)} %bitcast.232), channel_id=1, source_target_pairs={{0,4},{4,0},{8,12},{12,8},{16,20},{20,16},{24,28},{28,24},{1,5},{5... | collective-permute-start | bytes 1572872 | tf_op jit(solution)/shard_map/ppermute | solution.py:39
  121.3 32.1 %collective-permute-start.23 = (bf16[1024,512]{1,0:T(8,128)(2,1)}, bf16[1024,512]{1,0:T(8,128)(2,1)}, u32[]{:S(2)}, u32[]{:S(2)}) collective-permute-start(bf16[1024,512]{1,0:T(8,128)(2,1)} %bitcast.54), channel_id=1, source_target_pairs={{0,4},{4,0},{8,12},{12,8},{16,20},{20,16},{24,28},{28,24},{1,5},{5... | collective-permute-start | bytes 3145736 | tf_op jit(solution)/shard_map/ppermute | solution.py:39
  125.2 43.9 %collective-permute-start.22 = (bf16[1024,512]{1,0:T(8,128)(2,1)}, bf16[1024,512]{1,0:T(8,128)(2,1)}, u32[]{:S(2)}, u32[]{:S(2)}) collective-permute-start(bf16[1024,512]{1,0:T(8,128)(2,1)} %bitcast.51), channel_id=1, source_target_pairs={{0,8},{4,12},{8,0},{12,4},{16,24},{20,28},{24,16},{28,20},{1,9},{5... | collective-permute-start | bytes 3145736 | tf_op jit(solution)/shard_map/ppermute | solution.py:39
  126.8 42.3 %collective-permute-start.32 = (bf16[2,4,128,512]{3,2,1,0:T(8,128)(2,1)}, bf16[2,4,128,512]{3,2,1,0:T(8,128)(2,1)}, u32[]{:S(2)}, u32[]{:S(2)}) collective-permute-start(bf16[2,4,128,512]{3,2,1,0:T(8,128)(2,1)} %bitcast.53.refs_3_), channel_id=1, source_target_pairs={{0,1},{1,0},{2,3},{3,2},{4,5},{5,4},{6,7},{7,6},{8,9},{9,8},{10,11... | collective-permute-start | bytes 3145736 | tf_op jit(solution)/shard_map/ppermute | solution.py:39
  152.2 46.6 %collective-permute-start.34 = (bf16[1024,1024]{1,0:T(8,128)(2,1)}, bf16[1024,1024]{1,0:T(8,128)(2,1)}, u32[]{:S(2)}, u32[]{:S(2)}) collective-permute-start(bf16[1024,1024]{1,0:T(8,128)(2,1)} %bitcast.72), channel_id=1, source_target_pairs={{0,2},{1,3},{2,0},{3,1},{4,6},{5,7},{6,4},{7,5},{8,10},{9,11},{10,... | collective-permute-start | bytes 6291464 | tf_op jit(solution)/shard_map/ppermute | solution.py:39
  152.8 46.5 %collective-permute-start.37 = (bf16[1024,1024]{1,0:T(8,128)(2,1)}, bf16[1024,1024]{1,0:T(8,128)(2,1)}, u32[]{:S(2)}, u32[]{:S(2)}) collective-permute-start(bf16[1024,1024]{1,0:T(8,128)(2,1)} %bitcast.75), channel_id=1, source_target_pairs={{0,4},{4,0},{8,12},{12,8},{16,20},{20,16},{24,28},{28,24},{1,5},{5... | collective-permute-start | bytes 6291464 | tf_op jit(solution)/shard_map/ppermute | solution.py:39
  153.4 32.4 %collective-permute-start.30 = (bf16[2,2,256,512]{3,2,1,0:T(8,128)(2,1)}, bf16[2,2,256,512]{3,2,1,0:T(8,128)(2,1)}, u32[]{:S(2)}, u32[]{:S(2)}) collective-permute-start(bf16[2,2,256,512]{3,2,1,0:T(8,128)(2,1)} %bitcast.50.refs_1_), channel_id=1, source_target_pairs={{0,1},{1,0},{2,3},{3,2},{4,5},{5,4},{6,7},{7,6},{8,9},{9,8},{10,11... | collective-permute-start | bytes 3145736 | tf_op jit(solution)/shard_map/ppermute | solution.py:39
  238.6 61.8 %collective-permute-start.48 = (bf16[1024,1024]{1,0:T(8,128)(2,1)}, bf16[1024,1024]{1,0:T(8,128)(2,1)S(1)}, u32[]{:S(2)}, u32[]{:S(2)}) collective-permute-start(bf16[1024,1024]{1,0:T(8,128)(2,1)} %bitcast.78), channel_id=1, source_target_pairs={{0,4},{4,0},{8,12},{12,8},{16,20},{20,16},{24,28},{28,24},{1,5},{5... | collective-permute-start | bytes 6291464 | tf_op jit(solution)/shard_map/ppermute | solution.py:39
  252.1 48.3 %collective-permute-start.49 = (bf16[1024,1024]{1,0:T(8,128)(2,1)}, bf16[1024,1024]{1,0:T(8,128)(2,1)S(1)}, u32[]{:S(2)}, u32[]{:S(2)}) collective-permute-start(bf16[1024,1024]{1,0:T(8,128)(2,1)} %bitcast.81), channel_id=1, source_target_pairs={{0,8},{4,12},{8,0},{12,4},{16,24},{20,28},{24,16},{28,20},{1,9},{5... | collective-permute-start | bytes 6291464 | tf_op jit(solution)/shard_map/ppermute | solution.py:39
  278.8 34.7 %collective-permute-start.51 = (bf16[2,1024,512]{2,1,0:T(8,128)(2,1)}, bf16[2,1024,512]{2,1,0:T(8,128)(2,1)}, u32[]{:S(2)}, u32[]{:S(2)}) collective-permute-start(bf16[2,1024,512]{2,1,0:T(8,128)(2,1)} %get-tuple-element.247), channel_id=1, source_target_pairs={{0,1},{1,0},{2,3},{3,2},{4,5},{5,4},{6,7},{7,6},{8,9},{9,8},{10,11... | collective-permute-start | bytes 6291464 | tf_op jit(solution)/shard_map/ppermute | solution.py:39
  278.8 34.7 %collective-permute-start.52 = (bf16[2,1024,512]{2,1,0:T(8,128)(2,1)}, bf16[2,1024,512]{2,1,0:T(8,128)(2,1)}, u32[]{:S(2)}, u32[]{:S(2)}) collective-permute-start(bf16[2,1024,512]{2,1,0:T(8,128)(2,1)} %get-tuple-element.249), channel_id=1, source_target_pairs={{0,1},{1,0},{2,3},{3,2},{4,5},{5,4},{6,7},{7,6},{8,9},{9,8},{10,11... | collective-permute-start | bytes 6291464 | tf_op jit(solution)/shard_map/ppermute | solution.py:39
  325.2 26.4 %collective-permute-start.54 = (bf16[1024,512]{1,0:T(8,128)(2,1)}, bf16[1024,512]{1,0:T(8,128)(2,1)}, u32[]{:S(2)}, u32[]{:S(2)}) collective-permute-start(bf16[1024,512]{1,0:T(8,128)(2,1)} %bitcast.94), channel_id=1, source_target_pairs={{0,8},{4,12},{8,0},{12,4},{16,24},{20,28},{24,16},{28,20},{1,9},{5... | collective-permute-start | bytes 3145736 | tf_op jit(solution)/shard_map/ppermute | solution.py:39
  326.9 33.0 %collective-permute-start.55 = (bf16[1024,512]{1,0:T(8,128)(2,1)}, bf16[1024,512]{1,0:T(8,128)(2,1)}, u32[]{:S(2)}, u32[]{:S(2)}) collective-permute-start(bf16[1024,512]{1,0:T(8,128)(2,1)} %bitcast.97), channel_id=1, source_target_pairs={{0,4},{4,0},{8,12},{12,8},{16,20},{20,16},{24,28},{28,24},{1,5},{5... | collective-permute-start | bytes 3145736 | tf_op jit(solution)/shard_map/ppermute | solution.py:39
  333.1 35.6 %collective-permute-start.53 = (bf16[512,1024]{1,0:T(8,128)(2,1)S(1)}, bf16[512,1024]{1,0:T(8,128)(2,1)S(1)}, u32[]{:S(2)}, u32[]{:S(2)}) collective-permute-start(bf16[512,1024]{1,0:T(8,128)(2,1)S(1)} %bitcast.270), channel_id=1, source_target_pairs={{0,2},{1,3},{2,0},{3,1},{4,6},{5,7},{6,4},{7,5},{8,10},{9,11},{10,... | collective-permute-start | bytes 3145736 | tf_op jit(solution)/shard_map/ppermute | solution.py:39
  342.6 28.7 %collective-permute-start.61 = (bf16[256,1024]{1,0:T(8,128)(2,1)S(1)}, bf16[256,1024]{1,0:T(8,128)(2,1)S(1)}, u32[]{:S(2)}, u32[]{:S(2)}) collective-permute-start(bf16[256,1024]{1,0:T(8,128)(2,1)S(1)} %bitcast.274), channel_id=1, source_target_pairs={{0,8},{4,12},{8,0},{12,4},{16,24},{20,28},{24,16},{28,20},{1,9},{5... | collective-permute-start | bytes 1572872 | tf_op jit(solution)/shard_map/ppermute | solution.py:39
  408.8 29.0 %collective-permute-start.74 = (bf16[128,1024]{1,0:T(8,128)(2,1)}, bf16[128,1024]{1,0:T(8,128)(2,1)S(1)}, u32[]{:S(2)}, u32[]{:S(2)}) collective-permute-start(bf16[128,1024]{1,0:T(8,128)(2,1)} %bitcast.140), channel_id=1, source_target_pairs={{0,16},{4,20},{8,24},{12,28},{16,0},{20,4},{24,8},{28,12},{1,17},{... | collective-permute-start | bytes 786440 | tf_op jit(solution)/shard_map/ppermute | solution.py:39
  411.2 32.2 %collective-permute-start.75 = (bf16[128,1024]{1,0:T(8,128)(2,1)}, bf16[128,1024]{1,0:T(8,128)(2,1)S(1)}, u32[]{:S(2)}, u32[]{:S(2)}) collective-permute-start(bf16[128,1024]{1,0:T(8,128)(2,1)} %bitcast.142), channel_id=1, source_target_pairs={{0,16},{4,20},{8,24},{12,28},{16,0},{20,4},{24,8},{28,12},{1,17},{... | collective-permute-start | bytes 786440 | tf_op jit(solution)/shard_map/ppermute | solution.py:39
  411.7 34.5 %collective-permute-start.77 = (bf16[128,512]{1,0:T(8,128)(2,1)}, bf16[128,512]{1,0:T(8,128)(2,1)S(1)}, u32[]{:S(2)}, u32[]{:S(2)}) collective-permute-start(bf16[128,512]{1,0:T(8,128)(2,1)} %bitcast.144), channel_id=1, source_target_pairs={{0,16},{4,20},{8,24},{12,28},{16,0},{20,4},{24,8},{28,12},{1,17},{... | collective-permute-start | bytes 393224 | tf_op jit(solution)/shard_map/ppermute | solution.py:39
  414.1 34.9 %collective-permute-start.76 = (bf16[128,512]{1,0:T(8,128)(2,1)}, bf16[128,512]{1,0:T(8,128)(2,1)S(1)}, u32[]{:S(2)}, u32[]{:S(2)}) collective-permute-start(bf16[128,512]{1,0:T(8,128)(2,1)} %bitcast.143), channel_id=1, source_target_pairs={{0,16},{4,20},{8,24},{12,28},{16,0},{20,4},{24,8},{28,12},{1,17},{... | collective-permute-start | bytes 393224 | tf_op jit(solution)/shard_map/ppermute | solution.py:39
  414.6 36.7 %collective-permute-start.78 = (bf16[64,1024]{1,0:T(8,128)(2,1)}, bf16[64,1024]{1,0:T(8,128)(2,1)S(1)}, u32[]{:S(2)}, u32[]{:S(2)}) collective-permute-start(bf16[64,1024]{1,0:T(8,128)(2,1)} %bitcast.145), channel_id=1, source_target_pairs={{0,16},{4,20},{8,24},{12,28},{16,0},{20,4},{24,8},{28,12},{1,17},{... | collective-permute-start | bytes 393224 | tf_op jit(solution)/shard_map/ppermute | solution.py:39
  (156 other events, 1413.3 us)
